TPU v7x, 32 devices: a whole 2x2x4 slice. The times are simulated.
32 devices in a mesh: trow: 8 (over z, x), tcol: 4 (over y, core).
Axes of the slice: x: 2, y: 2, z: 4, core: 2. Of those that a mesh axis runs over, the one named last changes fastest.
Arguments:
- query: bfloat16 [16, 256, 1152], P('trow', 'tcol'), may hold values from -64 to 64
- key: bfloat16 [16, 256, 1152], P('trow', 'tcol'), may hold values from -6 to 6
- value: bfloat16 [16, 256, 1152], P('trow', 'tcol'), may hold values from -6 to 6
- control: bfloat16 [16, 256, 1152], P('trow', 'tcol'), may hold values from -6 to 6
- kernel: float32 [3, 3, 1152], replicated, may hold values from -3 to 3
- grad_out: bfloat16 [16, 256, 1152], P('trow', 'tcol'), may hold values from -96 to 96
- detail_blocks: int32 [8, 4, 4], P('trow'), may hold values from -1 to 0, as said below
Outputs:
- grad_query: bfloat16 [16, 256, 1152], P('trow', 'tcol')
- grad_key: bfloat16 [16, 256, 1152], P('trow', 'tcol')
- grad_value: bfloat16 [16, 256, 1152], P('trow', 'tcol')
- grad_control: bfloat16 [16, 256, 1152], P('trow', 'tcol')
- grad_kernel: float32 [3, 3, 1152], replicated
Inputs may be any that keep to these rules, and one draw needn't show every extreme that they name: `detail_blocks`: entry [i, j, p] is the key block of tile (i, p) that tile (i, j) also attends to, or -1 for none; entry [i, j, j] is -1; each tile names blocks of 1 to 3 other tiles, and in every tile row one tile names a block of each of the other 3 tiles.
All inputs are finite; a program needn't handle non-finite values.
Results may differ from a plain program's by a relative error of at most 0.0095.
Values may be sent and summed in bfloat16 or wider, within the bound.
No kernel may reach another device: no remote copies, remote signals or barrier semaphores. Data moves between devices by JAX's collectives and lax.ppermute only.
A program may use at most 128 MiB of HBM per device.

v0:
```python
import math

import jax
import jax.numpy as jnp
from jax import lax
from jax.sharding import PartitionSpec as P

HEADS = 16
HEAD_DIM = 72
BLOCK = 128


NEG = -1e30


def with_halo(block, sides, width):
    for axis, dim in sides:
        count = lax.axis_size(axis)
        forward = [(i, i + 1) for i in range(count - 1)]
        backward = [(target, source) for source, target in forward]
        low = lax.ppermute(
            lax.slice_in_dim(block, block.shape[dim] - width, None, axis=dim), axis, forward
        )
        high = lax.ppermute(lax.slice_in_dim(block, 0, width, axis=dim), axis, backward)
        block = jnp.concatenate([low, block, high], axis=dim)
    return block


def from_behind(shard, axis, by):
    length = lax.axis_size(axis)
    pairs = [(i, i + by) for i in range(length) if 0 <= i + by < length]
    return lax.ppermute(shard, axis, pairs)


def conv_taps(padded, kernel, rows, cols):
    total = jnp.zeros((rows, cols, padded.shape[2]), jnp.float32)
    for row_off in range(3):
        for col_off in range(3):
            total = (
                total
                + kernel[row_off, col_off][None, None, :]
                * padded[row_off : row_off + rows, col_off : col_off + cols]
            )
    return total


def conv_back(padded, kernel, rows, cols):
    total = jnp.zeros((rows, cols, padded.shape[2]), jnp.float32)
    for row_off in range(3):
        for col_off in range(3):
            total = (
                total
                + kernel[row_off, col_off][None, None, :]
                * padded[2 - row_off : 2 - row_off + rows, 2 - col_off : 2 - col_off + cols]
            )
    return total


def attend_group(queries, grads, keys, values, key_live):
    inv_root = HEAD_DIM ** (-0.5)
    scores = (
        jnp.einsum("qhd,khd->hqk", queries, keys, preferred_element_type=jnp.float32) * inv_root
    )
    scores = jnp.where(key_live[None, None, :], scores, NEG)
    row_top = jnp.max(scores, axis=2, keepdims=True)
    raised = jnp.exp(scores - row_top)
    weights = raised / jnp.sum(raised, axis=2, keepdims=True)
    weights_bf = weights.astype(jnp.bfloat16)
    attn_out = jnp.einsum("hqk,khd->qhd", weights_bf, values, preferred_element_type=jnp.float32)
    row_delta = jnp.sum(grads.astype(jnp.float32) * attn_out, axis=2)
    grad_weights = jnp.einsum("qhd,khd->hqk", grads, values, preferred_element_type=jnp.float32)
    grad_scores = weights * (grad_weights - jnp.transpose(row_delta)[:, :, None])
    grad_scores_bf = grad_scores.astype(jnp.bfloat16)
    grad_q = (
        jnp.einsum("hqk,khd->qhd", grad_scores_bf, keys, preferred_element_type=jnp.float32)
        * inv_root
    )
    grad_k = (
        jnp.einsum("hqk,qhd->khd", grad_scores_bf, queries, preferred_element_type=jnp.float32)
        * inv_root
    )
    grad_v = jnp.einsum("hqk,qhd->khd", weights_bf, grads, preferred_element_type=jnp.float32)
    return (grad_q, grad_k, grad_v)


def per_device(query, key, value, control, kernel, grad_out, detail_blocks):
    tile_rows, tile_column_count, channels = query.shape
    tile_tokens = tile_rows * tile_column_count
    tile_blocks = tile_tokens // BLOCK
    row_count = lax.axis_size("trow")
    col_count = lax.axis_size("tcol")
    my_row = lax.axis_index("trow")
    my_col = lax.axis_index("tcol")
    control_ext = with_halo(control, (("trow", 0), ("tcol", 1)), 1).astype(jnp.float32)
    v_ctrl = (
        value.astype(jnp.float32) + conv_taps(control_ext, kernel, tile_rows, tile_column_count)
    ).astype(jnp.bfloat16)
    query_flat = query.reshape(tile_tokens, channels)
    key_flat = key.reshape(tile_tokens, channels)
    value_flat = v_ctrl.reshape(tile_tokens, channels)
    grad_flat = grad_out.reshape(tile_tokens, channels)
    above = from_behind((key_flat, value_flat), "trow", 1)
    below = from_behind((key_flat, value_flat), "trow", -1)
    pattern = detail_blocks[0]
    wanted = lax.dynamic_index_in_dim(pattern, my_col, 0, keepdims=False)
    asked = lax.dynamic_index_in_dim(pattern, my_col, 1, keepdims=False)
    slot_ids = jnp.arange(col_count - 1, dtype=jnp.int32)
    others = slot_ids + (slot_ids >= my_col).astype(jnp.int32)
    wanted_others = wanted[others]
    row_keys, row_values = (
        lax.all_gather(key_flat, "tcol", axis=0, tiled=True),
        lax.all_gather(value_flat, "tcol", axis=0, tiled=True),
    )
    picked = others * tile_blocks + jnp.maximum(wanted_others, 0)
    detail_keys = row_keys.reshape(col_count * tile_blocks, BLOCK, channels)[picked]
    detail_values = row_values.reshape(col_count * tile_blocks, BLOCK, channels)[picked]
    detail_count = (col_count - 1) * BLOCK
    all_keys = jnp.concatenate(
        [key_flat, above[0], below[0], detail_keys.reshape(detail_count, channels)], axis=0
    )
    all_values = jnp.concatenate(
        [value_flat, above[1], below[1], detail_values.reshape(detail_count, channels)], axis=0
    )
    key_live = jnp.concatenate(
        [
            jnp.ones((tile_tokens,), bool),
            jnp.full((tile_tokens,), my_row >= 1),
            jnp.full((tile_tokens,), my_row + 1 < row_count),
            jnp.repeat(wanted_others >= 0, BLOCK),
        ],
        axis=0,
    )
    head_group = math.gcd(HEADS, 4)
    col_span = head_group * HEAD_DIM
    query_parts = []
    key_parts = []
    value_parts = []
    for group_index in range(HEADS // head_group):
        low = group_index * col_span
        high = low + col_span
        grad_q, grad_k, grad_v = attend_group(
            query_flat[:, low:high].reshape(-1, head_group, HEAD_DIM),
            grad_flat[:, low:high].reshape(-1, head_group, HEAD_DIM),
            all_keys[:, low:high].reshape(-1, head_group, HEAD_DIM),
            all_values[:, low:high].reshape(-1, head_group, HEAD_DIM),
            key_live,
        )
        query_parts.append(grad_q.reshape(-1, col_span))
        key_parts.append(grad_k.reshape(-1, col_span))
        value_parts.append(grad_v.reshape(-1, col_span))
    query_gradient_total = jnp.concatenate(query_parts, axis=1)
    grad_k_all = jnp.concatenate(key_parts, axis=1)
    grad_v_all = jnp.concatenate(value_parts, axis=1)
    up_terms = from_behind(
        (grad_k_all[tile_tokens : 2 * tile_tokens], grad_v_all[tile_tokens : 2 * tile_tokens]),
        "trow",
        -1,
    )
    down_terms = from_behind(
        (
            grad_k_all[2 * tile_tokens : 3 * tile_tokens],
            grad_v_all[2 * tile_tokens : 3 * tile_tokens],
        ),
        "trow",
        1,
    )
    slot_k = (
        grad_k_all[3 * tile_tokens :].reshape(col_count - 1, BLOCK, channels).astype(jnp.bfloat16)
    )
    slot_v = (
        grad_v_all[3 * tile_tokens :].reshape(col_count - 1, BLOCK, channels).astype(jnp.bfloat16)
    )
    detail_k = jnp.zeros((col_count, BLOCK, channels), jnp.bfloat16).at[others].set(slot_k)
    detail_v = jnp.zeros((col_count, BLOCK, channels), jnp.bfloat16).at[others].set(slot_v)
    returned_keys, returned_values = (
        lax.all_to_all(detail_k, "tcol", split_axis=0, concat_axis=0, tiled=True),
        lax.all_to_all(detail_v, "tcol", split_axis=0, concat_axis=0, tiled=True),
    )
    tile_owner_lookup = (
        asked[None, :] == jnp.arange(tile_blocks, dtype=jnp.int32)[:, None]
    ).astype(jnp.bfloat16)
    served_keys = jnp.einsum(
        "ev,vsw->esw", tile_owner_lookup, returned_keys, preferred_element_type=jnp.float32
    ).reshape(tile_tokens, channels)
    served_values = jnp.einsum(
        "ev,vsw->esw", tile_owner_lookup, returned_values, preferred_element_type=jnp.float32
    ).reshape(tile_tokens, channels)
    grad_key = (grad_k_all[:tile_tokens] + up_terms[0] + down_terms[0] + served_keys).astype(
        jnp.bfloat16
    )
    grad_value = (grad_v_all[:tile_tokens] + up_terms[1] + down_terms[1] + served_values).astype(
        jnp.bfloat16
    )
    grad_value_img = grad_value.reshape(tile_rows, tile_column_count, channels)
    value_ext = with_halo(grad_value_img, (("trow", 0), ("tcol", 1)), 1).astype(jnp.float32)
    grad_control = conv_back(value_ext, kernel, tile_rows, tile_column_count).astype(jnp.bfloat16)
    grad_value_f = grad_value_img.astype(jnp.float32)
    kernel_rows = []
    for row_off in range(3):
        kernel_cols = []
        for col_off in range(3):
            kernel_cols.append(
                jnp.sum(
                    control_ext[
                        row_off : row_off + tile_rows, col_off : col_off + tile_column_count
                    ]
                    * grad_value_f,
                    axis=(0, 1),
                )
            )
        kernel_rows.append(jnp.stack(kernel_cols, axis=0))
    grad_kernel = lax.psum(jnp.stack(kernel_rows, axis=0), ("trow", "tcol"))
    grad_query = query_gradient_total.astype(jnp.bfloat16).reshape(
        tile_rows, tile_column_count, channels
    )
    return (
        grad_query,
        grad_key.reshape(tile_rows, tile_column_count, channels),
        grad_value_img,
        grad_control,
        grad_kernel,
    )


def solution(mesh):
    return jax.shard_map(
        per_device,
        mesh=mesh,
        in_specs=(
            P("trow", "tcol", None),
            P("trow", "tcol", None),
            P("trow", "tcol", None),
            P("trow", "tcol", None),
            P(),
            P("trow", "tcol", None),
            P("trow", None, None),
        ),
        out_specs=(
            P("trow", "tcol", None),
            P("trow", "tcol", None),
            P("trow", "tcol", None),
            P("trow", "tcol", None),
            P(),
        ),
        check_vma=False,
    )
```

profile of v0, /device:TPU:0, one launch (start us, length us, event | category | flops | bytes accessed | tf_op | source)
XLA Modules:
  0.0 264.7 jit_solution(12409256994165526829)
XLA Ops:
  8.0 1.4 collective-permute-start.1
  9.4 5.5 %collective-permute-start = (bf16[128,1152]{1,0:T(8,128)(2,1)}, bf16[128,1152]{1,0:T(8,128)(2,1)S(1)}, u32[]{:S(2)}, u32[]{:S(2)}) collective-permute-start(bf16[128,1152]{1,0:T(8,128)(2,1)} %bitcast.257), channel_id=1, source_target_pairs={{0,4},{4,8},{8,12},{12,16},{16,20},{20,24},{24,28},{1,5},{5,9},{9,... | collective-permute-start | bytes 884744 | tf_op jit(solution)/shard_map/ppermute | solution.py:32
  15.9 4.8 %collective-permute-start.2 = (bf16[1,64,1152]{2,1,0:T(8,128)(2,1)S(1)}, bf16[1,64,1152]{2,1,0:T(8,128)(2,1)S(1)}, u32[]{:S(2)}, u32[]{:S(2)}) collective-permute-start(bf16[1,64,1152]{2,1,0:T(8,128)(2,1)S(1)} %get-tuple-element.55), channel_id=1, source_target_pairs={{0,4},{4,8},{8,12},{12,16},{16,20},{20,24},{24,28},{1,5},{5,9},{9,... | collective-permute-start | bytes 442376 | tf_op jit(solution)/shard_map/ppermute | solution.py:21
  20.7 1.3 collective-permute-start.3
  24.6 8.3 %collective-permute-done.2 = bf16[1,64,1152]{2,1,0:T(8,128)(2,1)S(1)} collective-permute-done((bf16[1,64,1152]{2,1,0:T(8,128)(2,1)S(1)}, bf16[1,64,1152]{2,1,0:T(8,128)(2,1)S(1)}, u32[]{:S(2)}, u32[]{:S(2)}) %collective-permute-start.2) | collective-permute-done | bytes 147488 | tf_op jit(solution)/shard_map/ppermute | solution.py:21
  34.4 3.0 %collective-permute-start.4 = (bf16[4,1,1152]{2,1,0:T(2,128)(2,1)S(1)}, bf16[4,1,1152]{2,1,0:T(2,128)(2,1)S(1)}, u32[]{:S(2)}, u32[]{:S(2)}) collective-permute-start(bf16[4,1,1152]{2,1,0:T(2,128)(2,1)S(1)} %get-tuple-element.42), channel_id=1, source_target_pairs={{0,1},{1,2},{2,3},{4,5},{5,6},{6,7},{8,9},{9,10},{10,11},{12,13},{... | collective-permute-start | bytes 27656 | tf_op jit(solution)/shard_map/ppermute | solution.py:21
  46.1 1.4 collective-permute-start.7
  47.5 5.7 %collective-permute-start.6 = (bf16[128,1152]{1,0:T(8,128)(2,1)}, bf16[128,1152]{1,0:T(8,128)(2,1)}, u32[]{:S(2)}, u32[]{:S(2)}) collective-permute-start(bf16[128,1152]{1,0:T(8,128)(2,1)} %bitcast.12), channel_id=1, source_target_pairs={{0,4},{4,8},{8,12},{12,16},{16,20},{20,24},{24,28},{1,5},{5,9},{9,... | collective-permute-start | bytes 884744 | tf_op jit(solution)/shard_map/ppermute | solution.py:32
  53.4 2.0 gather_fusion.1
  55.5 1.7 fusion.93
  60.4 1.9 fusion.101
  62.3 1.6 fusion.48
  65.4 1.4 copy.87
  66.8 2.8 %fusion.99 = (f32[4,128]{1,0:T(4,128)S(1)}, f32[4,128,768]{1,2,0:T(8,128)}) fusion(bf16[768,4,72]{0,2,1:T(8,128)(2,1)S(1)} %bitcast.241, bf16[128,4,72]{0,2,1:T(8,128)(2,1)} %bitcast.278, pred[768]{0:T(1024)(128)(4,1)} %pad_add_fusion), kind=kOutput, calls=%fused_computation.184 | convolution fusion | flops 58196736 | bytes 2091776 | tf_op jit(solution)/shard_map/sub | solution.py:66
  69.6 1.6 fusion.50
  71.2 1.9 fusion.100
  73.2 1.6 fusion.49
  76.2 1.4 copy.88
  78.2 1.4 copy.89
  79.7 2.0 fusion.98
  81.7 1.6 fusion.51
  83.3 1.5 fusion.105
  84.8 2.6 copy.90
  87.4 5.0 %concatenate.51 = f32[768,1152]{1,0:T(8,128)} concatenate(f32[768,288]{1,0:T(8,128)} %copy.87, f32[768,288]{1,0:T(8,128)} %copy.88, f32[768,288]{1,0:T(8,128)} %copy.89, f32[768,288]{1,0:T(8,128)} %copy.90), dimensions={1} | concatenate | bytes 7077888 | tf_op jit(solution)/shard_map/concatenate | solution.py:153
  92.4 2.5 slice.404
  94.9 2.4 fusion.90
  97.2 4.9 %collective-permute-start.11 = (f32[128,1152]{1,0:T(8,128)}, f32[128,1152]{1,0:T(8,128)}, u32[]{:S(2)}, u32[]{:S(2)}) collective-permute-start(f32[128,1152]{1,0:T(8,128)} %get-tuple-element.29), channel_id=1, source_target_pairs={{0,4},{4,8},{8,12},{12,16},{16,20},{20,24},{24,28},{1,5},{5,9},{9,... | collective-permute-start | bytes 1769480 | tf_op jit(solution)/shard_map/ppermute | solution.py:32
  102.2 1.5 collective-permute-start.10
  104.8 3.1 %scatter_fusion.1 = bf16[4,128,1152]{2,1,0:T(8,128)(2,1)} fusion(bf16[4,128,1152]{2,1,0:T(8,128)(2,1)} %broadcast.125.clone.1, s32[3]{0:T(128)S(1)} %copy-done.53, bf16[3,128,1152]{2,1,0:T(8,128)(2,1)} %bitcast.230), kind=kCustom, calls=%fused_computation.4 | custom fusion | bytes 2654220 | tf_op jit(solution)/shard_map/scatter | solution.py:174
  107.9 4.3 %all-to-all-start.1 = ((bf16[4,128,1152]{2,1,0:T(8,128)(2,1)}), bf16[4,128,1152]{2,1,0:T(8,128)(2,1)}, u32[]{:S(2)}, u32[]{:S(2)}) async-start(bf16[4,128,1152]{2,1,0:T(8,128)(2,1)} %scatter_fusion.1), calls=%async_computation.1 | async-start | bytes 2359296 | tf_op jit(solution)/shard_map/all_to_all | solution.py:177
  112.2 3.0 %gather_fusion.2 = bf16[3,128,1152]{2,1,0:T(8,128)(2,1)} fusion(bf16[4,128,1152]{2,1,0:T(8,128)(2,1)} %bitcast.260, s32[1024]{0:T(1024)} %copy-done.51), kind=kCustom, calls=%fused_computation.2 | custom fusion | bytes 1769484 | tf_op jit(solution)/shard_map/gather | solution.py:116
  115.2 1.5 pad_maximum_fusion.1
  116.7 2.1 fusion.92
  118.8 2.0 copy.53
  120.8 1.6 fusion.43
  122.4 2.1 fusion.14
  125.5 1.5 convolution_multiply_fusion.3
  127.0 2.1 copy.59
  129.1 1.6 fusion.42
  130.6 2.1 fusion.12
  133.7 1.5 convolution_multiply_fusion.2
  135.2 2.0 copy.65
  137.3 1.3 fusion.41
  138.6 2.1 fusion.10
  141.0 1.6 convolution_multiply_fusion.1
  143.3 1.9 fusion.8
  147.2 8.7 %pad_maximum_fusion.2 = bf16[2,64,1152]{1,0,2:T(2,128)(2,1)S(1)} fusion(bf16[2,64,288]{1,0,2:T(2,128)(2,1)S(1)} %concatenate.48, bf16[2,64,288]{1,0,2:T(2,128)(2,1)S(1)} %concatenate.47, bf16[2,64,288]{1,0,2:T(2,128)(2,1)S(1)} %concatenate.46, bf16[2,64,288]{1,0,2:T(2,128)(2,1)S(1)} %concatenate.45), kind=kLoop, calls=%fused_computation.127 | loop fusion | flops 442368 | bytes 589824 | tf_op jit(solution)/shard_map/concatenate | solution.py:151
  157.5 2.7 %copy.80 = f32[768,288]{1,0:T(8,128)} copy(f32[768,288]{0,1:T(8,128)} %bitcast.232) | data formatting | bytes 1769472 | tf_op jit(solution)/shard_map/reshape | solution.py:149
  160.2 1.5 copy.81
  161.6 1.7 convolution_multiply_fusion
  163.4 1.4 copy.82
  164.8 4.8 %concatenate.50 = f32[768,1152]{1,0:T(8,128)} concatenate(f32[768,288]{1,0:T(8,128)S(1)} %copy.79, f32[768,288]{1,0:T(8,128)} %copy.80, f32[768,288]{1,0:T(8,128)} %copy.81, f32[768,288]{1,0:T(8,128)} %copy.82), dimensions={1} | concatenate | bytes 7077888 | tf_op jit(solution)/shard_map/concatenate | solution.py:152
  169.6 1.6 slice.405
  171.1 2.4 fusion.91
  173.5 4.6 %collective-permute-start.9 = (f32[128,1152]{1,0:T(8,128)}, f32[128,1152]{1,0:T(8,128)S(1)}, u32[]{:S(2)}, u32[]{:S(2)}) collective-permute-start(f32[128,1152]{1,0:T(8,128)} %get-tuple-element.31), channel_id=1, source_target_pairs={{0,4},{4,8},{8,12},{12,16},{16,20},{20,24},{24,28},{1,5},{5,9},{9,... | collective-permute-start | bytes 1769480 | tf_op jit(solution)/shard_map/ppermute | solution.py:32
  180.5 2.8 %scatter_fusion = bf16[4,128,1152]{2,1,0:T(8,128)(2,1)} fusion(bf16[4,128,1152]{2,1,0:T(8,128)(2,1)} %broadcast.125.clone, s32[3]{0:T(128)S(1)} %copy-done.53, bf16[3,128,1152]{2,1,0:T(8,128)(2,1)S(1)} %bitcast.229), kind=kCustom, calls=%fused_computation.3 | custom fusion | bytes 2654220 | tf_op jit(solution)/shard_map/scatter | solution.py:173
  183.3 3.5 %all-to-all-start = ((bf16[4,128,1152]{2,1,0:T(8,128)(2,1)}), bf16[4,128,1152]{2,1,0:T(8,128)(2,1)S(1)}, u32[]{:S(2)}, u32[]{:S(2)}) async-start(bf16[4,128,1152]{2,1,0:T(8,128)(2,1)} %scatter_fusion), calls=%async_computation | async-start | bytes 2359296 | tf_op jit(solution)/shard_map/all_to_all | solution.py:176
  186.8 2.3 fusion.28
  189.1 1.5 fusion.72
  193.3 5.2 %collective-permute-start.12 = (bf16[1,64,1152]{2,1,0:T(8,128)(2,1)}, bf16[1,64,1152]{2,1,0:T(8,128)(2,1)S(1)}, u32[]{:S(2)}, u32[]{:S(2)}) collective-permute-start(bf16[1,64,1152]{2,1,0:T(8,128)(2,1)} %get-tuple-element.44), channel_id=1, source_target_pairs={{0,4},{4,8},{8,12},{12,16},{16,20},{20,24},{24,28},{1,5},{5,9},{9,... | collective-permute-start | bytes 442376 | tf_op jit(solution)/shard_map/ppermute | solution.py:21
  198.7 47.6 %psum.7 = f32[3,3,1152]{2,1,0:T(4,128)} all-reduce(f32[3,3,1152]{2,1,0:T(4,128)S(1)} %pad_maximum_fusion.3), channel_id=1, replica_groups=mesh['trow'=8,'tcol'=4] {'trow','tcol'}, use_global_device_ids=true, to_apply=%region_23.24 | all-reduce | flops 10368 | bytes 82944 | tf_op jit(solution)/shard_map/psum | solution.py:212
  247.7 3.6 %collective-permute-start.14 = (bf16[4,1,1152]{2,1,0:T(2,128)(2,1)S(1)}, bf16[4,1,1152]{2,1,0:T(2,128)(2,1)}, u32[]{:S(2)}, u32[]{:S(2)}) collective-permute-start(bf16[4,1,1152]{2,1,0:T(2,128)(2,1)S(1)} %get-tuple-element.40), channel_id=1, source_target_pairs={{0,1},{1,2},{2,3},{4,5},{5,6},{6,7},{8,9},{9,10},{10,11},{12,13},{... | collective-permute-start | bytes 27656 | tf_op jit(solution)/shard_map/ppermute | solution.py:21
  251.3 1.6 fusion.30
  252.9 2.1 fusion.75
  (231 shorter events, 38.0 us)
Async XLA Ops:
  7.2 16.8 %copy-start.23 = (bf16[2,64,1152]{2,1,0:T(8,128)(2,1)S(1)}, bf16[2,64,1152]{2,1,0:T(8,128)(2,1)}, u32[]{:S(2)}) copy-start(bf16[2,64,1152]{2,1,0:T(8,128)(2,1)} %param.12) | copy-start | bytes 884740
  7.2 17.0 %copy-start.24 = (bf16[2,64,1152]{2,1,0:T(8,128)(2,1)S(1)}, bf16[2,64,1152]{2,1,0:T(8,128)(2,1)}, u32[]{:S(2)}) copy-start(bf16[2,64,1152]{2,1,0:T(8,128)(2,1)} %param.7) | copy-start | bytes 884740
  7.2 17.2 %copy-start.49 = (f32[3,3,1152]{2,1,0:T(4,128)S(1)}, f32[3,3,1152]{2,1,0:T(4,128)}, u32[]{:S(2)}) copy-start(f32[3,3,1152]{2,1,0:T(4,128)} %param.11) | copy-start | bytes 124420
  7.2 46.1 %all-gather.3.cloned.1.call-start = ((), (), s32[]{:S(2)}) async-start(), calls=%async_computation.2 | async-start | bytes 1474560 | tf_op jit(solution)/shard_map/all_gather | solution.py:111
  7.9 25.1 %copy-start.15 = (bf16[2,64,1152]{2,1,0:T(8,128)(2,1)S(1)}, bf16[2,64,1152]{2,1,0:T(8,128)(2,1)}, u32[]{:S(2)}) copy-start(bf16[2,64,1152]{2,1,0:T(8,128)(2,1)} %param.10) | copy-start | bytes 884740
  7.9 104.2 %all-gather.5.cloned.1.call-start = ((), (), s32[]{:S(2)}) async-start(), calls=%async_computation.3 | async-start | bytes 1474560 | tf_op jit(solution)/shard_map/all_gather | solution.py:112
  8.0 47.3 %collective-permute-start.1 = (bf16[128,1152]{1,0:T(8,128)(2,1)}, bf16[128,1152]{1,0:T(8,128)(2,1)S(1)}, u32[]{:S(2)}, u32[]{:S(2)}) collective-permute-start(bf16[128,1152]{1,0:T(8,128)(2,1)} %bitcast.256), channel_id=1, source_target_pairs={{4,0},{8,4},{12,8},{16,12},{20,16},{24,20},{28,24},{5,1},{9,5},{13... | collective-permute-start | bytes 884744 | tf_op jit(solution)/shard_map/ppermute | solution.py:32
  9.4 45.9 %collective-permute-start = (bf16[128,1152]{1,0:T(8,128)(2,1)}, bf16[128,1152]{1,0:T(8,128)(2,1)S(1)}, u32[]{:S(2)}, u32[]{:S(2)}) collective-permute-start(bf16[128,1152]{1,0:T(8,128)(2,1)} %bitcast.257), channel_id=1, source_target_pairs={{0,4},{4,8},{8,12},{12,16},{16,20},{20,24},{24,28},{1,5},{5,9},{9,... | collective-permute-start | bytes 884744 | tf_op jit(solution)/shard_map/ppermute | solution.py:32
  15.9 17.0 %collective-permute-start.2 = (bf16[1,64,1152]{2,1,0:T(8,128)(2,1)S(1)}, bf16[1,64,1152]{2,1,0:T(8,128)(2,1)S(1)}, u32[]{:S(2)}, u32[]{:S(2)}) collective-permute-start(bf16[1,64,1152]{2,1,0:T(8,128)(2,1)S(1)} %get-tuple-element.55), channel_id=1, source_target_pairs={{0,4},{4,8},{8,12},{12,16},{16,20},{20,24},{24,28},{1,5},{5,9},{9,... | collective-permute-start | bytes 442376 | tf_op jit(solution)/shard_map/ppermute | solution.py:21
  20.7 12.3 %collective-permute-start.3 = (bf16[1,64,1152]{2,1,0:T(8,128)(2,1)S(1)}, bf16[1,64,1152]{2,1,0:T(8,128)(2,1)S(1)}, u32[]{:S(2)}, u32[]{:S(2)}) collective-permute-start(bf16[1,64,1152]{2,1,0:T(8,128)(2,1)S(1)} %get-tuple-element.54), channel_id=1, source_target_pairs={{4,0},{8,4},{12,8},{16,12},{20,16},{24,20},{28,24},{5,1},{9,5},{13... | collective-permute-start | bytes 442376 | tf_op jit(solution)/shard_map/ppermute | solution.py:24
  24.3 19.6 %copy-start.54 = (s32[1,4,4]{2,1,0:T(4,128)S(1)}, s32[1,4,4]{2,1,0:T(4,128)}, u32[]{:S(2)}) copy-start(s32[1,4,4]{2,1,0:T(4,128)} %param.13) | copy-start | bytes 196
  24.4 28.9 %copy-start.51 = (s32[1024]{0:T(1024)}, s32[1024]{0:T(1024)S(1)}, u32[]{:S(2)}) copy-start(s32[1024]{0:T(1024)S(1)} %pad_clamp_fusion) | copy-start | bytes 12292
  24.6 20.2 %copy-start.35 = (f32[1152]{0:T(1024)}, f32[1152]{0:T(1024)S(1)}, u32[]{:S(2)}) copy-start(f32[1152]{0:T(1024)S(1)} %get-tuple-element.21) | copy-start | bytes 13828
  24.6 20.2 %copy-start.37 = (f32[1152]{0:T(1024)}, f32[1152]{0:T(1024)S(1)}, u32[]{:S(2)}) copy-start(f32[1152]{0:T(1024)S(1)} %get-tuple-element.22) | copy-start | bytes 13828
  24.6 20.2 %copy-start.39 = (f32[1152]{0:T(1024)}, f32[1152]{0:T(1024)S(1)}, u32[]{:S(2)}) copy-start(f32[1152]{0:T(1024)S(1)} %get-tuple-element.23) | copy-start | bytes 13828
  24.6 20.2 %copy-start.41 = (f32[1152]{0:T(1024)}, f32[1152]{0:T(1024)S(1)}, u32[]{:S(2)}) copy-start(f32[1152]{0:T(1024)S(1)} %get-tuple-element.24) | copy-start | bytes 13828
  24.6 20.2 %copy-start.43 = (f32[1152]{0:T(1024)}, f32[1152]{0:T(1024)S(1)}, u32[]{:S(2)}) copy-start(f32[1152]{0:T(1024)S(1)} %get-tuple-element.25) | copy-start | bytes 13828
  24.6 20.2 %copy-start.45 = (f32[1152]{0:T(1024)}, f32[1152]{0:T(1024)S(1)}, u32[]{:S(2)}) copy-start(f32[1152]{0:T(1024)S(1)} %get-tuple-element.26) | copy-start | bytes 13828
  24.6 20.2 %copy-start.47 = (f32[1152]{0:T(1024)}, f32[1152]{0:T(1024)S(1)}, u32[]{:S(2)}) copy-start(f32[1152]{0:T(1024)S(1)} %get-tuple-element.27) | copy-start | bytes 13828
  33.1 11.5 %collective-permute-start.5 = (bf16[4,1,1152]{2,1,0:T(2,128)(2,1)S(1)}, bf16[4,1,1152]{2,1,0:T(2,128)(2,1)S(1)}, u32[]{:S(2)}, u32[]{:S(2)}) collective-permute-start(bf16[4,1,1152]{2,1,0:T(2,128)(2,1)S(1)} %get-tuple-element.43), channel_id=1, source_target_pairs={{1,0},{2,1},{3,2},{5,4},{6,5},{7,6},{9,8},{10,9},{11,10},{13,12},{... | collective-permute-start | bytes 27656 | tf_op jit(solution)/shard_map/ppermute | solution.py:24
  34.4 10.2 %collective-permute-start.4 = (bf16[4,1,1152]{2,1,0:T(2,128)(2,1)S(1)}, bf16[4,1,1152]{2,1,0:T(2,128)(2,1)S(1)}, u32[]{:S(2)}, u32[]{:S(2)}) collective-permute-start(bf16[4,1,1152]{2,1,0:T(2,128)(2,1)S(1)} %get-tuple-element.42), channel_id=1, source_target_pairs={{0,1},{1,2},{2,3},{4,5},{5,6},{6,7},{8,9},{9,10},{10,11},{12,13},{... | collective-permute-start | bytes 27656 | tf_op jit(solution)/shard_map/ppermute | solution.py:21
  38.8 6.1 %copy-start.25 = (bf16[2,64,1152]{2,1,0:T(8,128)(2,1)S(1)}, bf16[2,64,1152]{2,1,0:T(8,128)(2,1)}, u32[]{:S(2)}) copy-start(bf16[2,64,1152]{2,1,0:T(8,128)(2,1)} %param.9) | copy-start | bytes 884740
  46.1 9.2 %copy-start.14 = (bf16[2,64,1152]{2,1,0:T(8,128)(2,1)S(1)}, bf16[2,64,1152]{2,1,0:T(8,128)(2,1)}, u32[]{:S(2)}) copy-start(bf16[2,64,1152]{2,1,0:T(8,128)(2,1)} %param.8) | copy-start | bytes 884740
  46.1 69.0 %collective-permute-start.7 = (bf16[128,1152]{1,0:T(8,128)(2,1)}, bf16[128,1152]{1,0:T(8,128)(2,1)}, u32[]{:S(2)}, u32[]{:S(2)}) collective-permute-start(bf16[128,1152]{1,0:T(8,128)(2,1)} %bitcast.12), channel_id=1, source_target_pairs={{4,0},{8,4},{12,8},{16,12},{20,16},{24,20},{28,24},{5,1},{9,5},{13... | collective-permute-start | bytes 884744 | tf_op jit(solution)/shard_map/ppermute | solution.py:32
  47.5 67.6 %collective-permute-start.6 = (bf16[128,1152]{1,0:T(8,128)(2,1)}, bf16[128,1152]{1,0:T(8,128)(2,1)}, u32[]{:S(2)}, u32[]{:S(2)}) collective-permute-start(bf16[128,1152]{1,0:T(8,128)(2,1)} %bitcast.12), channel_id=1, source_target_pairs={{0,4},{4,8},{8,12},{12,16},{16,20},{20,24},{24,28},{1,5},{5,9},{9,... | collective-permute-start | bytes 884744 | tf_op jit(solution)/shard_map/ppermute | solution.py:32
  58.5 21.2 %copy-start.6 = (bf16[768,288]{0,1:T(8,128)(2,1)}, bf16[768,288]{0,1:T(8,128)(2,1)S(1)}, u32[]{:S(2)}) copy-start(bf16[768,288]{0,1:T(8,128)(2,1)S(1)} %copy.69) | copy-start | bytes 1327108
  59.7 11.5 %copy-start.10 = (bf16[768,288]{0,1:T(8,128)(2,1)}, bf16[768,288]{0,1:T(8,128)(2,1)S(1)}, u32[]{:S(2)}) copy-start(bf16[768,288]{0,1:T(8,128)(2,1)S(1)} %copy.57) | copy-start | bytes 1327108
  60.0 3.9 %copy-start.12 = (bf16[768,288]{0,1:T(8,128)(2,1)}, bf16[768,288]{0,1:T(8,128)(2,1)S(1)}, u32[]{:S(2)}) copy-start(bf16[768,288]{0,1:T(8,128)(2,1)S(1)} %copy.51) | copy-start | bytes 1327108
  62.3 2.5 copy-start.20
  64.8 2.0 copy-start.8
  69.6 3.5 %copy-start.55 = (f32[4,128]{1,0:T(4,128)}, f32[4,128]{1,0:T(4,128)S(1)}, u32[]{:S(2)}) copy-start(f32[4,128]{1,0:T(4,128)S(1)} %get-tuple-element.58) | copy-start | bytes 6148
  73.2 2.5 copy-start.19
  75.6 2.0 copy-start.18
  77.6 2.0 copy-start.65
  81.7 3.1 %copy-start.57 = (f32[4,128]{1,0:T(4,128)}, f32[4,128]{1,0:T(4,128)S(1)}, u32[]{:S(2)}) copy-start(f32[4,128]{1,0:T(4,128)S(1)} %get-tuple-element.56) | copy-start | bytes 6148
  94.9 9.9 %copy-start.53 = (s32[3]{0:T(128)S(1)}, s32[3]{0:T(128)}, u32[]{:S(2)}) copy-start(s32[3]{0:T(128)} %copy-done.52) | copy-start | bytes 40
  97.2 91.8 %collective-permute-start.11 = (f32[128,1152]{1,0:T(8,128)}, f32[128,1152]{1,0:T(8,128)}, u32[]{:S(2)}, u32[]{:S(2)}) collective-permute-start(f32[128,1152]{1,0:T(8,128)} %get-tuple-element.29), channel_id=1, source_target_pairs={{0,4},{4,8},{8,12},{12,16},{16,20},{20,24},{24,28},{1,5},{5,9},{9,... | collective-permute-start | bytes 1769480 | tf_op jit(solution)/shard_map/ppermute | solution.py:32
  102.2 86.9 %collective-permute-start.10 = (f32[128,1152]{1,0:T(8,128)}, f32[128,1152]{1,0:T(8,128)}, u32[]{:S(2)}, u32[]{:S(2)}) collective-permute-start(f32[128,1152]{1,0:T(8,128)} %get-tuple-element.28), channel_id=1, source_target_pairs={{4,0},{8,4},{12,8},{16,12},{20,16},{24,20},{28,24},{5,1},{9,5},{13... | collective-permute-start | bytes 1769480 | tf_op jit(solution)/shard_map/ppermute | solution.py:32
  107.9 75.4 %all-to-all-start.1 = ((bf16[4,128,1152]{2,1,0:T(8,128)(2,1)}), bf16[4,128,1152]{2,1,0:T(8,128)(2,1)}, u32[]{:S(2)}, u32[]{:S(2)}) async-start(bf16[4,128,1152]{2,1,0:T(8,128)(2,1)} %scatter_fusion.1), calls=%async_computation.1 | async-start | bytes 2359296 | tf_op jit(solution)/shard_map/all_to_all | solution.py:177
  118.8 3.6 %copy-start.62 = (f32[4,128]{1,0:T(4,128)S(1)}, f32[4,128]{1,0:T(4,128)}, u32[]{:S(2)}) copy-start(f32[4,128]{1,0:T(4,128)} %copy-done.61) | copy-start | bytes 6148
  122.4 2.1 copy-start.13
  122.4 3.1 %copy-start.34 = (bf16[128,288]{0,1:T(8,128)(2,1)S(1)}, bf16[128,288]{0,1:T(8,128)(2,1)}, u32[]{:S(2)}) copy-start(bf16[128,288]{0,1:T(8,128)(2,1)} %copy.112) | copy-start | bytes 221188
  127.0 3.6 %copy-start.60 = (f32[4,128]{1,0:T(4,128)S(1)}, f32[4,128]{1,0:T(4,128)}, u32[]{:S(2)}) copy-start(f32[4,128]{1,0:T(4,128)} %copy-done.59) | copy-start | bytes 6148
  130.6 2.1 copy-start.11
  130.6 3.0 %copy-start.32 = (bf16[128,288]{0,1:T(8,128)(2,1)S(1)}, bf16[128,288]{0,1:T(8,128)(2,1)}, u32[]{:S(2)}) copy-start(bf16[128,288]{0,1:T(8,128)(2,1)} %copy.114) | copy-start | bytes 221188
  135.2 3.4 %copy-start.56 = (f32[4,128]{1,0:T(4,128)S(1)}, f32[4,128]{1,0:T(4,128)}, u32[]{:S(2)}) copy-start(f32[4,128]{1,0:T(4,128)} %copy-done.55) | copy-start | bytes 6148
  138.6 2.1 copy-start.9
  138.6 2.4 copy-start.30
  141.0 1.8 copy-start.17
  143.3 2.8 %copy-start.7 = (bf16[768,288]{0,1:T(8,128)(2,1)S(1)}, bf16[768,288]{0,1:T(8,128)(2,1)}, u32[]{:S(2)}) copy-start(bf16[768,288]{0,1:T(8,128)(2,1)} %copy-done.6) | copy-start | bytes 1327108
  146.4 10.7 %copy-start.3 = (f32[4,768,72]{1,2,0:T(8,128)S(1)}, f32[4,768,72]{1,2,0:T(8,128)}, u32[]{:S(2)}) copy-start(f32[4,768,72]{1,2,0:T(8,128)} %convolution_multiply_fusion.3) | copy-start | bytes 2654212
  157.5 2.7 %copy-start.4 = (f32[4,768,72]{1,2,0:T(8,128)S(1)}, f32[4,768,72]{1,2,0:T(8,128)}, u32[]{:S(2)}) copy-start(f32[4,768,72]{1,2,0:T(8,128)} %convolution_multiply_fusion.1) | copy-start | bytes 2654212
  157.5 4.1 %copy-start.29 = (bf16[128,288]{0,1:T(8,128)(2,1)S(1)}, bf16[128,288]{0,1:T(8,128)(2,1)}, u32[]{:S(2)}) copy-start(bf16[128,288]{0,1:T(8,128)(2,1)} %copy.118) | copy-start | bytes 221188
  173.5 79.4 %collective-permute-start.9 = (f32[128,1152]{1,0:T(8,128)}, f32[128,1152]{1,0:T(8,128)S(1)}, u32[]{:S(2)}, u32[]{:S(2)}) collective-permute-start(f32[128,1152]{1,0:T(8,128)} %get-tuple-element.31), channel_id=1, source_target_pairs={{0,4},{4,8},{8,12},{12,16},{16,20},{20,24},{24,28},{1,5},{5,9},{9,... | collective-permute-start | bytes 1769480 | tf_op jit(solution)/shard_map/ppermute | solution.py:32
  178.1 74.8 %collective-permute-start.8 = (f32[128,1152]{1,0:T(8,128)}, f32[128,1152]{1,0:T(8,128)}, u32[]{:S(2)}, u32[]{:S(2)}) collective-permute-start(f32[128,1152]{1,0:T(8,128)} %get-tuple-element.30), channel_id=1, source_target_pairs={{4,0},{8,4},{12,8},{16,12},{20,16},{24,20},{28,24},{5,1},{9,5},{13... | collective-permute-start | bytes 1769480 | tf_op jit(solution)/shard_map/ppermute | solution.py:32
  183.3 3.5 %copy-start.66 = (pred[4]{0:T(512)(128)(4,1)S(1)}, pred[4]{0:T(512)(128)(4,1)}, u32[]{:S(2)}) copy-start(pred[4]{0:T(512)(128)(4,1)} %fusion.76) | copy-start | bytes 16
  183.3 68.0 %all-to-all-start = ((bf16[4,128,1152]{2,1,0:T(8,128)(2,1)}), bf16[4,128,1152]{2,1,0:T(8,128)(2,1)S(1)}, u32[]{:S(2)}, u32[]{:S(2)}) async-start(bf16[4,128,1152]{2,1,0:T(8,128)(2,1)} %scatter_fusion), calls=%async_computation | async-start | bytes 2359296 | tf_op jit(solution)/shard_map/all_to_all | solution.py:176
  190.6 65.0 %copy-start = (bf16[128,1152]{1,0:T(8,128)(2,1)}, bf16[128,1152]{1,0:T(8,128)(2,1)S(1)}, u32[]{:S(2)}) copy-start(bf16[128,1152]{1,0:T(8,128)(2,1)S(1)} %fusion.72) | copy-start | bytes 884740
  192.0 54.3 %collective-permute-start.13 = (bf16[1,64,1152]{2,1,0:T(8,128)(2,1)}, bf16[1,64,1152]{2,1,0:T(8,128)(2,1)S(1)}, u32[]{:S(2)}, u32[]{:S(2)}) collective-permute-start(bf16[1,64,1152]{2,1,0:T(8,128)(2,1)} %get-tuple-element.45), channel_id=1, source_target_pairs={{4,0},{8,4},{12,8},{16,12},{20,16},{24,20},{28,24},{5,1},{9,5},{13... | collective-permute-start | bytes 442376 | tf_op jit(solution)/shard_map/ppermute | solution.py:24
  193.3 53.0 %collective-permute-start.12 = (bf16[1,64,1152]{2,1,0:T(8,128)(2,1)}, bf16[1,64,1152]{2,1,0:T(8,128)(2,1)S(1)}, u32[]{:S(2)}, u32[]{:S(2)}) collective-permute-start(bf16[1,64,1152]{2,1,0:T(8,128)(2,1)} %get-tuple-element.44), channel_id=1, source_target_pairs={{0,4},{4,8},{8,12},{12,16},{16,20},{20,24},{24,28},{1,5},{5,9},{9,... | collective-permute-start | bytes 442376 | tf_op jit(solution)/shard_map/ppermute | solution.py:21
  246.3 5.0 %copy-start.21 = (bf16[1,64,1152]{2,1,0:T(8,128)(2,1)}, bf16[1,64,1152]{2,1,0:T(8,128)(2,1)S(1)}, u32[]{:S(2)}) copy-start(bf16[1,64,1152]{2,1,0:T(8,128)(2,1)S(1)} %collective-permute-done.12) | copy-start | bytes 442372
  246.4 8.7 %collective-permute-start.15 = (bf16[4,1,1152]{2,1,0:T(2,128)(2,1)S(1)}, bf16[4,1,1152]{2,1,0:T(2,128)(2,1)S(1)}, u32[]{:S(2)}, u32[]{:S(2)}) collective-permute-start(bf16[4,1,1152]{2,1,0:T(2,128)(2,1)S(1)} %get-tuple-element.41), channel_id=1, source_target_pairs={{1,0},{2,1},{3,2},{5,4},{6,5},{7,6},{9,8},{10,9},{11,10},{13,12},{... | collective-permute-start | bytes 27656 | tf_op jit(solution)/shard_map/ppermute | solution.py:24
  247.7 8.0 %collective-permute-start.14 = (bf16[4,1,1152]{2,1,0:T(2,128)(2,1)S(1)}, bf16[4,1,1152]{2,1,0:T(2,128)(2,1)}, u32[]{:S(2)}, u32[]{:S(2)}) collective-permute-start(bf16[4,1,1152]{2,1,0:T(2,128)(2,1)S(1)} %get-tuple-element.40), channel_id=1, source_target_pairs={{0,1},{1,2},{2,3},{4,5},{5,6},{6,7},{8,9},{9,10},{10,11},{12,13},{... | collective-permute-start | bytes 27656 | tf_op jit(solution)/shard_map/ppermute | solution.py:21
  252.9 2.8 %copy-start.22 = (bf16[1,64,1152]{2,1,0:T(8,128)(2,1)S(1)}, bf16[1,64,1152]{2,1,0:T(8,128)(2,1)}, u32[]{:S(2)}) copy-start(bf16[1,64,1152]{2,1,0:T(8,128)(2,1)} %copy-done.21) | copy-start | bytes 442372
  (23 other events, 28.7 us)
Sparse Core Ops, SparseCore 0:
  9.6 20.1 all-gather.2
  53.4 18.3 all-gather.4
where the time goes:
time: 268 us; the launch traced here: 265 us
  local copies, waits for them, and re-layouts  73.5 us (27%)
  starting transfers between devices  56 us (21%)
  blocking collectives  47.6 us (18%)
  matrix products  37.5 us (14%)
  other arithmetic  25.7 us (10%)
  between operations  15.2 us (6%)
  waiting for transfers between devices  9.13 us (3%)
    psum x1, blocking collectives, per_device(): grad_kernel = lax.psum(jnp.stack(kernel_rows, axis=0), ('trow', 'tcol'))  47.6 us
    ppermute x8, starting transfers between devices, from_behind(): return lax.ppermute(shard, axis, pairs)  26.3 us
    ppermute x4, starting transfers between devices, with_halo(): lax.ppermute(lax.slice_in_dim(block, block.shape[dim] - width, None, axis...  16.7 us
    unnamed x145, local copies, waits for them, and re-layouts  12.1 us
    concatenate x1, other arithmetic, per_device(): query_gradient_total = jnp.concatenate(query_parts, axis=1)  8.66 us
    sub x4, matrix products, attend_group(): raised = jnp.exp(scores - row_top)  8.63 us
    slice x5, local copies, waits for them, and re-layouts, per_device(): all_values[:, low:high].reshape(-1, head_group, HEAD_DIM)  8.46 us
    ppermute x4, waiting for transfers between devices, with_halo(): lax.ppermute(lax.slice_in_dim(block, block.shape[dim] - width, None, axis...  8.36 us
  transfers between devices with their start and end apart: 20, of which 1 were waited for; matrix products, arithmetic and copies ran while one was open for 49% of the time, Pallas kernels for 0%

commit v1 on v0

v1 whole, which is shorter than its diff:
```python
import functools

import jax
import jax.numpy as jnp
from jax import lax
from jax.experimental import pallas as pl
from jax.experimental.pallas import tpu as pltpu
from jax.sharding import Mesh, PartitionSpec as P

HEADS = 16
HEAD_DIM = 72
ROWS = 2
LANES = 128
HALF = 64
NEG = -1e30
INV_ROOT = HEAD_DIM ** (-0.5)
LOG2E = 1.4426950408889634
BF = jnp.bfloat16
F32 = jnp.float32


def params(mib):
    return pltpu.CompilerParams(vmem_limit_bytes=mib << 20)


def call(body, outs, *args, scratch=(), flops=0, mib=24):
    outs = [jax.ShapeDtypeStruct(shape, dtype) for shape, dtype in outs]
    moved = sum(a.size * a.dtype.itemsize for a in list(args) + outs)
    return pl.pallas_call(
        body,
        out_shape=outs,
        scratch_shapes=list(scratch),
        compiler_params=params(mib),
        cost_estimate=pl.CostEstimate(flops=flops, bytes_accessed=moved, transcendentals=0),
    )(*args)


def pack_body(parts, ch, *refs):
    ins, out = refs[:parts], refs[-1]
    pad = out.shape[2] - ch
    for n, ref in enumerate(ins):
        x = ref[...]
        if ch % 16:
            x = x.astype(F32)
        x = x.T
        for p in range(out.shape[0]):
            piece = x[p * ch : (p + 1) * ch]
            if pad:
                piece = jnp.concatenate([piece, jnp.zeros((pad, LANES), piece.dtype)], axis=0)
            out[p, n] = piece.astype(BF)


def pack_live_body(parts, ch, *refs):
    pack_body(parts, ch, *refs[:parts], refs[-2])
    refs[-1][...] = refs[parts][...]


def unpack_body(parts, ch, x_ref, g_ref, *outs):
    peers = x_ref.shape[0]
    for n in range(parts):
        pieces = [x_ref[p, n] for p in range(peers)]
        if ch % 16:
            pieces = [piece.astype(F32)[:ch] for piece in pieces]
        whole = jnp.concatenate(pieces, axis=0)
        outs[n][...] = whole.T.astype(BF)
    wide = outs[-1].shape[2]
    blocks = g_ref.shape[2]
    acc = outs[-1]
    total = [jnp.zeros((16, LANES), F32) for _ in range(wide // LANES + 2)]
    lane = lax.broadcasted_iota(jnp.int32, (16, LANES), 1)
    for p in range(peers):
        first, off = divmod(p * ch, LANES)
        for b in range(blocks):
            piece = g_ref[p, 0, b].astype(F32) + g_ref[p, 1, b].astype(F32)
            turned = pltpu.roll(piece, off, 1) if off else piece
            total[first + b] = total[first + b] + jnp.where(lane >= off, turned, 0.0)
            if off:
                total[first + b + 1] = total[first + b + 1] + jnp.where(lane < off, turned, 0.0)
    total = jnp.concatenate(total[: wide // LANES], axis=1)
    for a in range(3):
        acc[a] = total[3 * a : 3 * a + 3]


def lane_masks(rows):
    lane = lax.broadcasted_iota(jnp.int32, (rows, LANES), 1)
    col = lane & (HALF - 1)
    return lane >= HALF, col == 0, col == HALF - 1


def col_shifts(tiles, masks):
    _, first, last = masks
    swapped = [pltpu.roll(t, HALF, 1) for t in tiles]
    none = jnp.zeros_like(tiles[0])
    out = []
    for j, t in enumerate(tiles):
        before = swapped[j - 1] if j else none
        after = swapped[j + 1] if j + 1 < len(tiles) else none
        out.append(
            (
                pltpu.roll(jnp.where(last, before, t), 1, 1),
                t,
                pltpu.roll(jnp.where(first, after, t), LANES - 1, 1),
            )
        )
    return out


def conv_rows(rows, coef, masks):
    second = masks[0]
    count = len(rows)
    shifted = [col_shifts(row, masks) for row in rows]
    terms = []
    for i, row in enumerate(shifted):
        use = [i < count - 1, 0 < i < count - 1, i > 0]
        terms.append(
            [
                [
                    sum(coef[3 * a + b] * t[b] for b in range(3)) if use[a] else None
                    for a in range(3)
                ]
                for t in row
            ]
        )
    out = []
    for i in range(1, count - 1):
        line = []
        for j in range(len(rows[0])):
            up = jnp.where(second, terms[i - 1][j][0], terms[i][j][0])
            down = jnp.where(second, terms[i][j][2], terms[i + 1][j][2])
            line.append(terms[i][j][1] + pltpu.roll(up + down, HALF, 1))
        out.append(line)
    return out


def taps(kc_ref, at):
    block = kc_ref[at, :]
    return [jnp.broadcast_to(block[:, t : t + 1], (16, LANES)) for t in range(9)]


def attend_body(
    heads, a_ref, u_ref, d_ref, q_ref, live_ref, ends_ref, kc_ref, dq_ref, up_ref, down_ref, dk_ref, dv_ref,
    kt, vt, acc_k, acc_v,
):
    peers = a_ref.shape[0]
    cols = peers // ROWS
    chp = a_ref.shape[2]
    wide = cols * LANES

    @pl.loop(0, chp // 16)
    def _(step):
        at = pl.ds(pl.multiple_of(step * 16, 16), 16)
        masks = lane_masks(16)
        coef = taps(kc_ref, at)
        rows = (
            [[u_ref[j, 3, at, :].astype(F32) for j in range(cols)]]
            + [[u_ref[j, 2, at, :].astype(F32) for j in range(cols)]]
            + [[a_ref[r * cols + j, 2, at, :].astype(F32) for j in range(cols)] for r in range(ROWS)]
            + [[d_ref[j, 2, at, :].astype(F32) for j in range(cols)]]
            + [[d_ref[j, 3, at, :].astype(F32) for j in range(cols)]]
        )
        conv = conv_rows(rows, coef, masks)
        for j in range(cols):
            span = slice(j * LANES, (j + 1) * LANES)
            for i in range(ROWS + 2):
                if i == 0:
                    k, v = u_ref[j, 0, at, :], u_ref[j, 1, at, :]
                elif i <= ROWS:
                    k, v = a_ref[(i - 1) * cols + j, 0, at, :], a_ref[(i - 1) * cols + j, 1, at, :]
                else:
                    k, v = d_ref[j, 0, at, :], d_ref[j, 1, at, :]
                kt[i, at, span] = k
                vt[i, at, span] = (v.astype(F32) + conv[i][j]).astype(BF)

    acc_k[...] = jnp.zeros_like(acc_k)
    acc_v[...] = jnp.zeros_like(acc_v)
    chan = lax.broadcasted_iota(jnp.int32, (chp, LANES), 0)
    mine = [(chan >= h * HEAD_DIM) & (chan < (h + 1) * HEAD_DIM) for h in range(heads)]

    def spread(x):
        x = x.astype(F32)
        return jnp.concatenate([jnp.where(m, x, 0.0) for m in mine], axis=1).astype(BF)

    def dot(x, y, on_x, on_y):
        return lax.dot_general(
            x, y, (((on_x,), (on_y,)), ((), ())), preferred_element_type=F32
        )

    for r in range(ROWS):

        @pl.loop(0, cols)
        def _(j, r=r):
            tile = r * cols + j
            span = pl.ds(pl.multiple_of(j * LANES, LANES), LANES)
            q = spread(q_ref[tile, 0])
            g = spread(q_ref[tile, 1])
            k = jnp.concatenate([kt[r + 1], kt[r, :, span], kt[r + 2, :, span]], axis=1)
            v = jnp.concatenate([vt[r + 1], vt[r, :, span], vt[r + 2, :, span]], axis=1)
            live = live_ref[tile].astype(F32)
            zero = jnp.zeros((1, LANES), F32)
            bias = jnp.concatenate(
                [live[p : p + 1] for p in range(cols)]
                + [
                    ends_ref[0:1] if r == 0 else zero,
                    ends_ref[1:2] if r == ROWS - 1 else zero,
                ],
                axis=1,
            )
            s = dot(q, k, 0, 0) + bias
            top = jnp.max(s, axis=1, keepdims=True)
            e = jnp.exp2((s - top) * (INV_ROOT * LOG2E))
            w = e * (1.0 / jnp.sum(e, axis=1, keepdims=True))
            gw = dot(g, v, 0, 0)
            delta = jnp.sum(w * gw, axis=1, keepdims=True)
            gs = (w * (gw - delta)).astype(BF)
            dk = dot(q, gs, 1, 0)
            dv = dot(g, w.astype(BF), 1, 0)
            dq = dot(k, gs, 1, 1)
            own = dq[:, :LANES]
            for h in range(1, heads):
                own = jnp.where(mine[h], dq[:, h * LANES : (h + 1) * LANES], own)
            dq_ref[tile] = (own * INV_ROOT).astype(BF)
            for acc, part in ((acc_k, dk), (acc_v, dv)):
                acc[r + 1] += part[:, :wide]
                acc[r, :, span] += part[:, wide : wide + LANES]
                acc[r + 2, :, span] += part[:, wide + LANES :]

    second = lax.broadcasted_iota(jnp.int32, (chp, LANES), 1) >= HALF
    for r in range(ROWS):
        dk_ref[r] = acc_k[r + 1] * INV_ROOT
    dv_ref[...] = acc_v[...]
    for out, i, rim in ((up_ref, 0, 1), (down_ref, ROWS + 1, ROWS)):
        for j in range(cols):
            span = slice(j * LANES, (j + 1) * LANES)
            out[j] = (acc_k[i, :, span] * INV_ROOT).astype(BF)
            out[cols + j] = acc_v[i, :, span].astype(BF)
        for m in range(cols // 2):
            left = acc_v[rim, :, 2 * m * LANES : (2 * m + 1) * LANES]
            right = acc_v[rim, :, (2 * m + 1) * LANES : (2 * m + 2) * LANES]
            if i == 0:
                both = jnp.where(second, pltpu.roll(right, HALF, 1), left)
            else:
                both = jnp.where(second, right, pltpu.roll(left, HALF, 1))
            out[2 * cols + m] = both.astype(BF)


def kernel_grad_body(a_ref, u_ref, d_ref, dv_ref, out_ref):
    cols = a_ref.shape[0] // ROWS
    chp = a_ref.shape[2]

    @pl.loop(0, chp // 16)
    def _(step):
        at = pl.ds(pl.multiple_of(step * 16, 16), 16)
        masks = lane_masks(16)
        second = masks[0]
        rows = (
            [[u_ref[j, 3, at, :].astype(F32) for j in range(cols)]]
            + [[u_ref[j, 2, at, :].astype(F32) for j in range(cols)]]
            + [[a_ref[r * cols + j, 2, at, :].astype(F32) for j in range(cols)] for r in range(ROWS)]
            + [[d_ref[j, 2, at, :].astype(F32) for j in range(cols)]]
            + [[d_ref[j, 3, at, :].astype(F32) for j in range(cols)]]
        )
        shifted = [col_shifts(row, masks) for row in rows]
        acc = [jnp.zeros((16, LANES), F32) for _ in range(9)]
        for i in range(ROWS + 2):
            for j in range(cols):
                g = dv_ref[i, at, j * LANES : (j + 1) * LANES]
                turned = pltpu.roll(g, HALF, 1)
                above, here, below = (shifted[i + n][j] for n in range(3))
                for b in range(3):
                    acc[b] += jnp.where(second, above[b], here[b]) * turned
                    acc[3 + b] += here[b] * g
                    acc[6 + b] += jnp.where(second, here[b], below[b]) * turned
        lane = lax.broadcasted_iota(jnp.int32, (16, LANES), 1)
        out = jnp.zeros((16, LANES), F32)
        for t in range(9):
            out = jnp.where(lane == t, jnp.sum(acc[t], axis=1, keepdims=True), out)
        out_ref[at, :] = out


def finish_body(ch, dq_ref, dk_ref, dv_ref, u_ref, d_ref, kc_ref, gk_ref, out_ref, g_ref):
    cols = dq_ref.shape[0] // ROWS
    chp = dq_ref.shape[1]

    @pl.loop(0, chp // 16)
    def _(step):
        at = pl.ds(pl.multiple_of(step * 16, 16), 16)
        masks = lane_masks(16)
        second = masks[0]
        coef = taps(kc_ref, at)[::-1]

        def from_side(ref, n):
            return ref[n, at, :].astype(F32)

        def rounded(x):
            return x.astype(BF).astype(F32)

        rows = []
        for i in range(ROWS + 2):
            row = []
            for j in range(cols):
                x = dv_ref[i, at, j * LANES : (j + 1) * LANES]
                if i == 0:
                    rim = from_side(u_ref, 2 * cols + j // 2)
                    x = x + (rim if j % 2 else pltpu.roll(rim, HALF, 1))
                elif i == ROWS + 1:
                    rim = from_side(d_ref, 2 * cols + j // 2)
                    x = x + (pltpu.roll(rim, HALF, 1) if j % 2 else rim)
                else:
                    if i == 1:
                        x = x + from_side(u_ref, cols + j)
                    if i == ROWS:
                        x = x + from_side(d_ref, cols + j)
                row.append(rounded(x))
            rows.append(row)
        conv = conv_rows(rows, coef, masks)
        for r in range(ROWS):
            for j in range(cols):
                tile = r * cols + j
                k = dk_ref[r, at, j * LANES : (j + 1) * LANES]
                if r == 0:
                    k = k + from_side(u_ref, j)
                if r == ROWS - 1:
                    k = k + from_side(d_ref, j)
                out_ref[tile, 0, at, :] = dq_ref[tile, at, :]
                out_ref[tile, 1, at, :] = k.astype(BF)
                out_ref[tile, 2, at, :] = rows[r + 1][j].astype(BF)
                out_ref[tile, 3, at, :] = conv[r][j].astype(BF)

    turned = gk_ref[...].T[:16]
    blocks = g_ref.shape[2]
    if blocks * LANES > chp:
        turned = jnp.concatenate([turned, jnp.zeros((16, blocks * LANES - chp), F32)], axis=1)
    lane = lax.broadcasted_iota(jnp.int32, turned.shape, 1)
    turned = jnp.where(lane < ch, turned, 0.0)
    high = turned.astype(BF)
    low = (turned - high.astype(F32)).astype(BF)
    for tile in range(out_ref.shape[0]):
        for b in range(blocks):
            g_ref[tile, 0, b] = high[:, b * LANES : (b + 1) * LANES]
            g_ref[tile, 1, b] = low[:, b * LANES : (b + 1) * LANES]


def per_device(query, key, value, control, kernel, grad_out, detail_blocks):
    shape = query.shape
    channels = shape[2]
    planes = lax.axis_size("z")
    cols = lax.axis_size("c")
    peers = ROWS * cols
    heads = HEADS // peers
    ch = heads * HEAD_DIM
    chp = -(-ch // 16) * 16
    plane = ("x", "c")
    my_z = lax.axis_index("z")
    my_col = lax.axis_index("c")
    me = lax.axis_index("x") * cols + my_col

    def flat(x):
        return x.reshape(LANES, channels)

    def swap(x):
        rows = x.shape[1] * x.shape[2]
        out = lax.all_to_all(x.reshape(peers, rows, LANES), plane, 0, 0, tiled=True)
        return out.reshape(x.shape)

    (sent,) = call(
        functools.partial(pack_body, 3, ch),
        [((peers, 3, chp, LANES), BF)],
        flat(key), flat(value), flat(control),
    )
    mine = swap(sent)
    down_pairs = [(i, i + 1) for i in range(planes - 1)]
    up_pairs = [(i + 1, i) for i in range(planes - 1)]
    first, last = mine[:cols], mine[cols:]
    above = lax.ppermute(jnp.concatenate([last, first[:, 2:]], axis=1), "z", down_pairs)
    below = lax.ppermute(jnp.concatenate([first, last[:, 2:]], axis=1), "z", up_pairs)

    wanted = lax.dynamic_index_in_dim(detail_blocks[0], my_col, 0, keepdims=False)
    named = (wanted >= 0) | (jnp.arange(cols) == my_col)
    bias = jnp.where(named, 0.0, NEG).astype(F32)
    bias = jnp.broadcast_to(jnp.pad(bias, (0, 16 - cols))[:, None], (16, LANES)).astype(BF)
    (sent_q,) = call(
        functools.partial(pack_body, 2, ch),
        [((peers, 2, chp, LANES), BF)],
        flat(query), flat(grad_out),
    )
    got = lax.all_to_all(
        jnp.concatenate(
            [sent_q.reshape(peers, 2 * chp, LANES), jnp.broadcast_to(bias, (peers, 16, LANES))],
            axis=1,
        ),
        plane, 0, 0, tiled=True,
    )
    grads = got[:, : 2 * chp].reshape(peers, 2, chp, LANES)
    live = got[:, 2 * chp :]
    ends = jnp.where(jnp.stack([my_z >= 1, my_z + 1 < planes]), 0.0, NEG).astype(F32)
    ends = jnp.broadcast_to(jnp.pad(ends, (0, 6))[:, None], (8, LANES))
    coefs = lax.dynamic_slice_in_dim(kernel.reshape(9, channels), me * ch, ch, 1)
    coefs = jnp.pad(coefs.T, ((0, chp - ch), (0, LANES - 9)))

    wide = cols * LANES
    side = (2 * cols + cols // 2, chp, LANES)
    flops = 10 * peers * heads * LANES * (wide + 2 * LANES) * 256
    dq, to_up, to_down, dk, dv = call(
        functools.partial(attend_body, heads),
        [
            ((peers, chp, LANES), BF),
            (side, BF),
            (side, BF),
            ((ROWS, chp, wide), F32),
            ((ROWS + 2, chp, wide), F32),
        ],
        mine, above, below, grads, live, ends, coefs,
        scratch=[
            pltpu.VMEM((ROWS + 2, chp, wide), BF),
            pltpu.VMEM((ROWS + 2, chp, wide), BF),
            pltpu.VMEM((ROWS + 2, chp, wide), F32),
            pltpu.VMEM((ROWS + 2, chp, wide), F32),
        ],
        flops=flops,
        mib=32,
    )
    from_below = lax.ppermute(to_up, "z", up_pairs)
    from_above = lax.ppermute(to_down, "z", down_pairs)
    (gk,) = call(kernel_grad_body, [((chp, LANES), F32)], mine, above, below, dv)
    gk = lax.psum(gk, "z")
    blocks = -(-ch // LANES)
    results, gk_sent = call(
        functools.partial(finish_body, ch),
        [((peers, 4, chp, LANES), BF), ((peers, 2, blocks, 16, LANES), BF)],
        dq, dk, dv, from_above, from_below, coefs, gk,
    )
    back = lax.all_to_all(
        jnp.concatenate(
            [results.reshape(peers, 4 * chp, LANES), gk_sent.reshape(peers, 32 * blocks, LANES)],
            axis=1,
        ),
        plane, 0, 0, tiled=True,
    )
    outs = call(
        functools.partial(unpack_body, 4, ch),
        [((LANES, channels), BF)] * 4 + [((3, 3, channels), F32)],
        back[:, : 4 * chp].reshape(peers, 4, chp, LANES),
        back[:, 4 * chp :].reshape(peers, 2, blocks, 16, LANES),
    )
    return tuple(x.reshape(shape) for x in outs[:4]) + (outs[4],)


def solution(mesh):
    trow, tcol = mesh.shape["trow"], mesh.shape["tcol"]
    grid = Mesh(mesh.devices.reshape(trow // ROWS, ROWS, tcol), ("z", "x", "c"))
    tiled = P(("z", "x"), "c", None)
    return jax.shard_map(
        per_device,
        mesh=grid,
        in_specs=(tiled, tiled, tiled, tiled, P(), tiled, P(("z", "x"), None, None)),
        out_specs=(tiled, tiled, tiled, tiled, P()),
        check_vma=False,
    )
```

time: 268 us -> 146 us (0.54)
  local copies, waits for them, and re-layouts: 73.5 us -> 9.21 us
  waiting for transfers between devices: 9.13 us -> 54.5 us
  matrix products: 37.5 us -> 0 us
  starting transfers between devices: 56 us -> 20.4 us
  blocking collectives: 47.6 us -> 20.9 us
  Pallas kernels: 0 us -> 22.9 us
  other arithmetic: 25.7 us -> 2.92 us
    psum x1 -> x0, blocking collectives: 47.6 us -> none  [per_device(): grad_kernel = lax.psum(jnp.stack(kernel_rows, axis=0), ('trow', 'tcol'))]
    ppermute x16 -> x4, starting transfers between devices: 48.1 us -> 11.5 us  [the longest x1 4.58 us: per_device(): lax.ppermute(jnp.concatenate([last, first[:, 2:]], axis=1), 'z', down_pairs)]
    psum x0 -> x1, waiting for transfers between devices: none -> 34 us  [per_device(): gk = lax.psum(gk, 'z')]
    dot_general x22 -> x0, matrix products: 28.9 us -> none  [the longest x4 8.19 us: attend_group(): jnp.einsum('qhd,khd->hqk', grads, values, preferred_element_type=jnp.floa...]
    slice x20 -> x7, local copies, waits for them, and re-layouts: 24 us -> 0.21 us  [the longest x1 0.08 us: per_device(): back[:, :4 * chp].reshape(peers, 4, chp, LANES)]
    pallas_call x0 -> x6, Pallas kernels: none -> 22.9 us  [call(): pl.pallas_call(body, out_shape=outs, scratch_shapes=list(scratch), compil...]
    all_to_all x0 -> x1, blocking collectives: none -> 20.9 us  [per_device(): lax.all_to_all(jnp.concatenate([results.reshape(peers, 4 * chp, LANES), g...]
    all_to_all x2, waiting for transfers between devices: 0.01 us -> 20.5 us  [the longest x1 11.7 us: swap(): out = lax.all_to_all(x.reshape(peers, rows, LANES), plane, 0, 0, tiled=True)]
  transfers between devices with their start and end apart: 20 -> 7, of which waited for: 1 -> 3; matrix products, arithmetic and copies ran while one was open for 49% -> 2% of each run, Pallas kernels for 0% -> 2%
where the time goes in v1:
time: 146 us; the launch traced here: 145 us
  waiting for transfers between devices  54.5 us (37%)
  Pallas kernels  22.9 us (16%)
  blocking collectives  20.9 us (14%)
  starting transfers between devices  20.4 us (14%)
  between operations  14.2 us (10%)
  local copies, waits for them, and re-layouts  9.21 us (6%)
  other arithmetic  2.92 us (2%)
    psum x1, waiting for transfers between devices, per_device(): gk = lax.psum(gk, 'z')  34 us
    pallas_call x6, Pallas kernels, call(): pl.pallas_call(body, out_shape=outs, scratch_shapes=list(scratch), compil...  22.9 us
    all_to_all x1, blocking collectives, per_device(): lax.all_to_all(jnp.concatenate([results.reshape(peers, 4 * chp, LANES), g...  20.9 us
    all_to_all x1, waiting for transfers between devices, swap(): out = lax.all_to_all(x.reshape(peers, rows, LANES), plane, 0, 0, tiled=True)  11.7 us
    all_to_all x1, waiting for transfers between devices, per_device(): lax.all_to_all(jnp.concatenate([sent_q.reshape(peers, 2 * chp, LANES), jn...  8.79 us
    unnamed x25, local copies, waits for them, and re-layouts  8.17 us
    all_to_all x1, starting transfers between devices, swap(): out = lax.all_to_all(x.reshape(peers, rows, LANES), plane, 0, 0, tiled=True)  5.3 us
    ppermute x1, starting transfers between devices, per_device(): lax.ppermute(jnp.concatenate([last, first[:, 2:]], axis=1), 'z', down_pairs)  4.58 us
  transfers between devices with their start and end apart: 7, of which 3 were waited for; matrix products, arithmetic and copies ran while one was open for 2% of the time, Pallas kernels for 2%

profile of v1, /device:TPU:0, one launch (start us, length us, event | category | flops | bytes accessed | tf_op | source)
XLA Modules:
  0.0 145.0 jit_solution(10583241720178176375)
XLA Ops:
  7.2 0.0 copy-start.5
  7.2 1.0 copy-done.5
  8.1 0.0 copy-start.6
  8.1 1.0 copy-done.6
  9.1 0.0 copy-start.7
  9.1 1.0 copy-done.7
  10.1 1.2 shard_map.110
  11.3 0.0 copy-start.8
  11.3 0.0 copy-start.9
  11.3 5.3 %all-to-all-start = ((bf16[8,432,128]{2,1,0:T(8,128)(2,1)}), bf16[8,432,128]{2,1,0:T(8,128)(2,1)S(1)}, u32[]{:S(2)}, u32[]{:S(2)}) async-start(bf16[8,432,128]{2,1,0:T(8,128)(2,1)} %bitcast.3), calls=%async_computation | async-start | bytes 1769472 | tf_op jit(solution)/shard_map/all_to_all | solution.py:362
  16.6 0.0 copy-done.8
  16.6 0.0 copy-done.9
  16.6 0.2 shard_map.111
  16.8 0.7 fusion.2
  17.5 0.1 fusion
  17.6 11.7 %all-to-all-done = bf16[8,432,128]{2,1,0:T(8,128)(2,1)S(1)} async-done(((bf16[8,432,128]{2,1,0:T(8,128)(2,1)}), bf16[8,432,128]{2,1,0:T(8,128)(2,1)S(1)}, u32[]{:S(2)}, u32[]{:S(2)}) %all-to-all-start) | async-done | bytes 884768 | tf_op jit(solution)/shard_map/all_to_all | solution.py:362
  29.3 0.1 fusion.3
  29.4 0.1 pad_maximum_fusion.2
  29.5 0.9 pad_maximum_fusion.3
  30.3 0.0 copy-start.11
  30.3 1.4 collective-permute-start.1
  31.8 4.6 %collective-permute-start = (bf16[4,4,144,128]{3,2,1,0:T(8,128)(2,1)S(1)}, bf16[4,4,144,128]{3,2,1,0:T(8,128)(2,1)S(1)}, u32[]{:S(2)}, u32[]{:S(2)}) collective-permute-start(bf16[4,4,144,128]{3,2,1,0:T(8,128)(2,1)S(1)} %pad_maximum_fusion.2), channel_id=1, source_target_pairs={{0,8},{8,16},{16,24},{1,9},{9,17},{17,25},{2,10},{10,18},{18,26},{... | collective-permute-start | bytes 1769480 | tf_op jit(solution)/shard_map/ppermute | solution.py:374
  36.3 1.1 pad_maximum_fusion.1
  37.4 3.5 %all-to-all-start.1 = ((bf16[8,304,128]{2,1,0:T(8,128)(2,1)}), bf16[8,304,128]{2,1,0:T(8,128)(2,1)S(1)}, u32[]{:S(2)}, u32[]{:S(2)}) async-start(bf16[8,304,128]{2,1,0:T(8,128)(2,1)} %pad_maximum_fusion.1), calls=%async_computation.1 | async-start | bytes 1245184 | tf_op jit(solution)/shard_map/all_to_all | solution.py:386
  40.9 0.0 all-reduce.5.cloned.1.call-start
  41.0 0.0 copy-done.11
  41.0 0.1 constant_dynamic-slice_fusion
  41.1 0.1 copy.14
  41.2 0.1 add_select_fusion
  41.3 0.6 pad.15.kc_ref
  42.0 8.8 %all-to-all-done.1 = bf16[8,304,128]{2,1,0:T(8,128)(2,1)S(1)} async-done(((bf16[8,304,128]{2,1,0:T(8,128)(2,1)}), bf16[8,304,128]{2,1,0:T(8,128)(2,1)S(1)}, u32[]{:S(2)}, u32[]{:S(2)}) %all-to-all-start.1) | async-done | bytes 622624 | tf_op jit(solution)/shard_map/all_to_all | solution.py:386
  50.8 0.0 collective-permute-done.1.d_ref
  50.8 0.0 collective-permute-done.u_ref
  50.8 0.1 broadcast_in_dim.34.ends_ref
  50.9 0.0 copy-start.2
  50.9 0.9 copy-done.2
  51.8 13.4 %shard_map.112 = (bf16[8,144,128]{2,1,0:T(8,128)(2,1)S(1)}, bf16[10,144,128]{2,1,0:T(8,128)(2,1)}, bf16[10,144,128]{2,1,0:T(8,128)(2,1)}, f32[2,144,512]{2,1,0:T(8,128)S(1)}, f32[4,144,512]{2,1,0:T(8,128)S(1)}) custom-call(bf16[8,3,144,128]{3,2,1,0:T(8,128)(2,1)S(1)} %bitcast.28, bf16[4,4,144,128]{3,2,1,0:T(8,128)(2,1)S(1)} %collective-permute-done.u_ref, ...), custom_call_target="tpu_custom_call" | custom-call | flops 4026531840 | bytes 5566464 | tf_op jit(solution)/shard_map/pallas_call | solution.py:29
  65.2 0.0 copy-start
  65.2 0.8 copy-done
  66.0 4.2 %collective-permute-start.2 = (bf16[10,144,128]{2,1,0:T(8,128)(2,1)}, bf16[10,144,128]{2,1,0:T(8,128)(2,1)}, u32[]{:S(2)}, u32[]{:S(2)}) collective-permute-start(bf16[10,144,128]{2,1,0:T(8,128)(2,1)} %get-tuple-element.20), channel_id=1, source_target_pairs={{0,8},{8,16},{16,24},{1,9},{9,17},{17,25},{2,10},{10,18},{18,26},{... | collective-permute-start | bytes 1105928 | tf_op jit(solution)/shard_map/ppermute | solution.py:423
  70.2 1.3 collective-permute-start.3
  71.5 2.8 %shard_map.113 = f32[144,128]{1,0:T(8,128)S(1)} custom-call(bf16[8,3,144,128]{3,2,1,0:T(8,128)(2,1)S(1)} %bitcast.29, bf16[4,4,144,128]{3,2,1,0:T(8,128)(2,1)S(1)} %collective-permute-done.u_ref, bf16[4,4,144,128]{3,2,1,0:T(8,128)(2,1)S(1)} %collective-permute-done.1.d_ref, f32[4,144,512]{2,1,0:T(8,128)S(1)} %get-tuple-element.19.dv_ref), custom_call_target="tpu_custom_call" | custom-call | bytes 3317760 | tf_op jit(solution)/shard_map/pallas_call | solution.py:29
  74.3 0.0 copy-start.4
  74.3 0.6 copy-done.4
  74.9 0.0 all-reduce.5.cloned.1.call-update
  75.0 34.0 %all-reduce.5.cloned.1.call-done.gk_ref = f32[144,128]{1,0:T(8,128)} async-done(((f32[144,128]{1,0:T(8,128)}), f32[144,128]{1,0:T(8,128)}) %all-reduce.5.cloned.1.call-update) | async-done | bytes 73744 | tf_op jit(solution)/shard_map/psum | solution.py:425
  109.0 0.0 collective-permute-done.2.u_ref
  109.0 0.0 collective-permute-done.3.d_ref
  109.0 0.0 copy-start.1
  109.0 1.1 copy-done.1
  110.0 0.0 copy-start.3
  110.0 0.9 copy-done.3
  110.9 0.0 copy-start.10
  110.9 0.9 copy-done.10
  111.8 4.1 %shard_map.114 = (bf16[8,4,144,128]{3,2,1,0:T(8,128)(2,1)S(1)}, bf16[8,2,2,16,128]{4,3,2,1,0:T(8,128)(2,1)S(1)}) custom-call(bf16[8,144,128]{2,1,0:T(8,128)(2,1)S(1)} %get-tuple-element.17.dq_ref, f32[2,144,512]{2,1,0:T(8,128)S(1)} %copy-done.1, f32[4,144,512]{2,1,0:T(8,128)S(1)} %get-tuple-element.19.dv_ref, ...), custom_call_target="tpu_custom_call" | custom-call | bytes 4259840 | tf_op jit(solution)/shard_map/pallas_call | solution.py:29
  115.9 0.1 pad_maximum_fusion
  116.0 20.9 %all_to_all.15 = bf16[8,640,128]{2,1,0:T(8,128)(2,1)S(1)} all-to-all(bf16[8,640,128]{2,1,0:T(8,128)(2,1)S(1)} %pad_maximum_fusion), channel_id=1, replica_groups=mesh['z'=4,'x'=2,'c'=4] {'x','c'}, dimensions={0} | all-to-all | bytes 2621440 | tf_op jit(solution)/shard_map/all_to_all | solution.py:432
  136.9 0.1 slice.46
  137.0 1.2 shard_map.115
  (7 shorter events, 0.1 us)
Async XLA Ops:
  7.2 1.0 copy-start.5
  8.1 1.0 copy-start.6
  9.1 1.0 copy-start.7
  11.3 5.3 %copy-start.8 = (bf16[2,64,1152]{2,1,0:T(8,128)(2,1)S(1)}, bf16[2,64,1152]{2,1,0:T(8,128)(2,1)}, u32[]{:S(2)}) copy-start(bf16[2,64,1152]{2,1,0:T(8,128)(2,1)} %param.7) | copy-start | bytes 884740
  11.3 5.3 %copy-start.9 = (bf16[2,64,1152]{2,1,0:T(8,128)(2,1)S(1)}, bf16[2,64,1152]{2,1,0:T(8,128)(2,1)}, u32[]{:S(2)}) copy-start(bf16[2,64,1152]{2,1,0:T(8,128)(2,1)} %param.12) | copy-start | bytes 884740
  11.3 18.0 %all-to-all-start = ((bf16[8,432,128]{2,1,0:T(8,128)(2,1)}), bf16[8,432,128]{2,1,0:T(8,128)(2,1)S(1)}, u32[]{:S(2)}, u32[]{:S(2)}) async-start(bf16[8,432,128]{2,1,0:T(8,128)(2,1)} %bitcast.3), calls=%async_computation | async-start | bytes 1769472 | tf_op jit(solution)/shard_map/all_to_all | solution.py:362
  30.3 10.7 %copy-start.11 = (f32[3,3,1152]{2,1,0:T(4,128)S(1)}, f32[3,3,1152]{2,1,0:T(4,128)}, u32[]{:S(2)}) copy-start(f32[3,3,1152]{2,1,0:T(4,128)} %param.11) | copy-start | bytes 124420
  30.3 20.5 %collective-permute-start.1 = (bf16[4,4,144,128]{3,2,1,0:T(8,128)(2,1)}, bf16[4,4,144,128]{3,2,1,0:T(8,128)(2,1)S(1)}, u32[]{:S(2)}, u32[]{:S(2)}) collective-permute-start(bf16[4,4,144,128]{3,2,1,0:T(8,128)(2,1)} %pad_maximum_fusion.3), channel_id=1, source_target_pairs={{8,0},{16,8},{24,16},{9,1},{17,9},{25,17},{10,2},{18,10},{26,18},{... | collective-permute-start | bytes 1769480 | tf_op jit(solution)/shard_map/ppermute | solution.py:375
  31.8 19.1 %collective-permute-start = (bf16[4,4,144,128]{3,2,1,0:T(8,128)(2,1)S(1)}, bf16[4,4,144,128]{3,2,1,0:T(8,128)(2,1)S(1)}, u32[]{:S(2)}, u32[]{:S(2)}) collective-permute-start(bf16[4,4,144,128]{3,2,1,0:T(8,128)(2,1)S(1)} %pad_maximum_fusion.2), channel_id=1, source_target_pairs={{0,8},{8,16},{16,24},{1,9},{9,17},{17,25},{2,10},{10,18},{18,26},{... | collective-permute-start | bytes 1769480 | tf_op jit(solution)/shard_map/ppermute | solution.py:374
  37.4 13.4 %all-to-all-start.1 = ((bf16[8,304,128]{2,1,0:T(8,128)(2,1)}), bf16[8,304,128]{2,1,0:T(8,128)(2,1)S(1)}, u32[]{:S(2)}, u32[]{:S(2)}) async-start(bf16[8,304,128]{2,1,0:T(8,128)(2,1)} %pad_maximum_fusion.1), calls=%async_computation.1 | async-start | bytes 1245184 | tf_op jit(solution)/shard_map/all_to_all | solution.py:386
  40.9 68.0 %all-reduce.5.cloned.1.call-start = ((), (), s32[]{:S(2)}) async-start(), calls=%async_computation.3 | async-start | bytes 147456 | tf_op jit(solution)/shard_map/psum | solution.py:425
  50.9 0.9 copy-start.2
  65.2 0.8 copy-start
  66.0 43.0 %collective-permute-start.2 = (bf16[10,144,128]{2,1,0:T(8,128)(2,1)}, bf16[10,144,128]{2,1,0:T(8,128)(2,1)}, u32[]{:S(2)}, u32[]{:S(2)}) collective-permute-start(bf16[10,144,128]{2,1,0:T(8,128)(2,1)} %get-tuple-element.20), channel_id=1, source_target_pairs={{0,8},{8,16},{16,24},{1,9},{9,17},{17,25},{2,10},{10,18},{18,26},{... | collective-permute-start | bytes 1105928 | tf_op jit(solution)/shard_map/ppermute | solution.py:423
  70.2 38.8 %collective-permute-start.3 = (bf16[10,144,128]{2,1,0:T(8,128)(2,1)}, bf16[10,144,128]{2,1,0:T(8,128)(2,1)}, u32[]{:S(2)}, u32[]{:S(2)}) collective-permute-start(bf16[10,144,128]{2,1,0:T(8,128)(2,1)} %get-tuple-element.21), channel_id=1, source_target_pairs={{8,0},{16,8},{24,16},{9,1},{17,9},{25,17},{10,2},{18,10},{26,18},{... | collective-permute-start | bytes 1105928 | tf_op jit(solution)/shard_map/ppermute | solution.py:422
  74.3 0.6 copy-start.4
  109.0 1.1 copy-start.1
  110.0 0.9 copy-start.3
  110.9 0.9 copy-start.10
Sparse Core Ops, SparseCore 0:
  75.1 33.8 all-reduce.4

commit v2 on v1

v2 whole, which is shorter than its diff:
```python
import functools
import math

import jax
import jax.numpy as jnp
from jax import lax
from jax.experimental import pallas as pl
from jax.experimental.pallas import tpu as pltpu
from jax.sharding import Mesh, PartitionSpec as P

HEADS = 16
HEAD_DIM = 72
ROWS = 2
LANES = 128
HALF = 64
NEG = -1e30
INV_ROOT = HEAD_DIM ** (-0.5)
LOG2E = 1.4426950408889634
BF = jnp.bfloat16
F32 = jnp.float32


def params(mib):
    return pltpu.CompilerParams(vmem_limit_bytes=mib << 20)


def call(body, outs, *args, scratch=(), flops=0, mib=8, keep=(), near=()):
    moved = sum(a.size * a.dtype.itemsize for a in args)
    moved += sum(math.prod(shape) * jnp.dtype(dtype).itemsize for shape, dtype in outs)
    outs = [
        pltpu.VMEM(shape, dtype) if n in keep else jax.ShapeDtypeStruct(shape, dtype)
        for n, (shape, dtype) in enumerate(outs)
    ]
    args = [
        pltpu.with_memory_space_constraint(a, pltpu.VMEM) if n in near else a
        for n, a in enumerate(args)
    ]
    return pl.pallas_call(
        body,
        out_shape=outs,
        scratch_shapes=list(scratch),
        compiler_params=params(mib),
        cost_estimate=pl.CostEstimate(flops=flops, bytes_accessed=moved, transcendentals=0),
    )(*args)


def pack_into(refs, ch, chp, put):
    for n, ref in enumerate(refs):
        x = ref[...]
        if ch % 16:
            x = x.astype(F32)
        x = x.T
        for p in range(x.shape[0] // ch):
            piece = x[p * ch : (p + 1) * ch]
            if chp > ch:
                piece = jnp.concatenate([piece, jnp.zeros((chp - ch, LANES), piece.dtype)], axis=0)
            put(p, n, piece.astype(BF))


def pack_body(ch, *refs):
    out = refs[-1]

    def put(p, n, piece):
        out[p, n] = piece

    pack_into(refs[:-1], ch, out.shape[2], put)


def pack_live_body(ch, chp, query_ref, grad_ref, live_ref, out):
    def put(p, n, piece):
        out[p, n * chp : (n + 1) * chp] = piece

    pack_into((query_ref, grad_ref), ch, chp, put)
    live = live_ref[...].astype(BF)
    for p in range(out.shape[0]):
        out[p, 2 * chp :] = live


def unpack_body(ch, x_ref, *outs):
    peers = x_ref.shape[0]
    for n, out in enumerate(outs):
        pieces = [x_ref[p, n] for p in range(peers)]
        if ch % 16:
            pieces = [piece.astype(F32)[:ch] for piece in pieces]
        out[...] = jnp.concatenate(pieces, axis=0).T.astype(BF)


def unpack_query_body(ch, chp, x_ref, out, gk_ref):
    peers = x_ref.shape[0]
    pieces = [x_ref[p, :chp] for p in range(peers)]
    if ch % 16:
        pieces = [piece.astype(F32)[:ch] for piece in pieces]
    out[...] = jnp.concatenate(pieces, axis=0).T.astype(BF)
    blocks = (x_ref.shape[1] - chp) // 32
    wide = gk_ref.shape[1]
    total = [jnp.zeros((16, LANES), F32) for _ in range(wide // LANES + 2)]
    lane = lax.broadcasted_iota(jnp.int32, (16, LANES), 1)
    for p in range(peers):
        first, off = divmod(p * ch, LANES)
        for b in range(blocks):
            at = chp + 32 * b
            piece = x_ref[p, at : at + 16].astype(F32) + x_ref[p, at + 16 : at + 32].astype(F32)
            turned = pltpu.roll(piece, off, 1) if off else piece
            total[first + b] = total[first + b] + jnp.where(lane >= off, turned, 0.0)
            if off:
                total[first + b + 1] = total[first + b + 1] + jnp.where(lane < off, turned, 0.0)
    gk_ref[...] = jnp.concatenate(total[: wide // LANES], axis=1)


def taps_out_body(x_ref, y_ref, out):
    total = x_ref[...] + y_ref[...]
    for a in range(3):
        out[a] = total[3 * a : 3 * a + 3]


def add_body(x_ref, y_ref, out):
    out[...] = x_ref[...] + y_ref[...]


def lane_masks(rows):
    lane = lax.broadcasted_iota(jnp.int32, (rows, LANES), 1)
    col = lane & (HALF - 1)
    return lane >= HALF, col == 0, col == HALF - 1


def col_shifts(tiles, masks):
    _, first, last = masks
    swapped = [pltpu.roll(t, HALF, 1) for t in tiles]
    none = jnp.zeros_like(tiles[0])
    out = []
    for j, t in enumerate(tiles):
        before = swapped[j - 1] if j else none
        after = swapped[j + 1] if j + 1 < len(tiles) else none
        out.append(
            (
                pltpu.roll(jnp.where(last, before, t), 1, 1),
                t,
                pltpu.roll(jnp.where(first, after, t), LANES - 1, 1),
            )
        )
    return out


def conv_rows(rows, coef, masks):
    second = masks[0]
    count = len(rows)
    shifted = [col_shifts(row, masks) for row in rows]
    terms = []
    for i, row in enumerate(shifted):
        use = [i < count - 1, 0 < i < count - 1, i > 0]
        terms.append(
            [
                [
                    sum(coef[3 * a + b] * t[b] for b in range(3)) if use[a] else None
                    for a in range(3)
                ]
                for t in row
            ]
        )
    out = []
    for i in range(1, count - 1):
        line = []
        for j in range(len(rows[0])):
            up = jnp.where(second, terms[i - 1][j][0], terms[i][j][0])
            down = jnp.where(second, terms[i][j][2], terms[i + 1][j][2])
            line.append(terms[i][j][1] + pltpu.roll(up + down, HALF, 1))
        out.append(line)
    return out


def taps(kc_ref, at):
    block = kc_ref[at, :]
    return [jnp.broadcast_to(block[:, t : t + 1], (16, LANES)) for t in range(9)]


def join_halves(left, right, want_second, second):
    if want_second:
        return jnp.where(second, right, pltpu.roll(left, HALF, 1))
    return jnp.where(second, pltpu.roll(right, HALF, 1), left)


def split_halves(both, odd, have_second):
    return both if odd == have_second else pltpu.roll(both, HALF, 1)


def rim_body(a_ref, up_ref, down_ref):
    cols = a_ref.shape[0] // ROWS
    chp = a_ref.shape[2]
    second = lax.broadcasted_iota(jnp.int32, (chp, LANES), 1) >= HALF
    for out, row, further, want_second in (
        (up_ref, 0, 1, False),
        (down_ref, ROWS - 1, ROWS - 2, True),
    ):
        for j in range(cols):
            for n in range(3):
                out[n * cols + j] = a_ref[row * cols + j, n]
        for m in range(cols // 2):
            left, right = (
                a_ref[further * cols + 2 * m + odd, 2].astype(F32) for odd in range(2)
            )
            out[3 * cols + m] = join_halves(left, right, want_second, second).astype(BF)


def control_rows(a_ref, u_ref, d_ref, at):
    cols = a_ref.shape[0] // ROWS

    def outer(ref, have_second):
        return [
            split_halves(ref[3 * cols + j // 2, at, :].astype(F32), j % 2 == 1, have_second)
            for j in range(cols)
        ]

    def halo(ref):
        return [ref[2 * cols + j, at, :].astype(F32) for j in range(cols)]

    own = [[a_ref[r * cols + j, 2, at, :].astype(F32) for j in range(cols)] for r in range(ROWS)]
    return [outer(u_ref, True), halo(u_ref)] + own + [halo(d_ref), outer(d_ref, False)]


def values_body(a_ref, u_ref, d_ref, kc_ref, vt):
    cols = a_ref.shape[0] // ROWS
    chp = a_ref.shape[2]

    @pl.loop(0, chp // 16)
    def _(step):
        at = pl.ds(pl.multiple_of(step * 16, 16), 16)
        masks = lane_masks(16)
        coef = taps(kc_ref, at)
        rows = control_rows(a_ref, u_ref, d_ref, at)
        conv = conv_rows(rows, coef, masks)
        for j in range(cols):
            span = slice(j * LANES, (j + 1) * LANES)
            for i in range(ROWS + 2):
                if i == 0:
                    v = u_ref[cols + j, at, :]
                elif i <= ROWS:
                    v = a_ref[(i - 1) * cols + j, 1, at, :]
                else:
                    v = d_ref[cols + j, at, :]
                vt[i, at, span] = (v.astype(F32) + conv[i][j]).astype(BF)


def attend_body(heads, q_ref, a_ref, u_ref, d_ref, vt, dq_ref, up_ref, down_ref, dk_ref, acc_v, acc_k):
    peers = q_ref.shape[0]
    cols = peers // ROWS
    chp = vt.shape[1]
    wide = cols * LANES
    acc_k[...] = jnp.zeros_like(acc_k)
    acc_v[...] = jnp.zeros_like(acc_v)
    chan = lax.broadcasted_iota(jnp.int32, (chp, LANES), 0)
    mine = [(chan >= h * HEAD_DIM) & (chan < (h + 1) * HEAD_DIM) for h in range(heads)]

    def spread(x):
        x = x.astype(F32)
        return jnp.concatenate([jnp.where(m, x, 0.0) for m in mine], axis=1).astype(BF)

    def dot(x, y, on_x, on_y):
        return lax.dot_general(
            x, y, (((on_x,), (on_y,)), ((), ())), preferred_element_type=F32
        )

    for r in range(ROWS):

        @pl.loop(0, cols)
        def _(j, r=r):
            tile = r * cols + j
            span = pl.ds(pl.multiple_of(j * LANES, LANES), LANES)
            q = spread(q_ref[tile, :chp])
            g = spread(q_ref[tile, chp : 2 * chp])
            k = jnp.concatenate(
                [a_ref[r * cols + p, 0] for p in range(cols)]
                + [
                    u_ref[j] if r == 0 else a_ref[tile - cols, 0],
                    d_ref[j] if r == ROWS - 1 else a_ref[tile + cols, 0],
                ],
                axis=1,
            )
            v = jnp.concatenate([vt[r + 1], vt[r, :, span], vt[r + 2, :, span]], axis=1)
            live = q_ref[tile, 2 * chp :].astype(F32)
            zero = jnp.zeros((1, LANES), F32)
            bias = jnp.concatenate(
                [live[p : p + 1] for p in range(cols)]
                + [
                    live[cols : cols + 1] if r == 0 else zero,
                    live[cols + 1 : cols + 2] if r == ROWS - 1 else zero,
                ],
                axis=1,
            )
            s = dot(q, k, 0, 0) + bias
            top = jnp.max(s, axis=1, keepdims=True)
            e = jnp.exp2((s - top) * (INV_ROOT * LOG2E))
            w = e * (1.0 / jnp.sum(e, axis=1, keepdims=True))
            gw = dot(g, v, 0, 0)
            delta = jnp.sum(w * gw, axis=1, keepdims=True)
            gs = (w * (gw - delta)).astype(BF)
            dk = dot(q, gs, 1, 0)
            dv = dot(g, w.astype(BF), 1, 0)
            dq = dot(k, gs, 1, 1)
            own = dq[:, :LANES]
            for h in range(1, heads):
                own = jnp.where(mine[h], dq[:, h * LANES : (h + 1) * LANES], own)
            dq_ref[tile] = (own * INV_ROOT).astype(BF)
            for acc, part in ((acc_k, dk), (acc_v, dv)):
                acc[r + 1] += part[:, :wide]
                acc[r, :, span] += part[:, wide : wide + LANES]
                acc[r + 2, :, span] += part[:, wide + LANES :]

    second = lax.broadcasted_iota(jnp.int32, (chp, LANES), 1) >= HALF
    for r in range(ROWS):
        dk_ref[r] = acc_k[r + 1] * INV_ROOT
    for out, i, rim in ((up_ref, 0, 1), (down_ref, ROWS + 1, ROWS)):
        for j in range(cols):
            span = slice(j * LANES, (j + 1) * LANES)
            out[j] = (acc_k[i, :, span] * INV_ROOT).astype(BF)
            out[cols + j] = acc_v[i, :, span].astype(BF)
        for m in range(cols // 2):
            left = acc_v[rim, :, 2 * m * LANES : (2 * m + 1) * LANES]
            right = acc_v[rim, :, (2 * m + 1) * LANES : (2 * m + 2) * LANES]
            both = join_halves(left, right, i != 0, second)
            out[2 * cols + m] = both.astype(BF)


def kernel_grad_body(ch, dq_ref, a_ref, u_ref, d_ref, dv_ref, out_ref, sums):
    cols = a_ref.shape[0] // ROWS
    chp = a_ref.shape[2]

    @pl.loop(0, chp // 16)
    def _(step):
        at = pl.ds(pl.multiple_of(step * 16, 16), 16)
        masks = lane_masks(16)
        second = masks[0]
        rows = control_rows(a_ref, u_ref, d_ref, at)
        shifted = [col_shifts(row, masks) for row in rows]
        acc = [jnp.zeros((16, LANES), F32) for _ in range(9)]
        for i in range(ROWS + 2):
            for j in range(cols):
                g = dv_ref[i, at, j * LANES : (j + 1) * LANES]
                turned = pltpu.roll(g, HALF, 1)
                above, here, below = (shifted[i + n][j] for n in range(3))
                for b in range(3):
                    acc[b] += jnp.where(second, above[b], here[b]) * turned
                    acc[3 + b] += here[b] * g
                    acc[6 + b] += jnp.where(second, here[b], below[b]) * turned
        lane = lax.broadcasted_iota(jnp.int32, (16, LANES), 1)
        out = jnp.zeros((16, LANES), F32)
        for t in range(9):
            out = jnp.where(lane == t, jnp.sum(acc[t], axis=1, keepdims=True), out)
        sums[at, :] = out

    turned = sums[...].T[:16]
    blocks = (out_ref.shape[1] - chp) // 32
    if blocks * LANES > chp:
        turned = jnp.concatenate([turned, jnp.zeros((16, blocks * LANES - chp), F32)], axis=1)
    lane = lax.broadcasted_iota(jnp.int32, turned.shape, 1)
    turned = jnp.where(lane < ch, turned, 0.0)
    high = turned.astype(BF)
    low = (turned - high.astype(F32)).astype(BF)
    for tile in range(out_ref.shape[0]):
        out_ref[tile, :chp] = dq_ref[tile]
        for b in range(blocks):
            at = chp + 32 * b
            out_ref[tile, at : at + 16] = high[:, b * LANES : (b + 1) * LANES]
            out_ref[tile, at + 16 : at + 32] = low[:, b * LANES : (b + 1) * LANES]


def finish_body(dk_ref, dv_ref, u_ref, d_ref, kc_ref, out_ref):
    cols = out_ref.shape[0] // ROWS
    chp = out_ref.shape[2]

    @pl.loop(0, chp // 16)
    def _(step):
        at = pl.ds(pl.multiple_of(step * 16, 16), 16)
        masks = lane_masks(16)
        second = masks[0]
        coef = taps(kc_ref, at)[::-1]

        def from_side(ref, n):
            return ref[n, at, :].astype(F32)

        def rounded(x):
            return x.astype(BF).astype(F32)

        rows = []
        for i in range(ROWS + 2):
            row = []
            for j in range(cols):
                x = dv_ref[i, at, j * LANES : (j + 1) * LANES]
                if i == 0:
                    rim = from_side(u_ref, 2 * cols + j // 2)
                    x = x + split_halves(rim, j % 2 == 1, True)
                elif i == ROWS + 1:
                    rim = from_side(d_ref, 2 * cols + j // 2)
                    x = x + split_halves(rim, j % 2 == 1, False)
                else:
                    if i == 1:
                        x = x + from_side(u_ref, cols + j)
                    if i == ROWS:
                        x = x + from_side(d_ref, cols + j)
                row.append(rounded(x))
            rows.append(row)
        conv = conv_rows(rows, coef, masks)
        for r in range(ROWS):
            for j in range(cols):
                tile = r * cols + j
                k = dk_ref[r, at, j * LANES : (j + 1) * LANES]
                if r == 0:
                    k = k + from_side(u_ref, j)
                if r == ROWS - 1:
                    k = k + from_side(d_ref, j)
                out_ref[tile, 0, at, :] = k.astype(BF)
                out_ref[tile, 1, at, :] = rows[r + 1][j].astype(BF)
                out_ref[tile, 2, at, :] = conv[r][j].astype(BF)


def per_device(query, key, value, control, kernel, grad_out, detail_blocks):
    shape = query.shape
    channels = shape[2]
    planes = lax.axis_size("z")
    cols = lax.axis_size("c")
    peers = ROWS * cols
    heads = HEADS // peers
    ch = heads * HEAD_DIM
    chp = -(-ch // 16) * 16
    plane = ("x", "c")
    my_z = lax.axis_index("z")
    my_col = lax.axis_index("c")
    me = lax.axis_index("x") * cols + my_col

    def flat(x):
        return x.reshape(LANES, channels)

    def swap(x):
        out = lax.all_to_all(x.reshape(peers, -1, LANES), plane, 0, 0, tiled=True)
        return out.reshape(x.shape)

    (sent,) = call(
        functools.partial(pack_body, ch),
        [((peers, 3, chp, LANES), BF)],
        flat(key), flat(value), flat(control),
        mib=56,
    )
    mine = swap(sent)
    wanted = lax.dynamic_index_in_dim(detail_blocks[0], my_col, 0, keepdims=False)
    named = (wanted >= 0) | (jnp.arange(cols) == my_col)
    named = jnp.concatenate([named, jnp.stack([my_z >= 1, my_z + 1 < planes])])
    live = jnp.where(jnp.pad(named, (0, 14 - cols)), 0.0, NEG).astype(F32)
    live = jnp.broadcast_to(live[:, None], (16, LANES))
    (sent_q,) = call(
        functools.partial(pack_live_body, ch, chp),
        [((peers, 2 * chp + 16, LANES), BF)],
        flat(query), flat(grad_out), live,
        mib=56,
    )
    down_pairs = [(i, i + 1) for i in range(planes - 1)]
    up_pairs = [(i + 1, i) for i in range(planes - 1)]
    mine, sent_q = lax.optimization_barrier((mine, sent_q))
    rim = (3 * cols + cols // 2, chp, LANES)
    to_up, to_down = call(rim_body, [(rim, BF)] * 2, mine)
    below = lax.ppermute(to_up, "z", up_pairs)
    above = lax.ppermute(to_down, "z", down_pairs)

    coefs = lax.dynamic_slice_in_dim(kernel.reshape(9, channels), me * ch, ch, 1)
    coefs = jnp.pad(coefs.T, ((0, chp - ch), (0, LANES - 9)))
    queries = swap(sent_q)

    wide = cols * LANES
    (values,) = call(
        values_body, [((ROWS + 2, chp, wide), BF)], mine, above, below, coefs, flops=4 * 10**9, keep=(0,)
    )
    side = (2 * cols + cols // 2, chp, LANES)
    flops = 10 * peers * heads * LANES * (wide + 2 * LANES) * 256
    dq, to_up, to_down, dk, dv = call(
        functools.partial(attend_body, heads),
        [
            ((peers, chp, LANES), BF),
            (side, BF),
            (side, BF),
            ((ROWS, chp, wide), F32),
            ((ROWS + 2, chp, wide), F32),
        ],
        queries, mine, above, below, values,
        scratch=[pltpu.VMEM((ROWS + 2, chp, wide), F32)],
        flops=flops,
        mib=6,
        near=(0, 1, 2, 3, 4),
        keep=(0, 1, 2, 3, 4),
    )
    from_below = lax.ppermute(to_up, "z", up_pairs)
    from_above = lax.ppermute(to_down, "z", down_pairs)

    blocks = -(-ch // LANES)
    (sent_dq,) = call(
        functools.partial(kernel_grad_body, ch),
        [((peers, chp + 32 * blocks, LANES), BF)],
        dq, mine, above, below, dv,
        scratch=[pltpu.VMEM((chp, LANES), F32)],
        flops=4 * 10**9,
    )
    dq_back = swap(sent_dq)

    (results,) = call(
        finish_body, [((peers, 3, chp, LANES), BF)], dk, dv, from_above, from_below, coefs,
        flops=4 * 10**9, near=(0, 1, 2, 3),
    )
    back = swap(results)
    grad_query, taps_sum = call(
        functools.partial(unpack_query_body, ch, chp),
        [((LANES, channels), BF), ((16, channels), F32)],
        dq_back,
    )
    step = 1
    while 2 * step < planes:
        other = lax.ppermute(taps_sum, "z", [(i, i ^ step) for i in range(planes)])
        (taps_sum,) = call(add_body, [((16, channels), F32)], taps_sum, other)
        step *= 2
    other = lax.ppermute(taps_sum, "z", [(i, i ^ step) for i in range(planes)])
    (grad_kernel,) = call(taps_out_body, [((3, 3, channels), F32)], taps_sum, other)
    outs = call(functools.partial(unpack_body, ch), [((LANES, channels), BF)] * 3, back)
    return tuple(x.reshape(shape) for x in [grad_query] + list(outs)) + (grad_kernel,)


def solution(mesh):
    trow, tcol = mesh.shape["trow"], mesh.shape["tcol"]
    grid = Mesh(mesh.devices.reshape(trow // ROWS, ROWS, tcol), ("z", "x", "c"))
    tiled = P(("z", "x"), "c", None)
    return jax.shard_map(
        per_device,
        mesh=grid,
        in_specs=(tiled, tiled, tiled, tiled, P(), tiled, P(("z", "x"), None, None)),
        out_specs=(tiled, tiled, tiled, tiled, P()),
        check_vma=False,
    )
```

time: 146 us -> 96 us (0.66)
  waiting for transfers between devices: 54.5 us -> 26.9 us
  blocking collectives: 20.9 us -> 0 us
  between operations: 14.2 us -> 0.76 us
  starting transfers between devices: 20.4 us -> 30.3 us
  Pallas kernels: 22.9 us -> 29.7 us
  local copies, waits for them, and re-layouts: 9.21 us -> 6.96 us
  other arithmetic: 2.92 us -> 0.78 us
    psum x1 -> x0, waiting for transfers between devices: 34 us -> none  [per_device(): gk = lax.psum(gk, 'z')]
    all_to_all x1 -> x0, blocking collectives: 20.9 us -> none  [per_device(): lax.all_to_all(jnp.concatenate([results.reshape(peers, 4 * chp, LANES), g...]
    ppermute x2 -> x4, waiting for transfers between devices: 0.01 us -> 16.7 us  [the longest x2 6.9 us: per_device(): other = lax.ppermute(taps_sum, 'z', [(i, i ^ step) for i in range(planes)])]
    all_to_all x2 -> x4, waiting for transfers between devices: 20.5 us -> 9.15 us  [swap(): out = lax.all_to_all(x.reshape(peers, -1, LANES), plane, 0, 0, tiled=True)]
    all_to_all x2 -> x4, starting transfers between devices: 8.84 us -> 15.7 us  [swap(): out = lax.all_to_all(x.reshape(peers, -1, LANES), plane, 0, 0, tiled=True)]
    pallas_call x6 -> x11, Pallas kernels: 22.9 us -> 29.7 us  [call(): pl.pallas_call(body, out_shape=outs, scratch_shapes=list(scratch), compil...]
    ppermute x2 -> x4, starting transfers between devices: 5.99 us -> 9.8 us  [the longest x2 5 us: per_device(): other = lax.ppermute(taps_sum, 'z', [(i, i ^ step) for i in range(planes)])]
    concatenate x5 -> x1, other arithmetic: 2.15 us -> 0.08 us  [per_device(): named = jnp.concatenate([named, jnp.stack([my_z >= 1, my_z + 1 < planes])])]
  transfers between devices with their start and end apart: 7 -> 10, of which waited for: 3 -> 6; matrix products, arithmetic and copies ran while one was open for 2% -> 2% of each run, Pallas kernels for 2% -> 16%
where the time goes in v2:
time: 96 us; the launch traced here: 95.3 us
  starting transfers between devices  30.3 us (32%)
  Pallas kernels  29.7 us (31%)
  waiting for transfers between devices  26.9 us (28%)
  local copies, waits for them, and re-layouts  6.96 us (7%)
    pallas_call x11, Pallas kernels, call(): pl.pallas_call(body, out_shape=outs, scratch_shapes=list(scratch), compil...  29.7 us
    all_to_all x4, starting transfers between devices, swap(): out = lax.all_to_all(x.reshape(peers, -1, LANES), plane, 0, 0, tiled=True)  15.7 us
    all_to_all x4, waiting for transfers between devices, swap(): out = lax.all_to_all(x.reshape(peers, -1, LANES), plane, 0, 0, tiled=True)  9.15 us
    ppermute x2, waiting for transfers between devices, per_device(): other = lax.ppermute(taps_sum, 'z', [(i, i ^ step) for i in range(planes)])  6.9 us
    unnamed x15, local copies, waits for them, and re-layouts  6.17 us
    ppermute x1, waiting for transfers between devices, per_device(): above = lax.ppermute(to_down, 'z', down_pairs)  5.96 us
    ppermute x2, starting transfers between devices, per_device(): other = lax.ppermute(taps_sum, 'z', [(i, i ^ step) for i in range(planes)])  5 us
    ppermute x1, waiting for transfers between devices, per_device(): below = lax.ppermute(to_up, 'z', up_pairs)  3.83 us
  transfers between devices with their start and end apart: 10, of which 6 were waited for; matrix products, arithmetic and copies ran while one was open for 2% of the time, Pallas kernels for 16%

profile of v2, /device:TPU:0, one launch (start us, length us, event | category | flops | bytes accessed | tf_op | source)
XLA Modules:
  0.0 95.3 jit_solution(15346057751373577148)
XLA Ops:
  0.6 2.4 %shard_map.110 = bf16[8,3,144,128]{3,2,1,0:T(8,128)(2,1)} custom-call(bf16[128,1152]{1,0:T(8,128)(2,1)} %bitcast.24, bf16[128,1152]{1,0:T(8,128)(2,1)} %bitcast.25, bf16[128,1152]{1,0:T(8,128)(2,1)} %bitcast.26), custom_call_target="tpu_custom_call" | custom-call | bytes 1769472 | tf_op jit(solution)/shard_map/pallas_call | solution.py:38
  3.0 5.2 %all-to-all-start = ((bf16[8,432,128]{2,1,0:T(8,128)(2,1)}), bf16[8,432,128]{2,1,0:T(8,128)(2,1)S(1)}, u32[]{:S(2)}, u32[]{:S(2)}) async-start(bf16[8,432,128]{2,1,0:T(8,128)(2,1)} %bitcast.23), calls=%async_computation | async-start | bytes 1769472 | tf_op jit(solution)/shard_map/all_to_all | solution.py:433
  8.2 0.7 bitcast_or_fusion
  8.9 0.1 pad_add_fusion
  8.9 0.7 broadcast_in_dim.16.live_ref
  9.6 2.1 %shard_map.111 = bf16[8,304,128]{2,1,0:T(8,128)(2,1)} custom-call(bf16[128,1152]{1,0:T(8,128)(2,1)} %bitcast.28, bf16[128,1152]{1,0:T(8,128)(2,1)} %bitcast.29, f32[16,128]{1,0:T(8,128)} %broadcast_in_dim.16.live_ref), custom_call_target="tpu_custom_call" | custom-call | bytes 1220608 | tf_op jit(solution)/shard_map/pallas_call | solution.py:38
  11.7 0.0 copy-start.6
  11.7 9.1 %all-to-all-done = bf16[8,432,128]{2,1,0:T(8,128)(2,1)S(1)} async-done(((bf16[8,432,128]{2,1,0:T(8,128)(2,1)}), bf16[8,432,128]{2,1,0:T(8,128)(2,1)S(1)}, u32[]{:S(2)}, u32[]{:S(2)}) %all-to-all-start) | async-done | bytes 884768 | tf_op jit(solution)/shard_map/all_to_all | solution.py:433
  20.9 0.9 shard_map.112
  21.8 3.5 %collective-permute-start = (bf16[14,144,128]{2,1,0:T(8,128)(2,1)}, bf16[14,144,128]{2,1,0:T(8,128)(2,1)S(1)}, u32[]{:S(2)}, u32[]{:S(2)}) collective-permute-start(bf16[14,144,128]{2,1,0:T(8,128)(2,1)} %get-tuple-element.21), channel_id=1, source_target_pairs={{0,8},{8,16},{16,24},{1,9},{9,17},{17,25},{2,10},{10,18},{18,26},{... | collective-permute-start | bytes 1548296 | tf_op jit(solution)/shard_map/ppermute | solution.py:460
  25.3 1.3 %collective-permute-start.1 = (bf16[14,144,128]{2,1,0:T(8,128)(2,1)S(1)}, bf16[14,144,128]{2,1,0:T(8,128)(2,1)S(1)}, u32[]{:S(2)}, u32[]{:S(2)}) collective-permute-start(bf16[14,144,128]{2,1,0:T(8,128)(2,1)S(1)} %get-tuple-element.22), channel_id=1, source_target_pairs={{8,0},{16,8},{24,16},{9,1},{17,9},{25,17},{10,2},{18,10},{26,18},{... | collective-permute-start | bytes 1548296 | tf_op jit(solution)/shard_map/ppermute | solution.py:459
  26.6 3.6 %all-to-all-start.1 = ((bf16[8,304,128]{2,1,0:T(8,128)(2,1)}), bf16[8,304,128]{2,1,0:T(8,128)(2,1)S(1)}, u32[]{:S(2)}, u32[]{:S(2)}) async-start(bf16[8,304,128]{2,1,0:T(8,128)(2,1)} %shard_map.111), calls=%async_computation.1 | async-start | bytes 1245184 | tf_op jit(solution)/shard_map/all_to_all | solution.py:433
  30.2 0.0 copy-done.6
  30.2 0.1 constant_dynamic-slice_fusion
  30.3 0.1 copy.14
  30.4 6.0 %collective-permute-done.u_ref = bf16[14,144,128]{2,1,0:T(8,128)(2,1)S(1)} collective-permute-done((bf16[14,144,128]{2,1,0:T(8,128)(2,1)}, bf16[14,144,128]{2,1,0:T(8,128)(2,1)S(1)}, u32[]{:S(2)}, u32[]{:S(2)}) %collective-permute-start) | collective-permute-done | bytes 516128 | tf_op jit(solution)/shard_map/ppermute | solution.py:460
  36.4 3.8 %collective-permute-done.1.d_ref = bf16[14,144,128]{2,1,0:T(8,128)(2,1)S(1)} collective-permute-done((bf16[14,144,128]{2,1,0:T(8,128)(2,1)S(1)}, bf16[14,144,128]{2,1,0:T(8,128)(2,1)S(1)}, u32[]{:S(2)}, u32[]{:S(2)}) %collective-permute-start.1) | collective-permute-done | bytes 516128 | tf_op jit(solution)/shard_map/ppermute | solution.py:459
  40.2 2.9 %shard_map.113.vt = bf16[4,144,512]{2,1,0:T(8,128)(2,1)S(1)} custom-call(bf16[8,3,144,128]{3,2,1,0:T(8,128)(2,1)S(1)} %bitcast.19, bf16[14,144,128]{2,1,0:T(8,128)(2,1)S(1)} %collective-permute-done.u_ref, bf16[14,144,128]{2,1,0:T(8,128)(2,1)S(1)} %collective-permute-done.1.d_ref, f32[144,128]{1,0:T(8,128)S(1)} %pad.9.kc_ref), custom_call_target="tpu_custom_call" | custom-call | flops 4000000000 | bytes 2580480 | tf_op jit(solution)/shard_map/pallas_call | solution.py:38
  43.2 0.0 copy-start.4
  43.2 0.8 copy-done.4
  44.0 0.0 all-to-all-done.1.q_ref
  44.0 0.0 copy-start.5
  44.0 1.1 %copy-done.5 = bf16[4,144,512]{2,1,0:T(8,128)(2,1)S(1)} copy-done((bf16[4,144,512]{2,1,0:T(8,128)(2,1)S(1)}, bf16[4,144,512]{2,1,0:T(8,128)(2,1)}, u32[]{:S(2)}) %copy-start.5) | copy-done | bytes 589848
  45.0 10.2 %shard_map.114 = (bf16[8,144,128]{2,1,0:T(8,128)(2,1)S(1)}, bf16[10,144,128]{2,1,0:T(8,128)(2,1)S(1)}, bf16[10,144,128]{2,1,0:T(8,128)(2,1)}, f32[2,144,512]{2,1,0:T(8,128)S(1)}, f32[4,144,512]{2,1,0:T(8,128)S(1)}) custom-call(bf16[8,304,128]{2,1,0:T(8,128)(2,1)S(1)} %all-to-all-done.1.q_ref, bf16[8,3,144,128]{3,2,1,0:T(8,128)(2,1)S(1)} %bitcast.20, ...), custom_call_target="tpu_custom_call" | custom-call | flops 4026531840 | bytes 5931008 | tf_op jit(solution)/shard_map/pallas_call | solution.py:38
  55.2 0.0 copy-start.2
  55.2 0.8 copy-done.2
  56.1 3.5 %collective-permute-start.2 = (bf16[10,144,128]{2,1,0:T(8,128)(2,1)}, bf16[10,144,128]{2,1,0:T(8,128)(2,1)S(1)}, u32[]{:S(2)}, u32[]{:S(2)}) collective-permute-start(bf16[10,144,128]{2,1,0:T(8,128)(2,1)} %get-tuple-element.27), channel_id=1, source_target_pairs={{0,8},{8,16},{16,24},{1,9},{9,17},{17,25},{2,10},{10,18},{18,26},{... | collective-permute-start | bytes 1105928 | tf_op jit(solution)/shard_map/ppermute | solution.py:489
  59.5 1.3 %collective-permute-start.3 = (bf16[10,144,128]{2,1,0:T(8,128)(2,1)S(1)}, bf16[10,144,128]{2,1,0:T(8,128)(2,1)}, u32[]{:S(2)}, u32[]{:S(2)}) collective-permute-start(bf16[10,144,128]{2,1,0:T(8,128)(2,1)S(1)} %get-tuple-element.28), channel_id=1, source_target_pairs={{8,0},{16,8},{24,16},{9,1},{17,9},{25,17},{10,2},{18,10},{26,18},{... | collective-permute-start | bytes 1105928 | tf_op jit(solution)/shard_map/ppermute | solution.py:488
  60.8 3.8 %shard_map.115 = bf16[8,208,128]{2,1,0:T(8,128)(2,1)} custom-call(bf16[8,144,128]{2,1,0:T(8,128)(2,1)S(1)} %get-tuple-element.23.dq_ref, bf16[8,3,144,128]{3,2,1,0:T(8,128)(2,1)S(1)} %bitcast.21, bf16[14,144,128]{2,1,0:T(8,128)(2,1)S(1)} %collective-permute-done.u_ref, bf16[14,144,128]{2,1,0:T(8,128)(2,1)S(1)} %collective-permute-done.1.d_ref, ...), custom_call_target="tpu_custom_call" | custom-call | flops 4000000000 | bytes 3817472 | tf_op jit(solution)/shard_map/pallas_call | solution.py:38
  64.6 0.0 copy-start
  64.6 1.0 %copy-done = f32[4,144,512]{2,1,0:T(8,128)} copy-done((f32[4,144,512]{2,1,0:T(8,128)}, f32[4,144,512]{2,1,0:T(8,128)S(1)}, u32[]{:S(2)}) %copy-start) | copy-done | bytes 1179672
  65.7 3.5 %all-to-all-start.2 = ((bf16[8,208,128]{2,1,0:T(8,128)(2,1)}), bf16[8,208,128]{2,1,0:T(8,128)(2,1)S(1)}, u32[]{:S(2)}, u32[]{:S(2)}) async-start(bf16[8,208,128]{2,1,0:T(8,128)(2,1)} %shard_map.115), calls=%async_computation.2 | async-start | bytes 851968 | tf_op jit(solution)/shard_map/all_to_all | solution.py:433
  69.1 0.0 collective-permute-done.2.u_ref
  69.1 1.0 %collective-permute-done.3.d_ref = bf16[10,144,128]{2,1,0:T(8,128)(2,1)} collective-permute-done((bf16[10,144,128]{2,1,0:T(8,128)(2,1)S(1)}, bf16[10,144,128]{2,1,0:T(8,128)(2,1)}, u32[]{:S(2)}, u32[]{:S(2)}) %collective-permute-start.3) | collective-permute-done | bytes 368672 | tf_op jit(solution)/shard_map/ppermute | solution.py:488
  70.2 0.0 copy-start.1
  70.2 1.3 %copy-done.1 = f32[4,144,512]{2,1,0:T(8,128)S(1)} copy-done((f32[4,144,512]{2,1,0:T(8,128)S(1)}, f32[4,144,512]{2,1,0:T(8,128)}, u32[]{:S(2)}) %copy-start.1) | copy-done | bytes 1179672
  71.4 0.0 copy-start.3
  71.4 1.1 %copy-done.3 = f32[2,144,512]{2,1,0:T(8,128)S(1)} copy-done((f32[2,144,512]{2,1,0:T(8,128)S(1)}, f32[2,144,512]{2,1,0:T(8,128)}, u32[]{:S(2)}) %copy-start.3) | copy-done | bytes 589848
  72.5 4.8 %shard_map.117 = bf16[8,3,144,128]{3,2,1,0:T(8,128)(2,1)} custom-call(f32[2,144,512]{2,1,0:T(8,128)S(1)} %copy-done.3, f32[4,144,512]{2,1,0:T(8,128)S(1)} %copy-done.1, bf16[10,144,128]{2,1,0:T(8,128)(2,1)S(1)} %collective-permute-done.2.u_ref, bf16[10,144,128]{2,1,0:T(8,128)(2,1)} %collective-permute-done.3.d_ref, f32[144,128]{1,0:T(8,128)S(1)} %pad.9.kc_ref), custom_call_target="tpu_custom_call" | custom-call | flops 4000000000 | bytes 3465216 | tf_op jit(solution)/shard_map/pallas_call | solution.py:38
  77.3 0.0 all-to-all-done.2.x_ref
  77.3 3.6 %all-to-all-start.3 = ((bf16[8,432,128]{2,1,0:T(8,128)(2,1)}), bf16[8,432,128]{2,1,0:T(8,128)(2,1)S(1)}, u32[]{:S(2)}, u32[]{:S(2)}) async-start(bf16[8,432,128]{2,1,0:T(8,128)(2,1)} %bitcast.12), calls=%async_computation.3 | async-start | bytes 1769472 | tf_op jit(solution)/shard_map/all_to_all | solution.py:433
  80.9 0.9 shard_map.116
  81.7 2.2 %collective-permute-start.4 = (f32[16,1152]{1,0:T(8,128)S(1)}, f32[16,1152]{1,0:T(8,128)S(1)}, u32[]{:S(2)}, u32[]{:S(2)}) collective-permute-start(f32[16,1152]{1,0:T(8,128)S(1)} %get-tuple-element.32.x_ref), channel_id=1, source_target_pairs={{0,8},{8,0},{16,24},{24,16},{1,9},{9,1},{17,25},{25,17},{2,10},{10... | collective-permute-start | bytes 221192 | tf_op jit(solution)/shard_map/ppermute | solution.py:513
  83.9 2.9 %collective-permute-done.4.y_ref = f32[16,1152]{1,0:T(8,128)S(1)} collective-permute-done((f32[16,1152]{1,0:T(8,128)S(1)}, f32[16,1152]{1,0:T(8,128)S(1)}, u32[]{:S(2)}, u32[]{:S(2)}) %collective-permute-start.4) | collective-permute-done | bytes 73760 | tf_op jit(solution)/shard_map/ppermute | solution.py:513
  86.8 2.8 %collective-permute-start.5 = (f32[16,1152]{1,0:T(8,128)S(1)}, f32[16,1152]{1,0:T(8,128)S(1)}, u32[]{:S(2)}, u32[]{:S(2)}) collective-permute-start(f32[16,1152]{1,0:T(8,128)S(1)} %shard_map.119.x_ref), channel_id=1, source_target_pairs={{0,16},{8,24},{16,0},{24,8},{1,17},{9,25},{17,1},{25,9},{2,18},{10... | collective-permute-start | bytes 221192 | tf_op jit(solution)/shard_map/ppermute | solution.py:516
  89.6 4.0 %collective-permute-done.5.y_ref = f32[16,1152]{1,0:T(8,128)S(1)} collective-permute-done((f32[16,1152]{1,0:T(8,128)S(1)}, f32[16,1152]{1,0:T(8,128)S(1)}, u32[]{:S(2)}, u32[]{:S(2)}) %collective-permute-start.5) | collective-permute-done | bytes 73760 | tf_op jit(solution)/shard_map/ppermute | solution.py:516
  93.6 0.6 shard_map.120
  94.3 0.0 all-to-all-done.3
  94.3 1.0 %shard_map.118 = (bf16[128,1152]{1,0:T(8,128)(2,1)}, bf16[128,1152]{1,0:T(8,128)(2,1)}, bf16[128,1152]{1,0:T(8,128)(2,1)}) custom-call(bf16[8,3,144,128]{3,2,1,0:T(8,128)(2,1)S(1)} %bitcast.22), custom_call_target="tpu_custom_call" | custom-call | bytes 1769472 | tf_op jit(solution)/shard_map/pallas_call | solution.py:38
  (4 shorter events, 0.0 us)
Async XLA Ops:
  3.0 17.9 %all-to-all-start = ((bf16[8,432,128]{2,1,0:T(8,128)(2,1)}), bf16[8,432,128]{2,1,0:T(8,128)(2,1)S(1)}, u32[]{:S(2)}, u32[]{:S(2)}) async-start(bf16[8,432,128]{2,1,0:T(8,128)(2,1)} %bitcast.23), calls=%async_computation | async-start | bytes 1769472 | tf_op jit(solution)/shard_map/all_to_all | solution.py:433
  11.7 18.4 %copy-start.6 = (f32[3,3,1152]{2,1,0:T(4,128)S(1)}, f32[3,3,1152]{2,1,0:T(4,128)}, u32[]{:S(2)}) copy-start(f32[3,3,1152]{2,1,0:T(4,128)} %param.11) | copy-start | bytes 124420
  21.8 14.6 %collective-permute-start = (bf16[14,144,128]{2,1,0:T(8,128)(2,1)}, bf16[14,144,128]{2,1,0:T(8,128)(2,1)S(1)}, u32[]{:S(2)}, u32[]{:S(2)}) collective-permute-start(bf16[14,144,128]{2,1,0:T(8,128)(2,1)} %get-tuple-element.21), channel_id=1, source_target_pairs={{0,8},{8,16},{16,24},{1,9},{9,17},{17,25},{2,10},{10,18},{18,26},{... | collective-permute-start | bytes 1548296 | tf_op jit(solution)/shard_map/ppermute | solution.py:460
  25.3 14.9 %collective-permute-start.1 = (bf16[14,144,128]{2,1,0:T(8,128)(2,1)S(1)}, bf16[14,144,128]{2,1,0:T(8,128)(2,1)S(1)}, u32[]{:S(2)}, u32[]{:S(2)}) collective-permute-start(bf16[14,144,128]{2,1,0:T(8,128)(2,1)S(1)} %get-tuple-element.22), channel_id=1, source_target_pairs={{8,0},{16,8},{24,16},{9,1},{17,9},{25,17},{10,2},{18,10},{26,18},{... | collective-permute-start | bytes 1548296 | tf_op jit(solution)/shard_map/ppermute | solution.py:459
  26.6 17.4 %all-to-all-start.1 = ((bf16[8,304,128]{2,1,0:T(8,128)(2,1)}), bf16[8,304,128]{2,1,0:T(8,128)(2,1)S(1)}, u32[]{:S(2)}, u32[]{:S(2)}) async-start(bf16[8,304,128]{2,1,0:T(8,128)(2,1)} %shard_map.111), calls=%async_computation.1 | async-start | bytes 1245184 | tf_op jit(solution)/shard_map/all_to_all | solution.py:433
  43.2 0.8 copy-start.4
  44.0 1.1 %copy-start.5 = (bf16[4,144,512]{2,1,0:T(8,128)(2,1)S(1)}, bf16[4,144,512]{2,1,0:T(8,128)(2,1)}, u32[]{:S(2)}) copy-start(bf16[4,144,512]{2,1,0:T(8,128)(2,1)} %copy-done.4) | copy-start | bytes 1769476
  55.2 0.8 copy-start.2
  56.1 13.1 %collective-permute-start.2 = (bf16[10,144,128]{2,1,0:T(8,128)(2,1)}, bf16[10,144,128]{2,1,0:T(8,128)(2,1)S(1)}, u32[]{:S(2)}, u32[]{:S(2)}) collective-permute-start(bf16[10,144,128]{2,1,0:T(8,128)(2,1)} %get-tuple-element.27), channel_id=1, source_target_pairs={{0,8},{8,16},{16,24},{1,9},{9,17},{17,25},{2,10},{10,18},{18,26},{... | collective-permute-start | bytes 1105928 | tf_op jit(solution)/shard_map/ppermute | solution.py:489
  59.5 10.6 %collective-permute-start.3 = (bf16[10,144,128]{2,1,0:T(8,128)(2,1)S(1)}, bf16[10,144,128]{2,1,0:T(8,128)(2,1)}, u32[]{:S(2)}, u32[]{:S(2)}) collective-permute-start(bf16[10,144,128]{2,1,0:T(8,128)(2,1)S(1)} %get-tuple-element.28), channel_id=1, source_target_pairs={{8,0},{16,8},{24,16},{9,1},{17,9},{25,17},{10,2},{18,10},{26,18},{... | collective-permute-start | bytes 1105928 | tf_op jit(solution)/shard_map/ppermute | solution.py:488
  64.6 1.0 %copy-start = (f32[4,144,512]{2,1,0:T(8,128)}, f32[4,144,512]{2,1,0:T(8,128)S(1)}, u32[]{:S(2)}) copy-start(f32[4,144,512]{2,1,0:T(8,128)S(1)} %get-tuple-element.24.dv_ref) | copy-start | bytes 3538948
  65.7 11.6 %all-to-all-start.2 = ((bf16[8,208,128]{2,1,0:T(8,128)(2,1)}), bf16[8,208,128]{2,1,0:T(8,128)(2,1)S(1)}, u32[]{:S(2)}, u32[]{:S(2)}) async-start(bf16[8,208,128]{2,1,0:T(8,128)(2,1)} %shard_map.115), calls=%async_computation.2 | async-start | bytes 851968 | tf_op jit(solution)/shard_map/all_to_all | solution.py:433
  70.2 1.3 %copy-start.1 = (f32[4,144,512]{2,1,0:T(8,128)S(1)}, f32[4,144,512]{2,1,0:T(8,128)}, u32[]{:S(2)}) copy-start(f32[4,144,512]{2,1,0:T(8,128)} %copy-done) | copy-start | bytes 3538948
  71.4 1.1 %copy-start.3 = (f32[2,144,512]{2,1,0:T(8,128)S(1)}, f32[2,144,512]{2,1,0:T(8,128)}, u32[]{:S(2)}) copy-start(f32[2,144,512]{2,1,0:T(8,128)} %copy-done.2) | copy-start | bytes 1769476
  77.3 17.0 %all-to-all-start.3 = ((bf16[8,432,128]{2,1,0:T(8,128)(2,1)}), bf16[8,432,128]{2,1,0:T(8,128)(2,1)S(1)}, u32[]{:S(2)}, u32[]{:S(2)}) async-start(bf16[8,432,128]{2,1,0:T(8,128)(2,1)} %bitcast.12), calls=%async_computation.3 | async-start | bytes 1769472 | tf_op jit(solution)/shard_map/all_to_all | solution.py:433
  81.7 5.1 %collective-permute-start.4 = (f32[16,1152]{1,0:T(8,128)S(1)}, f32[16,1152]{1,0:T(8,128)S(1)}, u32[]{:S(2)}, u32[]{:S(2)}) collective-permute-start(f32[16,1152]{1,0:T(8,128)S(1)} %get-tuple-element.32.x_ref), channel_id=1, source_target_pairs={{0,8},{8,0},{16,24},{24,16},{1,9},{9,1},{17,25},{25,17},{2,10},{10... | collective-permute-start | bytes 221192 | tf_op jit(solution)/shard_map/ppermute | solution.py:513
  86.8 6.8 %collective-permute-start.5 = (f32[16,1152]{1,0:T(8,128)S(1)}, f32[16,1152]{1,0:T(8,128)S(1)}, u32[]{:S(2)}, u32[]{:S(2)}) collective-permute-start(f32[16,1152]{1,0:T(8,128)S(1)} %shard_map.119.x_ref), channel_id=1, source_target_pairs={{0,16},{8,24},{16,0},{24,8},{1,17},{9,25},{17,1},{25,9},{2,18},{10... | collective-permute-start | bytes 221192 | tf_op jit(solution)/shard_map/ppermute | solution.py:516

commit v3 on v2

v3 whole, which is shorter than its diff:
```python
import functools
import math

import jax
import jax.numpy as jnp
from jax import lax
from jax.experimental import pallas as pl
from jax.experimental.pallas import tpu as pltpu
from jax.sharding import Mesh, PartitionSpec as P

HEADS = 16
HEAD_DIM = 72
ROWS = 2
LANES = 128
HALF = 64
NEG = -1e30
INV_ROOT = HEAD_DIM ** (-0.5)
LOG2E = 1.4426950408889634
BF = jnp.bfloat16
F32 = jnp.float32


def params(mib):
    return pltpu.CompilerParams(vmem_limit_bytes=mib << 20)


ANY = pl.BlockSpec(memory_space=pl.ANY)
VMEM = pl.BlockSpec(memory_space=pltpu.VMEM)


def call(body, outs, *args, scratch=(), flops=0, mib=8, aliases=None, far_in=(), far_out=(), hbm=()):
    moved = sum(a.size * a.dtype.itemsize for a in args)
    moved += sum(math.prod(shape) * jnp.dtype(dtype).itemsize for shape, dtype in outs)
    return pl.pallas_call(
        body,
        out_shape=[
            pltpu.HBM(shape, dtype) if n in hbm else jax.ShapeDtypeStruct(shape, dtype)
            for n, (shape, dtype) in enumerate(outs)
        ],
        in_specs=[ANY if n in far_in else VMEM for n in range(len(args))],
        out_specs=[ANY if n in far_out else VMEM for n in range(len(outs))],
        scratch_shapes=list(scratch),
        input_output_aliases=aliases or {},
        compiler_params=params(mib),
        cost_estimate=pl.CostEstimate(flops=flops, bytes_accessed=moved, transcendentals=0),
    )(*args)


def my_halves():
    odd = lax.rem(lax.axis_index("c"), 2)
    return [pl.ds(pl.multiple_of(x * HALF, HALF), HALF) for x in (odd, 1 - odd)]


def store_halves(out, x):
    for i, half in enumerate(my_halves()):
        out[half] = x[i * HALF : (i + 1) * HALF]


def pack_body(parts, ch, chp, *refs):
    ins = refs[:parts]
    live, out = refs[parts:-4], refs[-4]
    held, packed, sems = refs[-3:]
    halves = my_halves()

    def get(n):
        return [
            pltpu.make_async_copy(
                ins[n].at[halves[i]], held.at[n, pl.ds(i * HALF, HALF)], sems.at[i, n]
            )
            for i in range(2)
        ]

    for n in range(parts):
        for copy in get(n):
            copy.start()
    backs = []
    for n in range(parts):
        for copy in get(n):
            copy.wait()
        x = held[n]
        if ch % 16:
            x = x.astype(F32)
        x = x.T
        rows = pl.ds(n * chp, chp)
        for p in range(out.shape[0]):
            piece = x[p * ch : (p + 1) * ch]
            if chp > ch:
                piece = jnp.concatenate([piece, jnp.zeros((chp - ch, LANES), piece.dtype)], axis=0)
            packed[p, n * chp : (n + 1) * chp] = piece.astype(BF)
        if n == parts - 1 and live:
            for p in range(out.shape[0]):
                packed[p, parts * chp :] = live[0][...].astype(BF)
            rows = pl.ds(n * chp, chp + 16)
        backs.append(pltpu.make_async_copy(packed.at[:, rows], out.at[:, rows], sems.at[2, n]))
        backs[n].start()
    for back in backs:
        back.wait()


def unpack_body(ch, x_ref, *outs):
    peers = x_ref.shape[0]
    for n, out in enumerate(outs):
        pieces = [x_ref[p, n] for p in range(peers)]
        if ch % 16:
            pieces = [piece.astype(F32)[:ch] for piece in pieces]
        store_halves(out, jnp.concatenate(pieces, axis=0).T.astype(BF))


def unpack_query_body(ch, chp, x_ref, out, gk_ref):
    peers = x_ref.shape[0]
    pieces = [x_ref[p, :chp] for p in range(peers)]
    if ch % 16:
        pieces = [piece.astype(F32)[:ch] for piece in pieces]
    store_halves(out, jnp.concatenate(pieces, axis=0).T.astype(BF))
    blocks = (x_ref.shape[1] - chp) // 32
    wide = gk_ref.shape[1]
    total = [jnp.zeros((16, LANES), F32) for _ in range(wide // LANES + 2)]
    lane = lax.broadcasted_iota(jnp.int32, (16, LANES), 1)
    for p in range(peers):
        first, off = divmod(p * ch, LANES)
        for b in range(blocks):
            at = chp + 32 * b
            piece = x_ref[p, at : at + 16].astype(F32) + x_ref[p, at + 16 : at + 32].astype(F32)
            turned = pltpu.roll(piece, off, 1) if off else piece
            total[first + b] = total[first + b] + jnp.where(lane >= off, turned, 0.0)
            if off:
                total[first + b + 1] = total[first + b + 1] + jnp.where(lane < off, turned, 0.0)
    gk_ref[...] = jnp.concatenate(total[: wide // LANES], axis=1)


def taps_out_body(x_ref, y_ref, out):
    total = x_ref[...] + y_ref[...]
    for a in range(3):
        out[a] = total[3 * a : 3 * a + 3]


def add_body(x_ref, y_ref, out):
    out[...] = x_ref[...] + y_ref[...]


def second_rows(rows):
    lane = lax.broadcasted_iota(jnp.int32, (rows, LANES), 1)
    return lane >= HALF, lane < HALF


def lane_masks(rows):
    col = lax.broadcasted_iota(jnp.int32, (rows, LANES), 1) & (HALF - 1)
    return second_rows(rows), col == 0, col == HALF - 1


def col_shifts(tiles, masks):
    _, first, last = masks
    none = jnp.zeros_like(tiles[0])
    out = []
    for j, t in enumerate(tiles):
        before = tiles[j - 1] if j else none
        after = tiles[j + 1] if j + 1 < len(tiles) else none
        out.append(
            (
                pltpu.roll(jnp.where(last, before, t), 1, 1),
                t,
                pltpu.roll(jnp.where(first, after, t), LANES - 1, 1),
            )
        )
    return out


def conv_rows(rows, coef, masks):
    second = masks[0]
    count = len(rows)
    out = []
    last = None
    for i in range(count):
        here = []
        for j, t in enumerate(col_shifts(rows[i], masks)):
            use = [i < count - 1, 0 < i < count - 1, i > 0]
            here.append(
                [
                    coef[3 * a] * t[0] + coef[3 * a + 1] * t[1] + coef[3 * a + 2] * t[2] if use[a] else None
                    for a in range(3)
                ]
            )
        if i >= 2:
            out.append(
                [
                    m + pltpu.roll(u + jnp.where(second[j % 2], d, n[2]), HALF, 1)
                    for j, ((m, u, d), n) in enumerate(zip(last, here))
                ]
            )
        if 0 < i < count - 1:
            last = [
                (n[1], jnp.where(second[j % 2], p, n[0]), n[2])
                for j, (p, n) in enumerate(zip(before, here))
            ]
        before = [n[0] for n in here]
    return out


def taps(kc_ref, at):
    block = kc_ref[at, :]
    return [jnp.broadcast_to(block[:, t : t + 1], (16, LANES)) for t in range(9)]


def rim_body(a_ref, up_ref, down_ref):
    cols = a_ref.shape[0] // ROWS
    second = second_rows(a_ref.shape[2])
    for out, row, further, want in ((up_ref, 0, 1, 0), (down_ref, ROWS - 1, ROWS - 2, 1)):
        for j in range(cols):
            for n in range(3):
                out[n * cols + j] = a_ref[row * cols + j, n]
        for m in range(0, cols, 2):
            even, odd = (a_ref[further * cols + m + i, 2].astype(F32) for i in range(2))
            out[3 * cols + m // 2] = jnp.where(second[want], odd, even).astype(BF)


def control_rows(a_ref, u_ref, d_ref, at):
    cols = a_ref.shape[0] // ROWS
    rows = [
        [u_ref[3 * cols + j // 2, at, :] for j in range(cols)],
        [u_ref[2 * cols + j, at, :] for j in range(cols)],
        *[[a_ref[r * cols + j, 2, at, :] for j in range(cols)] for r in range(ROWS)],
        [d_ref[2 * cols + j, at, :] for j in range(cols)],
        [d_ref[3 * cols + j // 2, at, :] for j in range(cols)],
    ]
    return [[x.astype(F32) for x in row] for row in rows]


def values_body(a_ref, u_ref, d_ref, kc_ref, a_out, u_out, d_out):
    cols = a_ref.shape[0] // ROWS
    chp = a_ref.shape[2]

    @pl.loop(0, chp // 16)
    def _(step):
        at = pl.ds(pl.multiple_of(step * 16, 16), 16)
        conv = conv_rows(control_rows(a_ref, u_ref, d_ref, at), taps(kc_ref, at), lane_masks(16))
        for ref, out in ((u_ref, u_out), (d_ref, d_out)):
            for n in range(ref.shape[0]):
                if not cols <= n < 2 * cols:
                    out[n, at, :] = ref[n, at, :]
        for j in range(cols):
            for ref, out, i in ((u_ref, u_out, 0), (d_ref, d_out, -1)):
                out[cols + j, at, :] = (ref[cols + j, at, :].astype(F32) + conv[i][j]).astype(BF)
            for r in range(ROWS):
                tile = r * cols + j
                a_out[tile, 0, at, :] = a_ref[tile, 0, at, :]
                a_out[tile, 1, at, :] = (a_ref[tile, 1, at, :].astype(F32) + conv[r + 1][j]).astype(BF)
                a_out[tile, 2, at, :] = a_ref[tile, 2, at, :]


def attend_body(heads, q_ref, a_ref, u_ref, d_ref, dq_ref, up_ref, down_ref, dk_ref, dv_ref):
    peers = q_ref.shape[0]
    cols = peers // ROWS
    chp = a_ref.shape[2]
    wide = cols * LANES

    dk_ref[...] = jnp.zeros_like(dk_ref)
    dv_ref[...] = jnp.zeros_like(dv_ref)
    chan = lax.broadcasted_iota(jnp.int32, (chp, LANES), 0)
    mine = [(chan >= h * HEAD_DIM) & (chan < (h + 1) * HEAD_DIM) for h in range(heads)]

    def spread(x):
        x = x.astype(F32)
        return jnp.concatenate([jnp.where(m, x, 0.0) for m in mine], axis=1).astype(BF)

    def dot(x, y, on_x, on_y):
        return lax.dot_general(
            x, y, (((on_x,), (on_y,)), ((), ())), preferred_element_type=F32
        )

    for r in range(ROWS):

        for j in range(cols):
            tile = r * cols + j
            span = slice(j * LANES, (j + 1) * LANES)
            q = spread(q_ref[tile, :chp])
            g = spread(q_ref[tile, chp : 2 * chp])

            def all_keys(n):
                above = u_ref[n * cols + j] if r == 0 else a_ref[tile - cols, n]
                below = d_ref[n * cols + j] if r == ROWS - 1 else a_ref[tile + cols, n]
                row = [a_ref[r * cols + p, n] for p in range(cols)]
                return jnp.concatenate(row + [above, below], axis=1)

            k = all_keys(0)
            v = all_keys(1)
            live = q_ref[tile, 2 * chp :].astype(F32)
            zero = jnp.zeros((1, LANES), F32)
            bias = jnp.concatenate(
                [live[p : p + 1] for p in range(cols)]
                + [
                    live[cols : cols + 1] if r == 0 else zero,
                    live[cols + 1 : cols + 2] if r == ROWS - 1 else zero,
                ],
                axis=1,
            )
            s = dot(q, k, 0, 0) + bias
            top = jnp.max(s, axis=1, keepdims=True)
            e = jnp.exp2((s - top) * (INV_ROOT * LOG2E))
            w = e * (1.0 / jnp.sum(e, axis=1, keepdims=True))
            gw = dot(g, v, 0, 0)
            delta = jnp.sum(w * gw, axis=1, keepdims=True)
            gs = (w * (gw - delta)).astype(BF)
            dk = dot(q, gs, 1, 0)
            dv = dot(g, w.astype(BF), 1, 0)
            dq = dot(k, gs, 1, 1)
            own = dq[:, :LANES]
            for h in range(1, heads):
                own = jnp.where(mine[h], dq[:, h * LANES : (h + 1) * LANES], own)
            dq_ref[tile] = (own * INV_ROOT).astype(BF)
            dk_ref[r] += dk[:, :wide]
            dv_ref[r] += dv[:, :wide]
            for side, at in ((r - 1, wide), (r + 1, wide + LANES)):
                dk_side, dv_side = dk[:, at : at + LANES], dv[:, at : at + LANES]
                if 0 <= side < ROWS:
                    dk_ref[side, :, span] += dk_side
                    dv_ref[side, :, span] += dv_side
                else:
                    out = up_ref if side < 0 else down_ref
                    out[j] = (dk_side * INV_ROOT).astype(BF)
                    out[cols + j] = dv_side.astype(BF)

    second = second_rows(chp)
    for out, row, want in ((up_ref, 0, 0), (down_ref, ROWS - 1, 1)):
        for m in range(0, cols, 2):
            even, odd = (dv_ref[row, :, (m + i) * LANES : (m + i + 1) * LANES] for i in range(2))
            out[2 * cols + m // 2] = jnp.where(second[1 - want], even, odd).astype(BF)


def value_terms(dv_ref, up_ref, down_ref, i, j, at):
    cols = dv_ref.shape[2] // LANES
    if i == 0:
        return up_ref[cols + j, at, :].astype(F32)
    if i == ROWS + 1:
        return down_ref[cols + j, at, :].astype(F32)
    return dv_ref[i - 1, at, j * LANES : (j + 1) * LANES]


def kernel_grad_body(
    ch, dq_ref, a_ref, u_ref, d_ref, dk_ref, dv_ref, up_ref, down_ref, out_ref, dk_out, dv_out, sums, rows, sems
):
    cols = dv_ref.shape[2] // LANES
    chp = dv_ref.shape[1]
    copies = [
        pltpu.make_async_copy(dq_ref, out_ref.at[:, pl.ds(0, chp)], sems.at[0]),
        pltpu.make_async_copy(dk_ref, dk_out, sems.at[1]),
        pltpu.make_async_copy(dv_ref, dv_out, sems.at[2]),
    ]
    for copy in copies:
        copy.start()

    @pl.loop(0, chp // 16)
    def _(step):
        at = pl.ds(pl.multiple_of(step * 16, 16), 16)
        masks = lane_masks(16)
        second = masks[0]
        acc = [jnp.zeros((16, LANES), F32) for _ in range(9)]
        above = here = None
        for i, row in enumerate(control_rows(a_ref, u_ref, d_ref, at)):
            below = col_shifts(row, masks)
            if i >= 2:
                for j in range(cols):
                    g = value_terms(dv_ref, up_ref, down_ref, i - 2, j, at)
                    turned = pltpu.roll(g, HALF, 1)
                    for b in range(3):
                        acc[b] += jnp.where(second[j % 2], above[j][b], here[j][b]) * turned
                        acc[3 + b] += here[j][b] * g
                        acc[6 + b] += jnp.where(second[j % 2], here[j][b], below[j][b]) * turned
            above, here = here, below
        lane = lax.broadcasted_iota(jnp.int32, (16, LANES), 1)
        out = jnp.zeros((16, LANES), F32)
        for t in range(9):
            out = jnp.where(lane == t, jnp.sum(acc[t], axis=1, keepdims=True), out)
        sums[at, :] = out

    turned = sums[...].T[:16]
    blocks = rows.shape[1] // 32
    if blocks * LANES > chp:
        turned = jnp.concatenate([turned, jnp.zeros((16, blocks * LANES - chp), F32)], axis=1)
    lane = lax.broadcasted_iota(jnp.int32, turned.shape, 1)
    turned = jnp.where(lane < ch, turned, 0.0)
    high = turned.astype(BF)
    low = (turned - high.astype(F32)).astype(BF)
    for tile in range(rows.shape[0]):
        for b in range(blocks):
            rows[tile, 32 * b : 32 * b + 16] = high[:, b * LANES : (b + 1) * LANES]
            rows[tile, 32 * b + 16 : 32 * b + 32] = low[:, b * LANES : (b + 1) * LANES]
    sums_out = pltpu.make_async_copy(rows, out_ref.at[:, pl.ds(chp, 32 * blocks)], sems.at[3])
    sums_out.start()
    for copy in copies + [sums_out]:
        copy.wait()


def finish_body(
    dk_hbm, dv_hbm, up_ref, down_ref, u_ref, d_ref, kc_ref, out_ref, dk_ref, dv_ref, held, sems
):
    cols = held.shape[0] // ROWS
    chp = held.shape[2]

    def chunk(step):
        return pl.ds(pl.multiple_of(step * 16, 16), 16)

    def get(step):
        at = chunk(step)
        return [
            pltpu.make_async_copy(dk_hbm.at[:, at], dk_ref.at[:, at], sems.at[0, step]),
            pltpu.make_async_copy(dv_hbm.at[:, at], dv_ref.at[:, at], sems.at[1, step]),
        ]

    def put(step):
        at = chunk(step)
        return pltpu.make_async_copy(held.at[:, :, at], out_ref.at[:, :, at], sems.at[2, step])

    @pl.loop(0, chp // 16)
    def _(step):
        for copy in get(step):
            copy.start()

    @pl.loop(0, chp // 16)
    def _(step):
        for copy in get(step):
            copy.wait()
        at = chunk(step)
        masks = lane_masks(16)
        coef = taps(kc_ref, at)[::-1]

        def from_side(ref, n):
            return ref[n, at, :].astype(F32)

        def rounded(x):
            return x.astype(BF).astype(F32)

        rows = []
        for i in range(ROWS + 2):
            row = []
            for j in range(cols):
                x = value_terms(dv_ref, up_ref, down_ref, i, j, at)
                if i == 0:
                    rim = from_side(u_ref, 2 * cols + j // 2)
                    x = x + rim
                elif i == ROWS + 1:
                    rim = from_side(d_ref, 2 * cols + j // 2)
                    x = x + rim
                else:
                    if i == 1:
                        x = x + from_side(u_ref, cols + j)
                    if i == ROWS:
                        x = x + from_side(d_ref, cols + j)
                row.append(rounded(x))
            rows.append(row)
        conv = conv_rows(rows, coef, masks)
        for r in range(ROWS):
            for j in range(cols):
                tile = r * cols + j
                k = dk_ref[r, at, j * LANES : (j + 1) * LANES] * INV_ROOT
                if r == 0:
                    k = k + from_side(u_ref, j)
                if r == ROWS - 1:
                    k = k + from_side(d_ref, j)
                held[tile, 0, at, :] = k.astype(BF)
                held[tile, 1, at, :] = rows[r + 1][j].astype(BF)
                held[tile, 2, at, :] = conv[r][j].astype(BF)
        put(step).start()

    @pl.loop(0, chp // 16)
    def _(step):
        put(step).wait()


def per_device(query, key, value, control, kernel, grad_out, detail_blocks):
    shape = query.shape
    channels = shape[2]
    planes = lax.axis_size("z")
    cols = lax.axis_size("c")
    peers = ROWS * cols
    heads = HEADS // peers
    ch = heads * HEAD_DIM
    chp = -(-ch // 16) * 16
    plane = ("x", "c")
    my_z = lax.axis_index("z")
    my_col = lax.axis_index("c")
    me = lax.axis_index("x") * cols + my_col

    def flat(x):
        return x.reshape(LANES, channels)

    def swap(x):
        return lax.all_to_all(x.reshape(peers, -1, LANES), plane, 0, 0, tiled=True)

    def pack(arrays, *live):
        parts = len(arrays)
        rows = parts * chp + 16 * len(live)
        (out,) = call(
            functools.partial(pack_body, parts, ch, chp),
            [((peers, rows, LANES), BF)],
            *[flat(x) for x in arrays], *live,
            scratch=[
                pltpu.VMEM((parts, LANES, channels), BF),
                pltpu.VMEM((peers, rows, LANES), BF),
                pltpu.SemaphoreType.DMA((3, parts)),
            ],
            mib=56,
            far_in=range(parts),
            far_out=(0,),
        )
        return out

    sent = pack([key, value, control])
    mine = swap(sent).reshape(peers, 3, chp, LANES)
    wanted = lax.dynamic_index_in_dim(detail_blocks[0], my_col, 0, keepdims=False)
    named = (wanted >= 0) | (jnp.arange(cols) == my_col)
    named = jnp.concatenate([named, jnp.stack([my_z >= 1, my_z + 1 < planes])])
    live = jnp.where(jnp.pad(named, (0, 14 - cols)), 0.0, NEG).astype(F32)
    live = jnp.broadcast_to(live[:, None], (16, LANES))
    sent_q = pack([query, grad_out], live)
    mine, sent_q = lax.optimization_barrier((mine, sent_q))
    down_pairs = [(i, i + 1) for i in range(planes - 1)]
    up_pairs = [(i + 1, i) for i in range(planes - 1)]
    rim = (3 * cols + cols // 2, chp, LANES)
    to_up, to_down = call(rim_body, [(rim, BF)] * 2, mine)
    below = lax.ppermute(to_up, "z", up_pairs)
    above = lax.ppermute(to_down, "z", down_pairs)

    coefs = lax.dynamic_slice_in_dim(kernel.reshape(9, channels), me * ch, ch, 1)
    coefs = jnp.pad(coefs.T, ((0, chp - ch), (0, LANES - 9)))
    queries = swap(sent_q)

    wide = cols * LANES

    def tiles(*lead):
        return lead + (chp, LANES), BF

    mine, above, below = call(
        values_body,
        [(x.shape, BF) for x in (mine, above, below)],
        mine, above, below, coefs,
        flops=4 * 10**9,
        aliases={0: 0, 1: 1, 2: 2},
    )
    side = (2 * cols + cols // 2, chp, LANES)
    flops = 10 * peers * heads * LANES * (wide + 2 * LANES) * 256
    dq, to_up, to_down, dk, dv = call(
        functools.partial(attend_body, heads),
        [
            ((peers, chp, LANES), BF),
            (side, BF),
            (side, BF),
            ((ROWS, chp, wide), F32),
            ((ROWS, chp, wide), F32),
        ],
        queries, mine, above, below,
        flops=flops,
        mib=6,
    )
    from_above = lax.ppermute(to_down, "z", down_pairs)
    from_below = lax.ppermute(to_up, "z", up_pairs)

    blocks = -(-ch // LANES)
    own = ((ROWS, chp, wide), F32)
    sent_dq, dk, dv = call(
        functools.partial(kernel_grad_body, ch),
        [((peers, chp + 32 * blocks, LANES), BF), own, own],
        dq, mine, above, below, dk, dv, to_up, to_down,
        scratch=[
            pltpu.VMEM((chp, LANES), F32),
            pltpu.VMEM((peers, 32 * blocks, LANES), BF),
            pltpu.SemaphoreType.DMA((4,)),
        ],
        far_out=(0, 1, 2),
        hbm=(1, 2),
        flops=4 * 10**9,
    )
    dq_back = swap(sent_dq)

    (results,) = call(
        finish_body, [tiles(peers, 3)],
        *[pltpu.with_memory_space_constraint(x, pltpu.HBM) for x in (dk, dv)],
        to_up, to_down, from_above, from_below, coefs,
        scratch=[
            pltpu.VMEM((ROWS, chp, wide), F32),
            pltpu.VMEM((ROWS, chp, wide), F32),
            pltpu.VMEM((peers, 3, chp, LANES), BF),
            pltpu.SemaphoreType.DMA((3, chp // 16)),
        ],
        far_in=(0, 1),
        far_out=(0,),
        flops=4 * 10**9,
    )
    back = swap(results).reshape(peers, 3, chp, LANES)
    grad_query, taps_sum = call(
        functools.partial(unpack_query_body, ch, chp),
        [((LANES, channels), BF), ((16, channels), F32)],
        dq_back,
    )
    step = 1
    while 2 * step < planes:
        other = lax.ppermute(taps_sum, "z", [(i, i ^ step) for i in range(planes)])
        (taps_sum,) = call(add_body, [((16, channels), F32)], taps_sum, other)
        step *= 2
    other = lax.ppermute(taps_sum, "z", [(i, i ^ step) for i in range(planes)])
    (grad_kernel,) = call(taps_out_body, [((3, 3, channels), F32)], taps_sum, other)
    outs = call(functools.partial(unpack_body, ch), [((LANES, channels), BF)] * 3, back)
    return tuple(x.reshape(shape) for x in [grad_query] + list(outs)) + (grad_kernel,)


def solution(mesh):
    trow, tcol = mesh.shape["trow"], mesh.shape["tcol"]
    grid = Mesh(mesh.devices.reshape(trow // ROWS, ROWS, tcol), ("z", "x", "c"))
    tiled = P(("z", "x"), "c", None)
    return jax.shard_map(
        per_device,
        mesh=grid,
        in_specs=(tiled, tiled, tiled, tiled, P(), tiled, P(("z", "x"), None, None)),
        out_specs=(tiled, tiled, tiled, tiled, P()),
        check_vma=False,
    )
```

time: 96 us -> 89.1 us (0.928)
  local copies, waits for them, and re-layouts: 6.96 us -> 0.91 us
  Pallas kernels: 29.7 us -> 26.3 us
  waiting for transfers between devices: 26.9 us -> 28.8 us
    unnamed x15 -> x3, local copies, waits for them, and re-layouts: 6.17 us -> 0.12 us
    pallas_call x11, Pallas kernels: 29.7 us -> 26.3 us  [call(): pl.pallas_call(body, out_shape=[pltpu.HBM(shape, dtype) if n in hbm else...]
    all_to_all x4, waiting for transfers between devices: 9.15 us -> 11.5 us  [swap(): return lax.all_to_all(x.reshape(peers, -1, LANES), plane, 0, 0, tiled=True)]
    ppermute x1, starting transfers between devices: 3.47 us -> 5.31 us  [per_device(): from_above = lax.ppermute(to_down, 'z', down_pairs)]
    ppermute x2, starting transfers between devices: 5 us -> 3.42 us  [per_device(): other = lax.ppermute(taps_sum, 'z', [(i, i ^ step) for i in range(planes)])]
    ppermute x1, waiting for transfers between devices: 1.04 us -> 0.01 us  [per_device(): from_below = lax.ppermute(to_up, 'z', up_pairs)]
  transfers between devices with their start and end apart: 10 -> 10, of which waited for: 6 -> 7; matrix products, arithmetic and copies ran while one was open for 2% -> 2% of each run, Pallas kernels for 16% -> 18%
where the time goes in v3:
time: 89.1 us; the launch traced here: 88.4 us
  starting transfers between devices  30.7 us (34%)
  waiting for transfers between devices  28.8 us (32%)
  Pallas kernels  26.3 us (30%)
  local copies, waits for them, and re-layouts  0.91 us (1%)
    pallas_call x11, Pallas kernels, call(): pl.pallas_call(body, out_shape=[pltpu.HBM(shape, dtype) if n in hbm else...  26.3 us
    all_to_all x4, starting transfers between devices, swap(): return lax.all_to_all(x.reshape(peers, -1, LANES), plane, 0, 0, tiled=True)  15.8 us
    all_to_all x4, waiting for transfers between devices, swap(): return lax.all_to_all(x.reshape(peers, -1, LANES), plane, 0, 0, tiled=True)  11.5 us
    ppermute x2, waiting for transfers between devices, per_device(): other = lax.ppermute(taps_sum, 'z', [(i, i ^ step) for i in range(planes)])  7.54 us
    ppermute x1, waiting for transfers between devices, per_device(): above = lax.ppermute(to_down, 'z', down_pairs)  5.81 us
    ppermute x1, starting transfers between devices, per_device(): from_above = lax.ppermute(to_down, 'z', down_pairs)  5.31 us
    ppermute x1, waiting for transfers between devices, per_device(): below = lax.ppermute(to_up, 'z', up_pairs)  3.97 us
    ppermute x1, starting transfers between devices, per_device(): above = lax.ppermute(to_down, 'z', down_pairs)  3.5 us
  transfers between devices with their start and end apart: 10, of which 7 were waited for; matrix products, arithmetic and copies ran while one was open for 2% of the time, Pallas kernels for 18%

profile of v3, /device:TPU:0, one launch (start us, length us, event | category | flops | bytes accessed | tf_op | source)
XLA Modules:
  0.0 88.4 jit_solution(4496040835237401014)
XLA Ops:
  0.6 2.2 %shard_map.110 = bf16[8,432,128]{2,1,0:T(8,128)(2,1)} custom-call(bf16[128,1152]{1,0:T(8,128)(2,1)} %bitcast.20, bf16[128,1152]{1,0:T(8,128)(2,1)} %bitcast.21, bf16[128,1152]{1,0:T(8,128)(2,1)} %bitcast.22), custom_call_target="tpu_custom_call" | custom-call | bytes 1769472 | tf_op jit(solution)/shard_map/pallas_call | solution.py:34
  2.9 5.2 %all-to-all-start = ((bf16[8,432,128]{2,1,0:T(8,128)(2,1)}), bf16[8,432,128]{2,1,0:T(8,128)(2,1)S(1)}, u32[]{:S(2)}, u32[]{:S(2)}) async-start(bf16[8,432,128]{2,1,0:T(8,128)(2,1)} %shard_map.110), calls=%async_computation | async-start | bytes 1769472 | tf_op jit(solution)/shard_map/all_to_all | solution.py:487
  8.1 0.7 bitcast_or_fusion
  8.7 0.1 pad_add_fusion
  8.8 0.7 broadcast_in_dim.16.refs_2_
  9.5 2.7 %shard_map.111 = bf16[8,304,128]{2,1,0:T(8,128)(2,1)} custom-call(bf16[128,1152]{1,0:T(8,128)(2,1)} %bitcast.24, bf16[128,1152]{1,0:T(8,128)(2,1)} %bitcast.25, f32[16,128]{1,0:T(8,128)} %broadcast_in_dim.16.refs_2_), custom_call_target="tpu_custom_call" | custom-call | bytes 1220608 | tf_op jit(solution)/shard_map/pallas_call | solution.py:34
  12.3 8.5 %all-to-all-done = bf16[8,432,128]{2,1,0:T(8,128)(2,1)S(1)} async-done(((bf16[8,432,128]{2,1,0:T(8,128)(2,1)}), bf16[8,432,128]{2,1,0:T(8,128)(2,1)S(1)}, u32[]{:S(2)}, u32[]{:S(2)}) %all-to-all-start) | async-done | bytes 884768 | tf_op jit(solution)/shard_map/all_to_all | solution.py:487
  20.8 0.9 shard_map.112
  21.6 3.5 %collective-permute-start = (bf16[14,144,128]{2,1,0:T(8,128)(2,1)}, bf16[14,144,128]{2,1,0:T(8,128)(2,1)S(1)}, u32[]{:S(2)}, u32[]{:S(2)}) collective-permute-start(bf16[14,144,128]{2,1,0:T(8,128)(2,1)} %get-tuple-element.27), channel_id=1, source_target_pairs={{0,8},{8,16},{16,24},{1,9},{9,17},{17,25},{2,10},{10,18},{18,26},{... | collective-permute-start | bytes 1548296 | tf_op jit(solution)/shard_map/ppermute | solution.py:521
  25.1 0.0 copy-start
  25.1 1.4 %collective-permute-start.1 = (bf16[14,144,128]{2,1,0:T(8,128)(2,1)S(1)}, bf16[14,144,128]{2,1,0:T(8,128)(2,1)S(1)}, u32[]{:S(2)}, u32[]{:S(2)}) collective-permute-start(bf16[14,144,128]{2,1,0:T(8,128)(2,1)S(1)} %get-tuple-element.28), channel_id=1, source_target_pairs={{8,0},{16,8},{24,16},{9,1},{17,9},{25,17},{10,2},{18,10},{26,18},{... | collective-permute-start | bytes 1548296 | tf_op jit(solution)/shard_map/ppermute | solution.py:520
  26.6 3.6 %all-to-all-start.1 = ((bf16[8,304,128]{2,1,0:T(8,128)(2,1)}), bf16[8,304,128]{2,1,0:T(8,128)(2,1)S(1)}, u32[]{:S(2)}, u32[]{:S(2)}) async-start(bf16[8,304,128]{2,1,0:T(8,128)(2,1)} %shard_map.111), calls=%async_computation.1 | async-start | bytes 1245184 | tf_op jit(solution)/shard_map/all_to_all | solution.py:487
  30.1 0.0 copy-done
  30.2 0.1 constant_dynamic-slice_fusion
  30.3 0.1 copy.17
  30.4 5.8 %collective-permute-done.u_ref = bf16[14,144,128]{2,1,0:T(8,128)(2,1)S(1)} collective-permute-done((bf16[14,144,128]{2,1,0:T(8,128)(2,1)}, bf16[14,144,128]{2,1,0:T(8,128)(2,1)S(1)}, u32[]{:S(2)}, u32[]{:S(2)}) %collective-permute-start) | collective-permute-done | bytes 516128 | tf_op jit(solution)/shard_map/ppermute | solution.py:521
  36.2 4.0 %collective-permute-done.1.d_ref = bf16[14,144,128]{2,1,0:T(8,128)(2,1)S(1)} collective-permute-done((bf16[14,144,128]{2,1,0:T(8,128)(2,1)S(1)}, bf16[14,144,128]{2,1,0:T(8,128)(2,1)S(1)}, u32[]{:S(2)}, u32[]{:S(2)}) %collective-permute-start.1) | collective-permute-done | bytes 516128 | tf_op jit(solution)/shard_map/ppermute | solution.py:520
  40.2 3.3 %shard_map.113 = (bf16[8,3,144,128]{3,2,1,0:T(8,128)(2,1)S(1)}, bf16[14,144,128]{2,1,0:T(8,128)(2,1)S(1)}, bf16[14,144,128]{2,1,0:T(8,128)(2,1)S(1)}) custom-call(bf16[8,3,144,128]{3,2,1,0:T(8,128)(2,1)S(1)} %bitcast.18, bf16[14,144,128]{2,1,0:T(8,128)(2,1)S(1)} %collective-permute-done.u_ref, ...), custom_call_target="tpu_custom_call", output_to_operand_aliasing={{0}: (0, {}), {1}: (1, {}), {2}: (2, {})} | custom-call | flops 4000000000 | bytes 3907584 | tf_op jit(solution)/shard_map/pallas_call | solution.py:34
  43.5 0.0 all-to-all-done.1.q_ref
  43.5 6.7 %shard_map.114 = (bf16[8,144,128]{2,1,0:T(8,128)(2,1)S(1)}, bf16[10,144,128]{2,1,0:T(8,128)(2,1)S(1)}, bf16[10,144,128]{2,1,0:T(8,128)(2,1)S(1)}, f32[2,144,512]{2,1,0:T(8,128)S(1)}, f32[2,144,512]{2,1,0:T(8,128)S(1)}) custom-call(bf16[8,304,128]{2,1,0:T(8,128)(2,1)S(1)} %all-to-all-done.1.q_ref, bf16[8,3,144,128]{3,2,1,0:T(8,128)(2,1)S(1)} %get-tuple-element.29.a_ref, ...), custom_call_target="tpu_custom_call" | custom-call | flops 4026531840 | bytes 4751360 | tf_op jit(solution)/shard_map/pallas_call | solution.py:34
  50.2 1.3 %collective-permute-start.3 = (bf16[10,144,128]{2,1,0:T(8,128)(2,1)S(1)}, bf16[10,144,128]{2,1,0:T(8,128)(2,1)}, u32[]{:S(2)}, u32[]{:S(2)}) collective-permute-start(bf16[10,144,128]{2,1,0:T(8,128)(2,1)S(1)} %get-tuple-element.35.up_ref), channel_id=1, source_target_pairs={{8,0},{16,8},{24,16},{9,1},{17,9},{25,17},{10,2},{18,10},{26,18},{... | collective-permute-start | bytes 1105928 | tf_op jit(solution)/shard_map/ppermute | solution.py:555
  51.5 5.3 %collective-permute-start.2 = (bf16[10,144,128]{2,1,0:T(8,128)(2,1)S(1)}, bf16[10,144,128]{2,1,0:T(8,128)(2,1)}, u32[]{:S(2)}, u32[]{:S(2)}) collective-permute-start(bf16[10,144,128]{2,1,0:T(8,128)(2,1)S(1)} %get-tuple-element.36.down_ref), channel_id=1, source_target_pairs={{0,8},{8,16},{16,24},{1,9},{9,17},{17,25},{2,10},{10,18},{18,26},{... | collective-permute-start | bytes 1105928 | tf_op jit(solution)/shard_map/ppermute | solution.py:554
  56.8 3.1 %shard_map.115 = (bf16[8,208,128]{2,1,0:T(8,128)(2,1)}, f32[2,144,512]{2,1,0:T(8,128)}, f32[2,144,512]{2,1,0:T(8,128)}) custom-call(bf16[8,144,128]{2,1,0:T(8,128)(2,1)S(1)} %get-tuple-element.32.dq_ref, bf16[8,3,144,128]{3,2,1,0:T(8,128)(2,1)S(1)} %get-tuple-element.29.a_ref, bf16[14,144,128]{2,1,0:T(8,128)(2,1)S(1)} %get-tuple-element.30.u_ref, ...), custom_call_target="tpu_custom_call" | custom-call | flops 4000000000 | bytes 5734400 | tf_op jit(solution)/shard_map/pallas_call | solution.py:34
  59.9 3.5 %all-to-all-start.2 = ((bf16[8,208,128]{2,1,0:T(8,128)(2,1)}), bf16[8,208,128]{2,1,0:T(8,128)(2,1)S(1)}, u32[]{:S(2)}, u32[]{:S(2)}) async-start(bf16[8,208,128]{2,1,0:T(8,128)(2,1)} %get-tuple-element.37), calls=%async_computation.2 | async-start | bytes 851968 | tf_op jit(solution)/shard_map/all_to_all | solution.py:487
  63.4 0.0 collective-permute-done.3.d_ref
  63.4 0.0 collective-permute-done.2.u_ref
  63.4 4.9 %shard_map.117 = bf16[8,3,144,128]{3,2,1,0:T(8,128)(2,1)} custom-call(f32[2,144,512]{2,1,0:T(8,128)} %get-tuple-element.39.dk_hbm, f32[2,144,512]{2,1,0:T(8,128)} %get-tuple-element.40.dv_hbm, bf16[10,144,128]{2,1,0:T(8,128)(2,1)S(1)} %get-tuple-element.35.up_ref, bf16[10,144,128]{2,1,0:T(8,128)(2,1)S(1)} %get-tuple-element.36.down_ref, ...), custom_call_target="tpu_custom_call" | custom-call | flops 4000000000 | bytes 3612672 | tf_op jit(solution)/shard_map/pallas_call | solution.py:34
  68.3 2.8 %all-to-all-done.2.x_ref = bf16[8,208,128]{2,1,0:T(8,128)(2,1)S(1)} async-done(((bf16[8,208,128]{2,1,0:T(8,128)(2,1)}), bf16[8,208,128]{2,1,0:T(8,128)(2,1)S(1)}, u32[]{:S(2)}, u32[]{:S(2)}) %all-to-all-start.2) | async-done | bytes 426016 | tf_op jit(solution)/shard_map/all_to_all | solution.py:487
  71.1 3.6 %all-to-all-start.3 = ((bf16[8,432,128]{2,1,0:T(8,128)(2,1)}), bf16[8,432,128]{2,1,0:T(8,128)(2,1)S(1)}, u32[]{:S(2)}, u32[]{:S(2)}) async-start(bf16[8,432,128]{2,1,0:T(8,128)(2,1)} %bitcast.11), calls=%async_computation.3 | async-start | bytes 1769472 | tf_op jit(solution)/shard_map/all_to_all | solution.py:487
  74.7 0.9 shard_map.116
  75.5 0.8 collective-permute-start.4
  76.4 3.8 %collective-permute-done.4.y_ref = f32[16,1152]{1,0:T(8,128)S(1)} collective-permute-done((f32[16,1152]{1,0:T(8,128)S(1)}, f32[16,1152]{1,0:T(8,128)S(1)}, u32[]{:S(2)}, u32[]{:S(2)}) %collective-permute-start.4) | collective-permute-done | bytes 73760 | tf_op jit(solution)/shard_map/ppermute | solution.py:596
  80.2 2.6 %collective-permute-start.5 = (f32[16,1152]{1,0:T(8,128)S(1)}, f32[16,1152]{1,0:T(8,128)S(1)}, u32[]{:S(2)}, u32[]{:S(2)}) collective-permute-start(f32[16,1152]{1,0:T(8,128)S(1)} %shard_map.119.x_ref), channel_id=1, source_target_pairs={{0,16},{8,24},{16,0},{24,8},{1,17},{9,25},{17,1},{25,9},{2,18},{10... | collective-permute-start | bytes 221192 | tf_op jit(solution)/shard_map/ppermute | solution.py:599
  82.8 3.7 %collective-permute-done.5.y_ref = f32[16,1152]{1,0:T(8,128)S(1)} collective-permute-done((f32[16,1152]{1,0:T(8,128)S(1)}, f32[16,1152]{1,0:T(8,128)S(1)}, u32[]{:S(2)}, u32[]{:S(2)}) %collective-permute-start.5) | collective-permute-done | bytes 73760 | tf_op jit(solution)/shard_map/ppermute | solution.py:599
  86.5 0.6 shard_map.120
  87.2 0.2 all-to-all-done.3
  87.3 1.0 %shard_map.118 = (bf16[128,1152]{1,0:T(8,128)(2,1)}, bf16[128,1152]{1,0:T(8,128)(2,1)}, bf16[128,1152]{1,0:T(8,128)(2,1)}) custom-call(bf16[8,3,144,128]{3,2,1,0:T(8,128)(2,1)S(1)} %bitcast.19), custom_call_target="tpu_custom_call" | custom-call | bytes 1769472 | tf_op jit(solution)/shard_map/pallas_call | solution.py:34
  (4 shorter events, 0.0 us)
Async XLA Ops:
  2.9 17.9 %all-to-all-start = ((bf16[8,432,128]{2,1,0:T(8,128)(2,1)}), bf16[8,432,128]{2,1,0:T(8,128)(2,1)S(1)}, u32[]{:S(2)}, u32[]{:S(2)}) async-start(bf16[8,432,128]{2,1,0:T(8,128)(2,1)} %shard_map.110), calls=%async_computation | async-start | bytes 1769472 | tf_op jit(solution)/shard_map/all_to_all | solution.py:487
  21.6 14.6 %collective-permute-start = (bf16[14,144,128]{2,1,0:T(8,128)(2,1)}, bf16[14,144,128]{2,1,0:T(8,128)(2,1)S(1)}, u32[]{:S(2)}, u32[]{:S(2)}) collective-permute-start(bf16[14,144,128]{2,1,0:T(8,128)(2,1)} %get-tuple-element.27), channel_id=1, source_target_pairs={{0,8},{8,16},{16,24},{1,9},{9,17},{17,25},{2,10},{10,18},{18,26},{... | collective-permute-start | bytes 1548296 | tf_op jit(solution)/shard_map/ppermute | solution.py:521
  25.1 5.0 %copy-start = (f32[3,3,1152]{2,1,0:T(4,128)S(1)}, f32[3,3,1152]{2,1,0:T(4,128)}, u32[]{:S(2)}) copy-start(f32[3,3,1152]{2,1,0:T(4,128)} %param.11) | copy-start | bytes 124420
  25.1 15.0 %collective-permute-start.1 = (bf16[14,144,128]{2,1,0:T(8,128)(2,1)S(1)}, bf16[14,144,128]{2,1,0:T(8,128)(2,1)S(1)}, u32[]{:S(2)}, u32[]{:S(2)}) collective-permute-start(bf16[14,144,128]{2,1,0:T(8,128)(2,1)S(1)} %get-tuple-element.28), channel_id=1, source_target_pairs={{8,0},{16,8},{24,16},{9,1},{17,9},{25,17},{10,2},{18,10},{26,18},{... | collective-permute-start | bytes 1548296 | tf_op jit(solution)/shard_map/ppermute | solution.py:520
  26.6 16.9 %all-to-all-start.1 = ((bf16[8,304,128]{2,1,0:T(8,128)(2,1)}), bf16[8,304,128]{2,1,0:T(8,128)(2,1)S(1)}, u32[]{:S(2)}, u32[]{:S(2)}) async-start(bf16[8,304,128]{2,1,0:T(8,128)(2,1)} %shard_map.111), calls=%async_computation.1 | async-start | bytes 1245184 | tf_op jit(solution)/shard_map/all_to_all | solution.py:487
  50.2 13.2 %collective-permute-start.3 = (bf16[10,144,128]{2,1,0:T(8,128)(2,1)S(1)}, bf16[10,144,128]{2,1,0:T(8,128)(2,1)}, u32[]{:S(2)}, u32[]{:S(2)}) collective-permute-start(bf16[10,144,128]{2,1,0:T(8,128)(2,1)S(1)} %get-tuple-element.35.up_ref), channel_id=1, source_target_pairs={{8,0},{16,8},{24,16},{9,1},{17,9},{25,17},{10,2},{18,10},{26,18},{... | collective-permute-start | bytes 1105928 | tf_op jit(solution)/shard_map/ppermute | solution.py:555
  51.5 11.9 %collective-permute-start.2 = (bf16[10,144,128]{2,1,0:T(8,128)(2,1)S(1)}, bf16[10,144,128]{2,1,0:T(8,128)(2,1)}, u32[]{:S(2)}, u32[]{:S(2)}) collective-permute-start(bf16[10,144,128]{2,1,0:T(8,128)(2,1)S(1)} %get-tuple-element.36.down_ref), channel_id=1, source_target_pairs={{0,8},{8,16},{16,24},{1,9},{9,17},{17,25},{2,10},{10,18},{18,26},{... | collective-permute-start | bytes 1105928 | tf_op jit(solution)/shard_map/ppermute | solution.py:554
  59.9 11.2 %all-to-all-start.2 = ((bf16[8,208,128]{2,1,0:T(8,128)(2,1)}), bf16[8,208,128]{2,1,0:T(8,128)(2,1)S(1)}, u32[]{:S(2)}, u32[]{:S(2)}) async-start(bf16[8,208,128]{2,1,0:T(8,128)(2,1)} %get-tuple-element.37), calls=%async_computation.2 | async-start | bytes 851968 | tf_op jit(solution)/shard_map/all_to_all | solution.py:487
  71.1 16.2 %all-to-all-start.3 = ((bf16[8,432,128]{2,1,0:T(8,128)(2,1)}), bf16[8,432,128]{2,1,0:T(8,128)(2,1)S(1)}, u32[]{:S(2)}, u32[]{:S(2)}) async-start(bf16[8,432,128]{2,1,0:T(8,128)(2,1)} %bitcast.11), calls=%async_computation.3 | async-start | bytes 1769472 | tf_op jit(solution)/shard_map/all_to_all | solution.py:487
  75.5 4.6 %collective-permute-start.4 = (f32[16,1152]{1,0:T(8,128)S(1)}, f32[16,1152]{1,0:T(8,128)S(1)}, u32[]{:S(2)}, u32[]{:S(2)}) collective-permute-start(f32[16,1152]{1,0:T(8,128)S(1)} %get-tuple-element.44.x_ref), channel_id=1, source_target_pairs={{0,8},{8,0},{16,24},{24,16},{1,9},{9,1},{17,25},{25,17},{2,10},{10... | collective-permute-start | bytes 221192 | tf_op jit(solution)/shard_map/ppermute | solution.py:596
  80.2 6.4 %collective-permute-start.5 = (f32[16,1152]{1,0:T(8,128)S(1)}, f32[16,1152]{1,0:T(8,128)S(1)}, u32[]{:S(2)}, u32[]{:S(2)}) collective-permute-start(f32[16,1152]{1,0:T(8,128)S(1)} %shard_map.119.x_ref), channel_id=1, source_target_pairs={{0,16},{8,24},{16,0},{24,8},{1,17},{9,25},{17,1},{25,9},{2,18},{10... | collective-permute-start | bytes 221192 | tf_op jit(solution)/shard_map/ppermute | solution.py:599

commit v4 on v3

--- a/solution.py
+++ b/solution.py
@@ -34,7 +34,7 @@
     return pl.pallas_call(
         body,
         out_shape=[
-            pltpu.HBM(shape, dtype) if n in hbm else jax.ShapeDtypeStruct(shape, dtype)
+            (pltpu.HBM if n in hbm else jax.ShapeDtypeStruct)(shape, dtype)
             for n, (shape, dtype) in enumerate(outs)
         ],
         in_specs=[ANY if n in far_in else VMEM for n in range(len(args))],
@@ -112,15 +112,18 @@
     if ch % 16:
         pieces = [piece.astype(F32)[:ch] for piece in pieces]
     store_halves(out, jnp.concatenate(pieces, axis=0).T.astype(BF))
-    blocks = (x_ref.shape[1] - chp) // 32
     wide = gk_ref.shape[1]
     total = [jnp.zeros((16, LANES), F32) for _ in range(wide // LANES + 2)]
     lane = lax.broadcasted_iota(jnp.int32, (16, LANES), 1)
     for p in range(peers):
+        table = x_ref[p, chp:].astype(F32)
+        pieces = [table[:16] + pltpu.roll(table, 32 - 9, 0)[:16]]
+        if ch > LANES:
+            more = pltpu.roll(table, 32 - 18, 0)[:16]
+            more = more + pltpu.roll(more, 2 * LANES - ch, 1)
+            pieces.append(jnp.where(lane < ch - LANES, more, 0.0))
         first, off = divmod(p * ch, LANES)
-        for b in range(blocks):
-            at = chp + 32 * b
-            piece = x_ref[p, at : at + 16].astype(F32) + x_ref[p, at + 16 : at + 32].astype(F32)
+        for b, piece in enumerate(pieces):
             turned = pltpu.roll(piece, off, 1) if off else piece
             total[first + b] = total[first + b] + jnp.where(lane >= off, turned, 0.0)
             if off:
@@ -267,57 +270,69 @@
             x, y, (((on_x,), (on_y,)), ((), ())), preferred_element_type=F32
         )
 
-    for r in range(ROWS):
-
-        for j in range(cols):
-            tile = r * cols + j
-            span = slice(j * LANES, (j + 1) * LANES)
-            q = spread(q_ref[tile, :chp])
-            g = spread(q_ref[tile, chp : 2 * chp])
-
-            def all_keys(n):
-                above = u_ref[n * cols + j] if r == 0 else a_ref[tile - cols, n]
-                below = d_ref[n * cols + j] if r == ROWS - 1 else a_ref[tile + cols, n]
-                row = [a_ref[r * cols + p, n] for p in range(cols)]
-                return jnp.concatenate(row + [above, below], axis=1)
-
-            k = all_keys(0)
-            v = all_keys(1)
-            live = q_ref[tile, 2 * chp :].astype(F32)
-            zero = jnp.zeros((1, LANES), F32)
-            bias = jnp.concatenate(
-                [live[p : p + 1] for p in range(cols)]
-                + [
-                    live[cols : cols + 1] if r == 0 else zero,
-                    live[cols + 1 : cols + 2] if r == ROWS - 1 else zero,
-                ],
-                axis=1,
-            )
-            s = dot(q, k, 0, 0) + bias
-            top = jnp.max(s, axis=1, keepdims=True)
-            e = jnp.exp2((s - top) * (INV_ROOT * LOG2E))
-            w = e * (1.0 / jnp.sum(e, axis=1, keepdims=True))
-            gw = dot(g, v, 0, 0)
-            delta = jnp.sum(w * gw, axis=1, keepdims=True)
-            gs = (w * (gw - delta)).astype(BF)
-            dk = dot(q, gs, 1, 0)
-            dv = dot(g, w.astype(BF), 1, 0)
-            dq = dot(k, gs, 1, 1)
-            own = dq[:, :LANES]
-            for h in range(1, heads):
-                own = jnp.where(mine[h], dq[:, h * LANES : (h + 1) * LANES], own)
-            dq_ref[tile] = (own * INV_ROOT).astype(BF)
-            dk_ref[r] += dk[:, :wide]
-            dv_ref[r] += dv[:, :wide]
-            for side, at in ((r - 1, wide), (r + 1, wide + LANES)):
-                dk_side, dv_side = dk[:, at : at + LANES], dv[:, at : at + LANES]
-                if 0 <= side < ROWS:
-                    dk_ref[side, :, span] += dk_side
-                    dv_ref[side, :, span] += dv_side
-                else:
-                    out = up_ref if side < 0 else down_ref
-                    out[j] = (dk_side * INV_ROOT).astype(BF)
-                    out[cols + j] = dv_side.astype(BF)
+    def front(tile):
+        r, j = divmod(tile, cols)
+        q = spread(q_ref[tile, :chp])
+        g = spread(q_ref[tile, chp : 2 * chp])
+
+        def all_keys(n):
+            above = u_ref[n * cols + j] if r == 0 else a_ref[tile - cols, n]
+            below = d_ref[n * cols + j] if r == ROWS - 1 else a_ref[tile + cols, n]
+            row = [a_ref[r * cols + p, n] for p in range(cols)]
+            return jnp.concatenate(row + [above, below], axis=1)
+
+        k = all_keys(0)
+        return q, g, k, dot(q, k, 0, 0), dot(g, all_keys(1), 0, 0)
+
+    def middle(tile, s, gw):
+        r = tile // cols
+        live = q_ref[tile, 2 * chp :].astype(F32)
+        zero = jnp.zeros((1, LANES), F32)
+        bias = jnp.concatenate(
+            [live[p : p + 1] for p in range(cols)]
+            + [
+                live[cols : cols + 1] if r == 0 else zero,
+                live[cols + 1 : cols + 2] if r == ROWS - 1 else zero,
+            ],
+            axis=1,
+        )
+        s = s + bias
+        top = jnp.max(s, axis=1, keepdims=True)
+        e = jnp.exp2((s - top) * (INV_ROOT * LOG2E))
+        w = e * (1.0 / jnp.sum(e, axis=1, keepdims=True))
+        delta = jnp.sum(w * gw, axis=1, keepdims=True)
+        return w.astype(BF), (w * (gw - delta)).astype(BF)
+
+    def back(tile, q, g, k, w, gs):
+        r, j = divmod(tile, cols)
+        span = slice(j * LANES, (j + 1) * LANES)
+        dk = dot(q, gs, 1, 0)
+        dv = dot(g, w, 1, 0)
+        dq = dot(k, gs, 1, 1)
+        own = dq[:, :LANES]
+        for h in range(1, heads):
+            own = jnp.where(mine[h], dq[:, h * LANES : (h + 1) * LANES], own)
+        dq_ref[tile] = (own * INV_ROOT).astype(BF)
+        dk_ref[r] += dk[:, :wide]
+        dv_ref[r] += dv[:, :wide]
+        for side, at in ((r - 1, wide), (r + 1, wide + LANES)):
+            dk_side, dv_side = dk[:, at : at + LANES], dv[:, at : at + LANES]
+            if 0 <= side < ROWS:
+                dk_ref[side, :, span] += dk_side
+                dv_ref[side, :, span] += dv_side
+            else:
+                out = up_ref if side < 0 else down_ref
+                out[j] = (dk_side * INV_ROOT).astype(BF)
+                out[cols + j] = dv_side.astype(BF)
+
+    ahead = front(0)
+    for tile in range(peers):
+        q, g, k, s, gw = ahead
+        if tile + 1 < peers:
+            ahead = front(tile + 1)
+        halves = [middle(tile, s[i : i + 64], gw[i : i + 64]) for i in range(0, s.shape[0], 64)]
+        w, gs = (jnp.concatenate(x, axis=0) for x in zip(*halves))
+        back(tile, q, g, k, w, gs)
 
     second = second_rows(chp)
     for out, row, want in ((up_ref, 0, 0), (down_ref, ROWS - 1, 1)):
@@ -372,26 +387,29 @@
             out = jnp.where(lane == t, jnp.sum(acc[t], axis=1, keepdims=True), out)
         sums[at, :] = out
 
-    turned = sums[...].T[:16]
-    blocks = rows.shape[1] // 32
-    if blocks * LANES > chp:
-        turned = jnp.concatenate([turned, jnp.zeros((16, blocks * LANES - chp), F32)], axis=1)
-    lane = lax.broadcasted_iota(jnp.int32, turned.shape, 1)
-    turned = jnp.where(lane < ch, turned, 0.0)
-    high = turned.astype(BF)
-    low = (turned - high.astype(F32)).astype(BF)
+    def split(x):
+        high = x.astype(BF).astype(F32)
+        return high, x - high
+
+    high, low = split(sums[: min(chp, LANES)])
+    table = high + pltpu.roll(low, 9, 1)
+    if chp < LANES:
+        table = jnp.concatenate([table, jnp.zeros((LANES - chp, LANES), F32)], axis=0)
+    if chp > LANES:
+        more = jnp.concatenate(split(sums[LANES:]), axis=0)
+        more = jnp.concatenate([more, jnp.zeros((LANES - more.shape[0], LANES), F32)], axis=0)
+        table = table + pltpu.roll(more, 18, 1)
+    table = table.T[:32].astype(BF)
     for tile in range(rows.shape[0]):
-        for b in range(blocks):
-            rows[tile, 32 * b : 32 * b + 16] = high[:, b * LANES : (b + 1) * LANES]
-            rows[tile, 32 * b + 16 : 32 * b + 32] = low[:, b * LANES : (b + 1) * LANES]
-    sums_out = pltpu.make_async_copy(rows, out_ref.at[:, pl.ds(chp, 32 * blocks)], sems.at[3])
+        rows[tile] = table
+    sums_out = pltpu.make_async_copy(rows, out_ref.at[:, pl.ds(chp, 32)], sems.at[3])
     sums_out.start()
     for copy in copies + [sums_out]:
         copy.wait()
 
 
 def finish_body(
-    dk_hbm, dv_hbm, up_ref, down_ref, u_ref, d_ref, kc_ref, out_ref, dk_ref, dv_ref, held, sems
+    dk_hbm, dv_hbm, up_ref, down_ref, d_ref, u_ref, kc_ref, out_ref, dk_ref, dv_ref, held, sems
 ):
     cols = held.shape[0] // ROWS
     chp = held.shape[2]
@@ -554,15 +572,14 @@
     from_above = lax.ppermute(to_down, "z", down_pairs)
     from_below = lax.ppermute(to_up, "z", up_pairs)
 
-    blocks = -(-ch // LANES)
     own = ((ROWS, chp, wide), F32)
     sent_dq, dk, dv = call(
         functools.partial(kernel_grad_body, ch),
-        [((peers, chp + 32 * blocks, LANES), BF), own, own],
+        [((peers, chp + 32, LANES), BF), own, own],
         dq, mine, above, below, dk, dv, to_up, to_down,
         scratch=[
             pltpu.VMEM((chp, LANES), F32),
-            pltpu.VMEM((peers, 32 * blocks, LANES), BF),
+            pltpu.VMEM((peers, 32, LANES), BF),
             pltpu.SemaphoreType.DMA((4,)),
         ],
         far_out=(0, 1, 2),
@@ -574,7 +591,7 @@
     (results,) = call(
         finish_body, [tiles(peers, 3)],
         *[pltpu.with_memory_space_constraint(x, pltpu.HBM) for x in (dk, dv)],
-        to_up, to_down, from_above, from_below, coefs,
+        to_up, to_down, from_below, from_above, coefs,
         scratch=[
             pltpu.VMEM((ROWS, chp, wide), F32),
             pltpu.VMEM((ROWS, chp, wide), F32),

time: 89.1 us -> 86.5 us (0.971)
  Pallas kernels: 26.3 us -> 24.5 us
    pallas_call x11, Pallas kernels: 26.3 us -> 24.5 us  [call(): pl.pallas_call(body, out_shape=[(pltpu.HBM if n in hbm else jax.ShapeDtyp...]
  transfers between devices with their start and end apart: 10 -> 10, of which waited for: 7 -> 6; matrix products, arithmetic and copies ran while one was open for 2% -> 2% of each run, Pallas kernels for 18% -> 18%
where the time goes in v4:
time: 86.5 us; the launch traced here: 85.8 us
  starting transfers between devices  30.7 us (35%)
  waiting for transfers between devices  28.1 us (32%)
  Pallas kernels  24.5 us (28%)
  local copies, waits for them, and re-layouts  0.91 us (1%)
    pallas_call x11, Pallas kernels, call(): pl.pallas_call(body, out_shape=[(pltpu.HBM if n in hbm else jax.ShapeDtyp...  24.5 us
    all_to_all x4, starting transfers between devices, swap(): return lax.all_to_all(x.reshape(peers, -1, LANES), plane, 0, 0, tiled=True)  15.7 us
    all_to_all x4, waiting for transfers between devices, swap(): return lax.all_to_all(x.reshape(peers, -1, LANES), plane, 0, 0, tiled=True)  10.7 us
    ppermute x2, waiting for transfers between devices, per_device(): other = lax.ppermute(taps_sum, 'z', [(i, i ^ step) for i in range(planes)])  7.57 us
    ppermute x1, waiting for transfers between devices, per_device(): above = lax.ppermute(to_down, 'z', down_pairs)  5.81 us
    ppermute x1, starting transfers between devices, per_device(): from_above = lax.ppermute(to_down, 'z', down_pairs)  5.32 us
    ppermute x1, waiting for transfers between devices, per_device(): below = lax.ppermute(to_up, 'z', up_pairs)  3.97 us
    ppermute x1, starting transfers between devices, per_device(): above = lax.ppermute(to_down, 'z', down_pairs)  3.5 us
  transfers between devices with their start and end apart: 10, of which 6 were waited for; matrix products, arithmetic and copies ran while one was open for 2% of the time, Pallas kernels for 18%

profile of v4, /device:TPU:0, one launch (start us, length us, event | category | flops | bytes accessed | tf_op | source)
XLA Modules:
  0.0 85.8 jit_solution(15076571244015063671)
XLA Ops:
  0.6 2.2 %shard_map.110 = bf16[8,432,128]{2,1,0:T(8,128)(2,1)} custom-call(bf16[128,1152]{1,0:T(8,128)(2,1)} %bitcast.20, bf16[128,1152]{1,0:T(8,128)(2,1)} %bitcast.21, bf16[128,1152]{1,0:T(8,128)(2,1)} %bitcast.22), custom_call_target="tpu_custom_call" | custom-call | bytes 1769472 | tf_op jit(solution)/shard_map/pallas_call | solution.py:34
  2.9 5.2 %all-to-all-start = ((bf16[8,432,128]{2,1,0:T(8,128)(2,1)}), bf16[8,432,128]{2,1,0:T(8,128)(2,1)S(1)}, u32[]{:S(2)}, u32[]{:S(2)}) async-start(bf16[8,432,128]{2,1,0:T(8,128)(2,1)} %shard_map.110), calls=%async_computation | async-start | bytes 1769472 | tf_op jit(solution)/shard_map/all_to_all | solution.py:505
  8.1 0.7 bitcast_or_fusion
  8.7 0.1 pad_add_fusion
  8.8 0.7 broadcast_in_dim.16.refs_2_
  9.5 2.7 %shard_map.111 = bf16[8,304,128]{2,1,0:T(8,128)(2,1)} custom-call(bf16[128,1152]{1,0:T(8,128)(2,1)} %bitcast.24, bf16[128,1152]{1,0:T(8,128)(2,1)} %bitcast.25, f32[16,128]{1,0:T(8,128)} %broadcast_in_dim.16.refs_2_), custom_call_target="tpu_custom_call" | custom-call | bytes 1220608 | tf_op jit(solution)/shard_map/pallas_call | solution.py:34
  12.3 8.5 %all-to-all-done = bf16[8,432,128]{2,1,0:T(8,128)(2,1)S(1)} async-done(((bf16[8,432,128]{2,1,0:T(8,128)(2,1)}), bf16[8,432,128]{2,1,0:T(8,128)(2,1)S(1)}, u32[]{:S(2)}, u32[]{:S(2)}) %all-to-all-start) | async-done | bytes 884768 | tf_op jit(solution)/shard_map/all_to_all | solution.py:505
  20.8 0.9 %shard_map.112 = (bf16[14,144,128]{2,1,0:T(8,128)(2,1)S(1)}, bf16[14,144,128]{2,1,0:T(8,128)(2,1)}) custom-call(bf16[8,3,144,128]{3,2,1,0:T(8,128)(2,1)S(1)} %bitcast.17), custom_call_target="tpu_custom_call" | custom-call | bytes 1916928 | tf_op jit(solution)/shard_map/pallas_call | solution.py:34
  21.6 3.5 %collective-permute-start = (bf16[14,144,128]{2,1,0:T(8,128)(2,1)}, bf16[14,144,128]{2,1,0:T(8,128)(2,1)S(1)}, u32[]{:S(2)}, u32[]{:S(2)}) collective-permute-start(bf16[14,144,128]{2,1,0:T(8,128)(2,1)} %get-tuple-element.27), channel_id=1, source_target_pairs={{0,8},{8,16},{16,24},{1,9},{9,17},{17,25},{2,10},{10,18},{18,26},{... | collective-permute-start | bytes 1548296 | tf_op jit(solution)/shard_map/ppermute | solution.py:539
  25.1 0.0 copy-start
  25.1 1.4 %collective-permute-start.1 = (bf16[14,144,128]{2,1,0:T(8,128)(2,1)S(1)}, bf16[14,144,128]{2,1,0:T(8,128)(2,1)S(1)}, u32[]{:S(2)}, u32[]{:S(2)}) collective-permute-start(bf16[14,144,128]{2,1,0:T(8,128)(2,1)S(1)} %get-tuple-element.28), channel_id=1, source_target_pairs={{8,0},{16,8},{24,16},{9,1},{17,9},{25,17},{10,2},{18,10},{26,18},{... | collective-permute-start | bytes 1548296 | tf_op jit(solution)/shard_map/ppermute | solution.py:538
  26.6 3.6 %all-to-all-start.1 = ((bf16[8,304,128]{2,1,0:T(8,128)(2,1)}), bf16[8,304,128]{2,1,0:T(8,128)(2,1)S(1)}, u32[]{:S(2)}, u32[]{:S(2)}) async-start(bf16[8,304,128]{2,1,0:T(8,128)(2,1)} %shard_map.111), calls=%async_computation.1 | async-start | bytes 1245184 | tf_op jit(solution)/shard_map/all_to_all | solution.py:505
  30.1 0.0 copy-done
  30.2 0.1 constant_dynamic-slice_fusion
  30.3 0.1 copy.17
  30.4 5.8 %collective-permute-done.u_ref = bf16[14,144,128]{2,1,0:T(8,128)(2,1)S(1)} collective-permute-done((bf16[14,144,128]{2,1,0:T(8,128)(2,1)}, bf16[14,144,128]{2,1,0:T(8,128)(2,1)S(1)}, u32[]{:S(2)}, u32[]{:S(2)}) %collective-permute-start) | collective-permute-done | bytes 516128 | tf_op jit(solution)/shard_map/ppermute | solution.py:539
  36.2 4.0 %collective-permute-done.1.d_ref = bf16[14,144,128]{2,1,0:T(8,128)(2,1)S(1)} collective-permute-done((bf16[14,144,128]{2,1,0:T(8,128)(2,1)S(1)}, bf16[14,144,128]{2,1,0:T(8,128)(2,1)S(1)}, u32[]{:S(2)}, u32[]{:S(2)}) %collective-permute-start.1) | collective-permute-done | bytes 516128 | tf_op jit(solution)/shard_map/ppermute | solution.py:538
  40.2 3.3 %shard_map.113 = (bf16[8,3,144,128]{3,2,1,0:T(8,128)(2,1)S(1)}, bf16[14,144,128]{2,1,0:T(8,128)(2,1)S(1)}, bf16[14,144,128]{2,1,0:T(8,128)(2,1)S(1)}) custom-call(bf16[8,3,144,128]{3,2,1,0:T(8,128)(2,1)S(1)} %bitcast.18, bf16[14,144,128]{2,1,0:T(8,128)(2,1)S(1)} %collective-permute-done.u_ref, ...), custom_call_target="tpu_custom_call", output_to_operand_aliasing={{0}: (0, {}), {1}: (1, {}), {2}: (2, {})} | custom-call | flops 4000000000 | bytes 3907584 | tf_op jit(solution)/shard_map/pallas_call | solution.py:34
  43.5 0.0 all-to-all-done.1.q_ref
  43.5 4.7 %shard_map.114 = (bf16[8,144,128]{2,1,0:T(8,128)(2,1)S(1)}, bf16[10,144,128]{2,1,0:T(8,128)(2,1)S(1)}, bf16[10,144,128]{2,1,0:T(8,128)(2,1)S(1)}, f32[2,144,512]{2,1,0:T(8,128)S(1)}, f32[2,144,512]{2,1,0:T(8,128)S(1)}) custom-call(bf16[8,304,128]{2,1,0:T(8,128)(2,1)S(1)} %all-to-all-done.1.q_ref, bf16[8,3,144,128]{3,2,1,0:T(8,128)(2,1)S(1)} %get-tuple-element.29.a_ref, ...), custom_call_target="tpu_custom_call" | custom-call | flops 4026531840 | bytes 4751360 | tf_op jit(solution)/shard_map/pallas_call | solution.py:34
  48.2 1.3 %collective-permute-start.2 = (bf16[10,144,128]{2,1,0:T(8,128)(2,1)S(1)}, bf16[10,144,128]{2,1,0:T(8,128)(2,1)}, u32[]{:S(2)}, u32[]{:S(2)}) collective-permute-start(bf16[10,144,128]{2,1,0:T(8,128)(2,1)S(1)} %get-tuple-element.35.up_ref), channel_id=1, source_target_pairs={{8,0},{16,8},{24,16},{9,1},{17,9},{25,17},{10,2},{18,10},{26,18},{... | collective-permute-start | bytes 1105928 | tf_op jit(solution)/shard_map/ppermute | solution.py:573
  49.5 5.3 %collective-permute-start.3 = (bf16[10,144,128]{2,1,0:T(8,128)(2,1)S(1)}, bf16[10,144,128]{2,1,0:T(8,128)(2,1)}, u32[]{:S(2)}, u32[]{:S(2)}) collective-permute-start(bf16[10,144,128]{2,1,0:T(8,128)(2,1)S(1)} %get-tuple-element.36.down_ref), channel_id=1, source_target_pairs={{0,8},{8,16},{16,24},{1,9},{9,17},{17,25},{2,10},{10,18},{18,26},{... | collective-permute-start | bytes 1105928 | tf_op jit(solution)/shard_map/ppermute | solution.py:572
  54.8 3.2 %shard_map.115 = (bf16[8,176,128]{2,1,0:T(8,128)(2,1)}, f32[2,144,512]{2,1,0:T(8,128)}, f32[2,144,512]{2,1,0:T(8,128)}) custom-call(bf16[8,144,128]{2,1,0:T(8,128)(2,1)S(1)} %get-tuple-element.32.dq_ref, bf16[8,3,144,128]{3,2,1,0:T(8,128)(2,1)S(1)} %get-tuple-element.29.a_ref, bf16[14,144,128]{2,1,0:T(8,128)(2,1)S(1)} %get-tuple-element.30.u_ref, ...), custom_call_target="tpu_custom_call" | custom-call | flops 4000000000 | bytes 5668864 | tf_op jit(solution)/shard_map/pallas_call | solution.py:34
  58.0 3.5 %all-to-all-start.2 = ((bf16[8,176,128]{2,1,0:T(8,128)(2,1)}), bf16[8,176,128]{2,1,0:T(8,128)(2,1)S(1)}, u32[]{:S(2)}, u32[]{:S(2)}) async-start(bf16[8,176,128]{2,1,0:T(8,128)(2,1)} %get-tuple-element.37), calls=%async_computation.2 | async-start | bytes 720896 | tf_op jit(solution)/shard_map/all_to_all | solution.py:505
  61.5 0.0 collective-permute-done.2.d_ref
  61.5 0.0 collective-permute-done.3.u_ref
  61.5 4.9 %shard_map.117 = bf16[8,3,144,128]{3,2,1,0:T(8,128)(2,1)} custom-call(f32[2,144,512]{2,1,0:T(8,128)} %get-tuple-element.39.dk_hbm, f32[2,144,512]{2,1,0:T(8,128)} %get-tuple-element.40.dv_hbm, bf16[10,144,128]{2,1,0:T(8,128)(2,1)S(1)} %get-tuple-element.35.up_ref, bf16[10,144,128]{2,1,0:T(8,128)(2,1)S(1)} %get-tuple-element.36.down_ref, ...), custom_call_target="tpu_custom_call" | custom-call | flops 4000000000 | bytes 3612672 | tf_op jit(solution)/shard_map/pallas_call | solution.py:34
  66.4 2.2 %all-to-all-done.2.x_ref = bf16[8,176,128]{2,1,0:T(8,128)(2,1)S(1)} async-done(((bf16[8,176,128]{2,1,0:T(8,128)(2,1)}), bf16[8,176,128]{2,1,0:T(8,128)(2,1)S(1)}, u32[]{:S(2)}, u32[]{:S(2)}) %all-to-all-start.2) | async-done | bytes 360480 | tf_op jit(solution)/shard_map/all_to_all | solution.py:505
  68.5 3.6 %all-to-all-start.3 = ((bf16[8,432,128]{2,1,0:T(8,128)(2,1)}), bf16[8,432,128]{2,1,0:T(8,128)(2,1)S(1)}, u32[]{:S(2)}, u32[]{:S(2)}) async-start(bf16[8,432,128]{2,1,0:T(8,128)(2,1)} %bitcast.11), calls=%async_computation.3 | async-start | bytes 1769472 | tf_op jit(solution)/shard_map/all_to_all | solution.py:505
  72.1 1.0 %shard_map.116 = (bf16[128,1152]{1,0:T(8,128)(2,1)}, f32[16,1152]{1,0:T(8,128)S(1)}) custom-call(bf16[8,176,128]{2,1,0:T(8,128)(2,1)S(1)} %all-to-all-done.2.x_ref), custom_call_target="tpu_custom_call" | custom-call | bytes 729088 | tf_op jit(solution)/shard_map/pallas_call | solution.py:34
  73.1 0.8 collective-permute-start.4
  73.9 3.8 %collective-permute-done.4.y_ref = f32[16,1152]{1,0:T(8,128)S(1)} collective-permute-done((f32[16,1152]{1,0:T(8,128)S(1)}, f32[16,1152]{1,0:T(8,128)S(1)}, u32[]{:S(2)}, u32[]{:S(2)}) %collective-permute-start.4) | collective-permute-done | bytes 73760 | tf_op jit(solution)/shard_map/ppermute | solution.py:613
  77.7 2.6 %collective-permute-start.5 = (f32[16,1152]{1,0:T(8,128)S(1)}, f32[16,1152]{1,0:T(8,128)S(1)}, u32[]{:S(2)}, u32[]{:S(2)}) collective-permute-start(f32[16,1152]{1,0:T(8,128)S(1)} %shard_map.119.x_ref), channel_id=1, source_target_pairs={{0,16},{8,24},{16,0},{24,8},{1,17},{9,25},{17,1},{25,9},{2,18},{10... | collective-permute-start | bytes 221192 | tf_op jit(solution)/shard_map/ppermute | solution.py:616
  80.3 3.8 %collective-permute-done.5.y_ref = f32[16,1152]{1,0:T(8,128)S(1)} collective-permute-done((f32[16,1152]{1,0:T(8,128)S(1)}, f32[16,1152]{1,0:T(8,128)S(1)}, u32[]{:S(2)}, u32[]{:S(2)}) %collective-permute-start.5) | collective-permute-done | bytes 73760 | tf_op jit(solution)/shard_map/ppermute | solution.py:616
  84.0 0.6 shard_map.120
  84.7 0.0 all-to-all-done.3
  84.7 1.0 %shard_map.118 = (bf16[128,1152]{1,0:T(8,128)(2,1)}, bf16[128,1152]{1,0:T(8,128)(2,1)}, bf16[128,1152]{1,0:T(8,128)(2,1)}) custom-call(bf16[8,3,144,128]{3,2,1,0:T(8,128)(2,1)S(1)} %bitcast.19), custom_call_target="tpu_custom_call" | custom-call | bytes 1769472 | tf_op jit(solution)/shard_map/pallas_call | solution.py:34
  (4 shorter events, 0.0 us)
Async XLA Ops:
  2.9 17.9 %all-to-all-start = ((bf16[8,432,128]{2,1,0:T(8,128)(2,1)}), bf16[8,432,128]{2,1,0:T(8,128)(2,1)S(1)}, u32[]{:S(2)}, u32[]{:S(2)}) async-start(bf16[8,432,128]{2,1,0:T(8,128)(2,1)} %shard_map.110), calls=%async_computation | async-start | bytes 1769472 | tf_op jit(solution)/shard_map/all_to_all | solution.py:505
  21.6 14.6 %collective-permute-start = (bf16[14,144,128]{2,1,0:T(8,128)(2,1)}, bf16[14,144,128]{2,1,0:T(8,128)(2,1)S(1)}, u32[]{:S(2)}, u32[]{:S(2)}) collective-permute-start(bf16[14,144,128]{2,1,0:T(8,128)(2,1)} %get-tuple-element.27), channel_id=1, source_target_pairs={{0,8},{8,16},{16,24},{1,9},{9,17},{17,25},{2,10},{10,18},{18,26},{... | collective-permute-start | bytes 1548296 | tf_op jit(solution)/shard_map/ppermute | solution.py:539
  25.1 5.0 %copy-start = (f32[3,3,1152]{2,1,0:T(4,128)S(1)}, f32[3,3,1152]{2,1,0:T(4,128)}, u32[]{:S(2)}) copy-start(f32[3,3,1152]{2,1,0:T(4,128)} %param.11) | copy-start | bytes 124420
  25.1 15.0 %collective-permute-start.1 = (bf16[14,144,128]{2,1,0:T(8,128)(2,1)S(1)}, bf16[14,144,128]{2,1,0:T(8,128)(2,1)S(1)}, u32[]{:S(2)}, u32[]{:S(2)}) collective-permute-start(bf16[14,144,128]{2,1,0:T(8,128)(2,1)S(1)} %get-tuple-element.28), channel_id=1, source_target_pairs={{8,0},{16,8},{24,16},{9,1},{17,9},{25,17},{10,2},{18,10},{26,18},{... | collective-permute-start | bytes 1548296 | tf_op jit(solution)/shard_map/ppermute | solution.py:538
  26.6 16.9 %all-to-all-start.1 = ((bf16[8,304,128]{2,1,0:T(8,128)(2,1)}), bf16[8,304,128]{2,1,0:T(8,128)(2,1)S(1)}, u32[]{:S(2)}, u32[]{:S(2)}) async-start(bf16[8,304,128]{2,1,0:T(8,128)(2,1)} %shard_map.111), calls=%async_computation.1 | async-start | bytes 1245184 | tf_op jit(solution)/shard_map/all_to_all | solution.py:505
  48.2 13.2 %collective-permute-start.2 = (bf16[10,144,128]{2,1,0:T(8,128)(2,1)S(1)}, bf16[10,144,128]{2,1,0:T(8,128)(2,1)}, u32[]{:S(2)}, u32[]{:S(2)}) collective-permute-start(bf16[10,144,128]{2,1,0:T(8,128)(2,1)S(1)} %get-tuple-element.35.up_ref), channel_id=1, source_target_pairs={{8,0},{16,8},{24,16},{9,1},{17,9},{25,17},{10,2},{18,10},{26,18},{... | collective-permute-start | bytes 1105928 | tf_op jit(solution)/shard_map/ppermute | solution.py:573
  49.5 12.0 %collective-permute-start.3 = (bf16[10,144,128]{2,1,0:T(8,128)(2,1)S(1)}, bf16[10,144,128]{2,1,0:T(8,128)(2,1)}, u32[]{:S(2)}, u32[]{:S(2)}) collective-permute-start(bf16[10,144,128]{2,1,0:T(8,128)(2,1)S(1)} %get-tuple-element.36.down_ref), channel_id=1, source_target_pairs={{0,8},{8,16},{16,24},{1,9},{9,17},{17,25},{2,10},{10,18},{18,26},{... | collective-permute-start | bytes 1105928 | tf_op jit(solution)/shard_map/ppermute | solution.py:572
  58.0 10.5 %all-to-all-start.2 = ((bf16[8,176,128]{2,1,0:T(8,128)(2,1)}), bf16[8,176,128]{2,1,0:T(8,128)(2,1)S(1)}, u32[]{:S(2)}, u32[]{:S(2)}) async-start(bf16[8,176,128]{2,1,0:T(8,128)(2,1)} %get-tuple-element.37), calls=%async_computation.2 | async-start | bytes 720896 | tf_op jit(solution)/shard_map/all_to_all | solution.py:505
  68.5 16.2 %all-to-all-start.3 = ((bf16[8,432,128]{2,1,0:T(8,128)(2,1)}), bf16[8,432,128]{2,1,0:T(8,128)(2,1)S(1)}, u32[]{:S(2)}, u32[]{:S(2)}) async-start(bf16[8,432,128]{2,1,0:T(8,128)(2,1)} %bitcast.11), calls=%async_computation.3 | async-start | bytes 1769472 | tf_op jit(solution)/shard_map/all_to_all | solution.py:505
  73.1 4.6 %collective-permute-start.4 = (f32[16,1152]{1,0:T(8,128)S(1)}, f32[16,1152]{1,0:T(8,128)S(1)}, u32[]{:S(2)}, u32[]{:S(2)}) collective-permute-start(f32[16,1152]{1,0:T(8,128)S(1)} %get-tuple-element.44.x_ref), channel_id=1, source_target_pairs={{0,8},{8,0},{16,24},{24,16},{1,9},{9,1},{17,25},{25,17},{2,10},{10... | collective-permute-start | bytes 221192 | tf_op jit(solution)/shard_map/ppermute | solution.py:613
  77.7 6.4 %collective-permute-start.5 = (f32[16,1152]{1,0:T(8,128)S(1)}, f32[16,1152]{1,0:T(8,128)S(1)}, u32[]{:S(2)}, u32[]{:S(2)}) collective-permute-start(f32[16,1152]{1,0:T(8,128)S(1)} %shard_map.119.x_ref), channel_id=1, source_target_pairs={{0,16},{8,24},{16,0},{24,8},{1,17},{9,25},{17,1},{25,9},{2,18},{10... | collective-permute-start | bytes 221192 | tf_op jit(solution)/shard_map/ppermute | solution.py:616

commit v5 on v4

--- a/solution.py
+++ b/solution.py
@@ -44,6 +44,24 @@
         compiler_params=params(mib),
         cost_estimate=pl.CostEstimate(flops=flops, bytes_accessed=moved, transcendentals=0),
     )(*args)
+
+
+def facing(body, *places):
+    def kernel(*refs):
+        odd = lax.rem(lax.axis_index("z"), 2)
+        turned = list(refs)
+        for place in places:
+            turned[place], turned[place + 1] = refs[place + 1], refs[place]
+
+        @pl.when(odd == 1)
+        def _():
+            body(*refs)
+
+        @pl.when(odd == 0)
+        def _():
+            body(*turned)
+
+    return kernel
 
 
 def my_halves():
@@ -168,34 +186,41 @@
     return out
 
 
-def conv_rows(rows, coef, masks):
+def merge(tiles_second, tiles_first, masks):
     second = masks[0]
-    count = len(rows)
-    out = []
-    last = None
-    for i in range(count):
-        here = []
-        for j, t in enumerate(col_shifts(rows[i], masks)):
-            use = [i < count - 1, 0 < i < count - 1, i > 0]
-            here.append(
-                [
-                    coef[3 * a] * t[0] + coef[3 * a + 1] * t[1] + coef[3 * a + 2] * t[2] if use[a] else None
-                    for a in range(3)
-                ]
-            )
-        if i >= 2:
-            out.append(
-                [
-                    m + pltpu.roll(u + jnp.where(second[j % 2], d, n[2]), HALF, 1)
-                    for j, ((m, u, d), n) in enumerate(zip(last, here))
-                ]
-            )
-        if 0 < i < count - 1:
-            last = [
-                (n[1], jnp.where(second[j % 2], p, n[0]), n[2])
-                for j, (p, n) in enumerate(zip(before, here))
-            ]
-        before = [n[0] for n in here]
+    return [
+        jnp.where(second[j % 2], x, y) for j, (x, y) in enumerate(zip(tiles_second, tiles_first))
+    ]
+
+
+def row_terms(tiles, coef, masks):
+    return [
+        [sum(coef[3 * a + b] * t[b] for b in range(3)) for a in range(3)]
+        for t in col_shifts(tiles, masks)
+    ]
+
+
+def edge_terms(tiles, coef, masks):
+    second = masks[0]
+    mixed = [[jnp.where(second[p], coef[b], coef[6 + b]) for b in range(3)] for p in range(2)]
+    return [
+        sum(mixed[j % 2][b] * t[b] for b in range(3))
+        for j, t in enumerate(col_shifts(tiles, masks))
+    ]
+
+
+def turn(x):
+    return pltpu.roll(x, HALF, 1)
+
+
+def conv_pair(first, last, edge, coef, masks):
+    second = masks[0]
+    top, bottom = row_terms(first, coef, masks), row_terms(last, coef, masks)
+    out = ([], [])
+    for j, ((tu, tm, td), (bu, bm, bd)) in enumerate(zip(top, bottom)):
+        e = edge[j] if edge else 0.0
+        out[0].append(tm + turn(jnp.where(second[j % 2], e + td, tu + bd)))
+        out[1].append(bm + turn(jnp.where(second[j % 2], tu + bd, bu + e)))
     return out
 
 
@@ -216,37 +241,77 @@
             out[3 * cols + m // 2] = jnp.where(second[want], odd, even).astype(BF)
 
 
-def control_rows(a_ref, u_ref, d_ref, at):
+def outer_controls(u_ref, d_ref, at, masks):
+    half = u_ref.shape[0] * 2 // 7
+    above, below = (
+        [ref[3 * half + j // 2, at, :].astype(F32) for j in range(half)] for ref in (u_ref, d_ref)
+    )
+    return merge(above, below, masks)
+
+
+def load(ref, first, count, at):
+    return [ref[first + j, at, :].astype(F32) for j in range(count)]
+
+
+def load_own(a_ref, r, n, at):
     cols = a_ref.shape[0] // ROWS
-    rows = [
-        [u_ref[3 * cols + j // 2, at, :] for j in range(cols)],
-        [u_ref[2 * cols + j, at, :] for j in range(cols)],
-        *[[a_ref[r * cols + j, 2, at, :] for j in range(cols)] for r in range(ROWS)],
-        [d_ref[2 * cols + j, at, :] for j in range(cols)],
-        [d_ref[3 * cols + j // 2, at, :] for j in range(cols)],
-    ]
-    return [[x.astype(F32) for x in row] for row in rows]
-
-
-def values_body(a_ref, u_ref, d_ref, kc_ref, a_out, u_out, d_out):
+    return [a_ref[r * cols + j, n, at, :].astype(F32) for j in range(cols)]
+
+
+def own_values_body(a_ref, kc_ref, a_out, part_ref):
     cols = a_ref.shape[0] // ROWS
-    chp = a_ref.shape[2]
-
-    @pl.loop(0, chp // 16)
+
+    @pl.loop(0, a_ref.shape[2] // 16)
     def _(step):
         at = pl.ds(pl.multiple_of(step * 16, 16), 16)
-        conv = conv_rows(control_rows(a_ref, u_ref, d_ref, at), taps(kc_ref, at), lane_masks(16))
+        masks = lane_masks(16)
+        second = masks[0]
+        conv = conv_pair(
+            load_own(a_ref, 0, 2, at), load_own(a_ref, 1, 2, at), None, taps(kc_ref, at), masks
+        )
+        for j in range(cols):
+            part_ref[j, at, :] = jnp.where(second[j % 2], conv[1][j], conv[0][j])
+            for r in range(ROWS):
+                tile = r * cols + j
+                value = a_ref[tile, 1, at, :].astype(F32)
+                inner = second[j % 2] if r == 0 else second[1 - j % 2]
+                a_out[tile, 0, at, :] = a_ref[tile, 0, at, :]
+                a_out[tile, 1, at, :] = jnp.where(inner, value + conv[r][j], value).astype(BF)
+                a_out[tile, 2, at, :] = a_ref[tile, 2, at, :]
+
+
+def values_body(a_ref, u_ref, d_ref, part_ref, kc_ref, a_out, u_out, d_out):
+    cols = a_ref.shape[0] // ROWS
+
+    @pl.loop(0, a_ref.shape[2] // 16)
+    def _(step):
+        at = pl.ds(pl.multiple_of(step * 16, 16), 16)
+        masks = lane_masks(16)
+        second = masks[0]
+        coef = taps(kc_ref, at)
+        far = edge_terms(outer_controls(u_ref, d_ref, at, masks), coef, masks)
+        own = merge(load_own(a_ref, ROWS - 1, 2, at), load_own(a_ref, 0, 2, at), masks)
+        own = edge_terms(own, coef, masks)
+        above = row_terms(load(u_ref, 2 * cols, cols, at), coef, masks)
+        below = row_terms(load(d_ref, 2 * cols, cols, at), coef, masks)
         for ref, out in ((u_ref, u_out), (d_ref, d_out)):
             for n in range(ref.shape[0]):
                 if not cols <= n < 2 * cols:
                     out[n, at, :] = ref[n, at, :]
         for j in range(cols):
-            for ref, out, i in ((u_ref, u_out, 0), (d_ref, d_out, -1)):
-                out[cols + j, at, :] = (ref[cols + j, at, :].astype(F32) + conv[i][j]).astype(BF)
+            (uu, um, ud), (du, dm, dd) = above[j], below[j]
+            pick = second[j % 2]
+            u_conv = um + turn(jnp.where(pick, far[j] + ud, uu + own[j]))
+            d_conv = dm + turn(jnp.where(pick, own[j] + dd, du + far[j]))
+            rim = part_ref[j, at, :] + turn(jnp.where(pick, uu, dd))
+            u_out[cols + j, at, :] = (u_ref[cols + j, at, :].astype(F32) + u_conv).astype(BF)
+            d_out[cols + j, at, :] = (d_ref[cols + j, at, :].astype(F32) + d_conv).astype(BF)
             for r in range(ROWS):
                 tile = r * cols + j
+                value = a_ref[tile, 1, at, :].astype(F32)
+                inner = pick if r == 0 else second[1 - j % 2]
                 a_out[tile, 0, at, :] = a_ref[tile, 0, at, :]
-                a_out[tile, 1, at, :] = (a_ref[tile, 1, at, :].astype(F32) + conv[r + 1][j]).astype(BF)
+                a_out[tile, 1, at, :] = jnp.where(inner, value, value + rim).astype(BF)
                 a_out[tile, 2, at, :] = a_ref[tile, 2, at, :]
 
 
@@ -369,17 +434,22 @@
         masks = lane_masks(16)
         second = masks[0]
         acc = [jnp.zeros((16, LANES), F32) for _ in range(9)]
-        above = here = None
-        for i, row in enumerate(control_rows(a_ref, u_ref, d_ref, at)):
-            below = col_shifts(row, masks)
-            if i >= 2:
-                for j in range(cols):
-                    g = value_terms(dv_ref, up_ref, down_ref, i - 2, j, at)
-                    turned = pltpu.roll(g, HALF, 1)
-                    for b in range(3):
-                        acc[b] += jnp.where(second[j % 2], above[j][b], here[j][b]) * turned
-                        acc[3 + b] += here[j][b] * g
-                        acc[6 + b] += jnp.where(second[j % 2], here[j][b], below[j][b]) * turned
+        outer = col_shifts(outer_controls(u_ref, d_ref, at, masks), masks)
+        above, here = outer, col_shifts(load(u_ref, 2 * cols, cols, at), masks)
+        for i in range(ROWS + 2):
+            if i < ROWS:
+                below = col_shifts(load_own(a_ref, i, 2, at), masks)
+            elif i == ROWS:
+                below = col_shifts(load(d_ref, 2 * cols, cols, at), masks)
+            else:
+                below = outer
+            for j in range(cols):
+                g = value_terms(dv_ref, up_ref, down_ref, i, j, at)
+                turned = turn(g)
+                for b in range(3):
+                    acc[b] += jnp.where(second[j % 2], above[j][b], here[j][b]) * turned
+                    acc[3 + b] += here[j][b] * g
+                    acc[6 + b] += jnp.where(second[j % 2], here[j][b], below[j][b]) * turned
             above, here = here, below
         lane = lax.broadcasted_iota(jnp.int32, (16, LANES), 1)
         out = jnp.zeros((16, LANES), F32)
@@ -409,7 +479,7 @@
 
 
 def finish_body(
-    dk_hbm, dv_hbm, up_ref, down_ref, d_ref, u_ref, kc_ref, out_ref, dk_ref, dv_ref, held, sems
+    dk_hbm, dv_hbm, up_ref, down_ref, u_ref, d_ref, kc_ref, out_ref, dk_ref, dv_ref, held, sems
 ):
     cols = held.shape[0] // ROWS
     chp = held.shape[2]
@@ -465,7 +535,8 @@
                         x = x + from_side(d_ref, cols + j)
                 row.append(rounded(x))
             rows.append(row)
-        conv = conv_rows(rows, coef, masks)
+        edge = edge_terms(merge(rows[0], rows[-1], masks), coef, masks)
+        conv = conv_pair(rows[1], rows[2], edge, coef, masks)
         for r in range(ROWS):
             for j in range(cols):
                 tile = r * cols + j
@@ -531,12 +602,16 @@
     live = jnp.broadcast_to(live[:, None], (16, LANES))
     sent_q = pack([query, grad_out], live)
     mine, sent_q = lax.optimization_barrier((mine, sent_q))
-    down_pairs = [(i, i + 1) for i in range(planes - 1)]
-    up_pairs = [(i + 1, i) for i in range(planes - 1)]
+    rounds = [
+        [pair for i in range(start, planes - 1, 2) for pair in ((i, i + 1), (i + 1, i))]
+        for start in range(2)
+    ]
+
+    def exchange(messages):
+        return [lax.ppermute(x, "z", pairs) for x, pairs in zip(messages, rounds)]
+
     rim = (3 * cols + cols // 2, chp, LANES)
-    to_up, to_down = call(rim_body, [(rim, BF)] * 2, mine)
-    below = lax.ppermute(to_up, "z", up_pairs)
-    above = lax.ppermute(to_down, "z", down_pairs)
+    sides = exchange(call(facing(rim_body, 1), [(rim, BF)] * 2, mine))
 
     coefs = lax.dynamic_slice_in_dim(kernel.reshape(9, channels), me * ch, ch, 1)
     coefs = jnp.pad(coefs.T, ((0, chp - ch), (0, LANES - 9)))
@@ -547,17 +622,24 @@
     def tiles(*lead):
         return lead + (chp, LANES), BF
 
-    mine, above, below = call(
-        values_body,
-        [(x.shape, BF) for x in (mine, above, below)],
-        mine, above, below, coefs,
+    mine, part = call(
+        own_values_body,
+        [(mine.shape, BF), ((cols, chp, LANES), F32)],
+        mine, coefs,
+        flops=3 * 10**9,
+        aliases={0: 0},
+    )
+    mine, *sides = call(
+        facing(values_body, 1, 6),
+        [(x.shape, BF) for x in (mine, *sides)],
+        mine, *sides, part, coefs,
         flops=4 * 10**9,
         aliases={0: 0, 1: 1, 2: 2},
     )
     side = (2 * cols + cols // 2, chp, LANES)
     flops = 10 * peers * heads * LANES * (wide + 2 * LANES) * 256
-    dq, to_up, to_down, dk, dv = call(
-        functools.partial(attend_body, heads),
+    dq, *terms, dk, dv = call(
+        facing(functools.partial(attend_body, heads), 2, 5),
         [
             ((peers, chp, LANES), BF),
             (side, BF),
@@ -565,18 +647,17 @@
             ((ROWS, chp, wide), F32),
             ((ROWS, chp, wide), F32),
         ],
-        queries, mine, above, below,
+        queries, mine, *sides,
         flops=flops,
         mib=6,
     )
-    from_above = lax.ppermute(to_down, "z", down_pairs)
-    from_below = lax.ppermute(to_up, "z", up_pairs)
+    got_terms = exchange(terms)
 
     own = ((ROWS, chp, wide), F32)
     sent_dq, dk, dv = call(
-        functools.partial(kernel_grad_body, ch),
+        facing(functools.partial(kernel_grad_body, ch), 2, 6),
         [((peers, chp + 32, LANES), BF), own, own],
-        dq, mine, above, below, dk, dv, to_up, to_down,
+        dq, mine, *sides, dk, dv, *terms,
         scratch=[
             pltpu.VMEM((chp, LANES), F32),
             pltpu.VMEM((peers, 32, LANES), BF),
@@ -589,9 +670,9 @@
     dq_back = swap(sent_dq)
 
     (results,) = call(
-        finish_body, [tiles(peers, 3)],
+        facing(finish_body, 2, 4), [tiles(peers, 3)],
         *[pltpu.with_memory_space_constraint(x, pltpu.HBM) for x in (dk, dv)],
-        to_up, to_down, from_below, from_above, coefs,
+        *terms, *got_terms, coefs,
         scratch=[
             pltpu.VMEM((ROWS, chp, wide), F32),
             pltpu.VMEM((ROWS, chp, wide), F32),

time: 86.5 us -> 81.2 us (0.939)
  waiting for transfers between devices: 28.1 us -> 23.7 us
  starting transfers between devices: 30.7 us -> 27.7 us
  Pallas kernels: 24.5 us -> 26.7 us
    ppermute x4, waiting for transfers between devices: 9.79 us -> 4.96 us  [exchange(): return [lax.ppermute(x, 'z', pairs) for x, pairs in zip(messages, rounds)]]
    ppermute x4, starting transfers between devices: 11.5 us -> 8.14 us  [exchange(): return [lax.ppermute(x, 'z', pairs) for x, pairs in zip(messages, rounds)]]
    pallas_call x11 -> x12, Pallas kernels: 24.5 us -> 26.7 us  [call(): pl.pallas_call(body, out_shape=[(pltpu.HBM if n in hbm else jax.ShapeDtyp...]
  transfers between devices with their start and end apart: 10 -> 10, of which waited for: 6 -> 5; matrix products, arithmetic and copies ran while one was open for 2% -> 2% of each run, Pallas kernels for 18% -> 22%
where the time goes in v5:
time: 81.2 us; the launch traced here: 80.5 us
  starting transfers between devices  27.7 us (34%)
  Pallas kernels  26.7 us (33%)
  waiting for transfers between devices  23.7 us (29%)
  local copies, waits for them, and re-layouts  0.9 us (1%)
    pallas_call x12, Pallas kernels, call(): pl.pallas_call(body, out_shape=[(pltpu.HBM if n in hbm else jax.ShapeDtyp...  26.7 us
    all_to_all x4, starting transfers between devices, swap(): return lax.all_to_all(x.reshape(peers, -1, LANES), plane, 0, 0, tiled=True)  15.7 us
    all_to_all x4, waiting for transfers between devices, swap(): return lax.all_to_all(x.reshape(peers, -1, LANES), plane, 0, 0, tiled=True)  10.7 us
    ppermute x4, starting transfers between devices, exchange(): return [lax.ppermute(x, 'z', pairs) for x, pairs in zip(messages, rounds)]  8.14 us
    ppermute x2, waiting for transfers between devices, per_device(): other = lax.ppermute(taps_sum, 'z', [(i, i ^ step) for i in range(planes)])  8.03 us
    ppermute x4, waiting for transfers between devices, exchange(): return [lax.ppermute(x, 'z', pairs) for x, pairs in zip(messages, rounds)]  4.96 us
    ppermute x2, starting transfers between devices, per_device(): other = lax.ppermute(taps_sum, 'z', [(i, i ^ step) for i in range(planes)])  3.84 us
  transfers between devices with their start and end apart: 10, of which 5 were waited for; matrix products, arithmetic and copies ran while one was open for 2% of the time, Pallas kernels for 22%

profile of v5, /device:TPU:0, one launch (start us, length us, event | category | flops | bytes accessed | tf_op | source)
XLA Modules:
  0.0 80.5 jit_solution(13325273991061407403)
XLA Ops:
  0.6 2.2 %shard_map.110 = bf16[8,432,128]{2,1,0:T(8,128)(2,1)} custom-call(bf16[128,1152]{1,0:T(8,128)(2,1)} %bitcast.20, bf16[128,1152]{1,0:T(8,128)(2,1)} %bitcast.21, bf16[128,1152]{1,0:T(8,128)(2,1)} %bitcast.22), custom_call_target="tpu_custom_call" | custom-call | bytes 1769472 | tf_op jit(solution)/shard_map/pallas_call | solution.py:34
  2.9 5.2 %all-to-all-start = ((bf16[8,432,128]{2,1,0:T(8,128)(2,1)}), bf16[8,432,128]{2,1,0:T(8,128)(2,1)S(1)}, u32[]{:S(2)}, u32[]{:S(2)}) async-start(bf16[8,432,128]{2,1,0:T(8,128)(2,1)} %shard_map.110), calls=%async_computation | async-start | bytes 1769472 | tf_op jit(solution)/shard_map/all_to_all | solution.py:576
  8.1 0.7 bitcast_or_fusion
  8.7 0.1 pad_add_fusion
  8.8 0.7 broadcast_in_dim.16.refs_2_
  9.5 2.8 %shard_map.111 = bf16[8,304,128]{2,1,0:T(8,128)(2,1)} custom-call(bf16[128,1152]{1,0:T(8,128)(2,1)} %bitcast.24, bf16[128,1152]{1,0:T(8,128)(2,1)} %bitcast.25, f32[16,128]{1,0:T(8,128)} %broadcast_in_dim.16.refs_2_), custom_call_target="tpu_custom_call" | custom-call | bytes 1220608 | tf_op jit(solution)/shard_map/pallas_call | solution.py:34
  12.3 8.5 %all-to-all-done = bf16[8,432,128]{2,1,0:T(8,128)(2,1)S(1)} async-done(((bf16[8,432,128]{2,1,0:T(8,128)(2,1)}), bf16[8,432,128]{2,1,0:T(8,128)(2,1)S(1)}, u32[]{:S(2)}, u32[]{:S(2)}) %all-to-all-start) | async-done | bytes 884768 | tf_op jit(solution)/shard_map/all_to_all | solution.py:576
  20.8 0.0 copy-start
  20.8 0.9 %shard_map.113 = (bf16[14,144,128]{2,1,0:T(8,128)(2,1)}, bf16[14,144,128]{2,1,0:T(8,128)(2,1)S(1)}) custom-call(bf16[8,3,144,128]{3,2,1,0:T(8,128)(2,1)S(1)} %bitcast.17), custom_call_target="tpu_custom_call" | custom-call | bytes 1916928 | tf_op jit(solution)/shard_map/pallas_call | solution.py:34
  21.6 1.6 %collective-permute-start = (bf16[14,144,128]{2,1,0:T(8,128)(2,1)}, bf16[14,144,128]{2,1,0:T(8,128)(2,1)S(1)}, u32[]{:S(2)}, u32[]{:S(2)}) collective-permute-start(bf16[14,144,128]{2,1,0:T(8,128)(2,1)} %get-tuple-element.30), channel_id=1, source_target_pairs={{0,8},{8,0},{16,24},{24,16},{1,9},{9,1},{17,25},{25,17},{2,10},{10... | collective-permute-start | bytes 1548296 | tf_op jit(solution)/shard_map/ppermute | solution.py:611
  23.2 0.7 collective-permute-start.1
  23.9 0.0 copy-done
  24.0 0.1 constant_dynamic-slice_fusion
  24.0 0.1 copy.18
  24.2 3.6 %all-to-all-start.1 = ((bf16[8,304,128]{2,1,0:T(8,128)(2,1)}), bf16[8,304,128]{2,1,0:T(8,128)(2,1)S(1)}, u32[]{:S(2)}, u32[]{:S(2)}) async-start(bf16[8,304,128]{2,1,0:T(8,128)(2,1)} %shard_map.111), calls=%async_computation.1 | async-start | bytes 1245184 | tf_op jit(solution)/shard_map/all_to_all | solution.py:576
  27.7 2.5 %shard_map.112 = (bf16[8,3,144,128]{3,2,1,0:T(8,128)(2,1)S(1)}, f32[4,144,128]{2,1,0:T(8,128)S(1)}) custom-call(bf16[8,3,144,128]{3,2,1,0:T(8,128)(2,1)S(1)} %bitcast.18, f32[144,128]{1,0:T(8,128)S(1)} %pad.9.kc_ref.refs_4_.refs_6_), custom_call_target="tpu_custom_call", output_to_operand_aliasing={{0}: (0, {})} | custom-call | flops 3000000000 | bytes 2138112 | tf_op jit(solution)/shard_map/pallas_call | solution.py:34
  30.2 5.0 %collective-permute-done.refs_1_ = bf16[14,144,128]{2,1,0:T(8,128)(2,1)S(1)} collective-permute-done((bf16[14,144,128]{2,1,0:T(8,128)(2,1)}, bf16[14,144,128]{2,1,0:T(8,128)(2,1)S(1)}, u32[]{:S(2)}, u32[]{:S(2)}) %collective-permute-start) | collective-permute-done | bytes 516128 | tf_op jit(solution)/shard_map/ppermute | solution.py:611
  35.1 0.0 collective-permute-done.1.refs_2_
  35.1 2.9 %shard_map.114 = (bf16[8,3,144,128]{3,2,1,0:T(8,128)(2,1)S(1)}, bf16[14,144,128]{2,1,0:T(8,128)(2,1)S(1)}, bf16[14,144,128]{2,1,0:T(8,128)(2,1)S(1)}) custom-call(bf16[8,3,144,128]{3,2,1,0:T(8,128)(2,1)S(1)} %get-tuple-element.29.refs_0_, ...), custom_call_target="tpu_custom_call", output_to_operand_aliasing={{0}: (0, {}), {1}: (1, {}), {2}: (2, {})} | custom-call | flops 4000000000 | bytes 4202496 | tf_op jit(solution)/shard_map/pallas_call | solution.py:34
  38.1 0.0 all-to-all-done.1.refs_0_
  38.1 4.8 %shard_map.115 = (bf16[8,144,128]{2,1,0:T(8,128)(2,1)S(1)}, bf16[10,144,128]{2,1,0:T(8,128)(2,1)S(1)}, bf16[10,144,128]{2,1,0:T(8,128)(2,1)S(1)}, f32[2,144,512]{2,1,0:T(8,128)S(1)}, f32[2,144,512]{2,1,0:T(8,128)S(1)}) custom-call(bf16[8,304,128]{2,1,0:T(8,128)(2,1)S(1)} %all-to-all-done.1.refs_0_, bf16[8,3,144,128]{3,2,1,0:T(8,128)(2,1)S(1)} %get-tuple-element.33.refs_1_, ...), custom_call_target="tpu_custom_call" | custom-call | flops 4026531840 | bytes 4751360 | tf_op jit(solution)/shard_map/pallas_call | solution.py:34
  42.8 4.5 %collective-permute-start.2 = (bf16[10,144,128]{2,1,0:T(8,128)(2,1)S(1)}, bf16[10,144,128]{2,1,0:T(8,128)(2,1)}, u32[]{:S(2)}, u32[]{:S(2)}) collective-permute-start(bf16[10,144,128]{2,1,0:T(8,128)(2,1)S(1)} %get-tuple-element.39.refs_6_.refs_2_), channel_id=1, source_target_pairs={{0,8},{8,0},{16,24},{24,16},{1,9},{9,1},{17,25},{25,17},{2,10},{10... | collective-permute-start | bytes 1105928 | tf_op jit(solution)/shard_map/ppermute | solution.py:611
  47.3 1.4 %collective-permute-start.3 = (bf16[10,144,128]{2,1,0:T(8,128)(2,1)S(1)}, bf16[10,144,128]{2,1,0:T(8,128)(2,1)}, u32[]{:S(2)}, u32[]{:S(2)}) collective-permute-start(bf16[10,144,128]{2,1,0:T(8,128)(2,1)S(1)} %get-tuple-element.40.refs_7_.refs_3_), channel_id=1, source_target_pairs={{8,16},{16,8},{9,17},{17,9},{10,18},{18,10},{11,19},{19,11},{12,20... | collective-permute-start | bytes 1105928 | tf_op jit(solution)/shard_map/ppermute | solution.py:611
  48.7 3.2 %shard_map.116 = (bf16[8,176,128]{2,1,0:T(8,128)(2,1)}, f32[2,144,512]{2,1,0:T(8,128)}, f32[2,144,512]{2,1,0:T(8,128)}) custom-call(bf16[8,144,128]{2,1,0:T(8,128)(2,1)S(1)} %get-tuple-element.36.refs_0_, bf16[8,3,144,128]{3,2,1,0:T(8,128)(2,1)S(1)} %get-tuple-element.33.refs_1_, bf16[14,144,128]{2,1,0:T(8,128)(2,1)S(1)} %get-tuple-element.34.refs_2_, ...), custom_call_target="tpu_custom_call" | custom-call | flops 4000000000 | bytes 5668864 | tf_op jit(solution)/shard_map/pallas_call | solution.py:34
  51.9 3.5 %all-to-all-start.2 = ((bf16[8,176,128]{2,1,0:T(8,128)(2,1)}), bf16[8,176,128]{2,1,0:T(8,128)(2,1)S(1)}, u32[]{:S(2)}, u32[]{:S(2)}) async-start(bf16[8,176,128]{2,1,0:T(8,128)(2,1)} %get-tuple-element.41), calls=%async_computation.2 | async-start | bytes 720896 | tf_op jit(solution)/shard_map/all_to_all | solution.py:576
  55.4 0.0 collective-permute-done.2.refs_4_
  55.4 0.0 collective-permute-done.3.refs_5_
  55.4 4.8 %shard_map.118 = bf16[8,3,144,128]{3,2,1,0:T(8,128)(2,1)} custom-call(f32[2,144,512]{2,1,0:T(8,128)} %get-tuple-element.43.refs_0_, f32[2,144,512]{2,1,0:T(8,128)} %get-tuple-element.44.refs_1_, bf16[10,144,128]{2,1,0:T(8,128)(2,1)S(1)} %get-tuple-element.39.refs_6_.refs_2_, bf16[10,144,128]{2,1,0:T(8,128)(2,1)S(1)} %get-tuple-element.40.refs_7_.refs_3_, ...), custom_call_target="tpu_custom_call" | custom-call | flops 4000000000 | bytes 3612672 | tf_op jit(solution)/shard_map/pallas_call | solution.py:34
  60.2 2.2 %all-to-all-done.2.x_ref = bf16[8,176,128]{2,1,0:T(8,128)(2,1)S(1)} async-done(((bf16[8,176,128]{2,1,0:T(8,128)(2,1)}), bf16[8,176,128]{2,1,0:T(8,128)(2,1)S(1)}, u32[]{:S(2)}, u32[]{:S(2)}) %all-to-all-start.2) | async-done | bytes 360480 | tf_op jit(solution)/shard_map/all_to_all | solution.py:576
  62.4 3.6 %all-to-all-start.3 = ((bf16[8,432,128]{2,1,0:T(8,128)(2,1)}), bf16[8,432,128]{2,1,0:T(8,128)(2,1)S(1)}, u32[]{:S(2)}, u32[]{:S(2)}) async-start(bf16[8,432,128]{2,1,0:T(8,128)(2,1)} %bitcast.11), calls=%async_computation.3 | async-start | bytes 1769472 | tf_op jit(solution)/shard_map/all_to_all | solution.py:576
  66.0 1.0 %shard_map.117 = (bf16[128,1152]{1,0:T(8,128)(2,1)}, f32[16,1152]{1,0:T(8,128)S(1)}) custom-call(bf16[8,176,128]{2,1,0:T(8,128)(2,1)S(1)} %all-to-all-done.2.x_ref), custom_call_target="tpu_custom_call" | custom-call | bytes 729088 | tf_op jit(solution)/shard_map/pallas_call | solution.py:34
  67.0 2.3 %collective-permute-start.4 = (f32[16,1152]{1,0:T(8,128)S(1)}, f32[16,1152]{1,0:T(8,128)S(1)}, u32[]{:S(2)}, u32[]{:S(2)}) collective-permute-start(f32[16,1152]{1,0:T(8,128)S(1)} %get-tuple-element.48.x_ref), channel_id=1, source_target_pairs={{0,8},{8,0},{16,24},{24,16},{1,9},{9,1},{17,25},{25,17},{2,10},{10... | collective-permute-start | bytes 221192 | tf_op jit(solution)/shard_map/ppermute | solution.py:694
  69.2 2.8 %collective-permute-done.4.y_ref = f32[16,1152]{1,0:T(8,128)S(1)} collective-permute-done((f32[16,1152]{1,0:T(8,128)S(1)}, f32[16,1152]{1,0:T(8,128)S(1)}, u32[]{:S(2)}, u32[]{:S(2)}) %collective-permute-start.4) | collective-permute-done | bytes 73760 | tf_op jit(solution)/shard_map/ppermute | solution.py:694
  72.1 1.6 %collective-permute-start.5 = (f32[16,1152]{1,0:T(8,128)S(1)}, f32[16,1152]{1,0:T(8,128)S(1)}, u32[]{:S(2)}, u32[]{:S(2)}) collective-permute-start(f32[16,1152]{1,0:T(8,128)S(1)} %shard_map.120.x_ref), channel_id=1, source_target_pairs={{0,16},{8,24},{16,0},{24,8},{1,17},{9,25},{17,1},{25,9},{2,18},{10... | collective-permute-start | bytes 221192 | tf_op jit(solution)/shard_map/ppermute | solution.py:697
  73.6 5.2 %collective-permute-done.5.y_ref = f32[16,1152]{1,0:T(8,128)S(1)} collective-permute-done((f32[16,1152]{1,0:T(8,128)S(1)}, f32[16,1152]{1,0:T(8,128)S(1)}, u32[]{:S(2)}, u32[]{:S(2)}) %collective-permute-start.5) | collective-permute-done | bytes 73760 | tf_op jit(solution)/shard_map/ppermute | solution.py:697
  78.8 0.6 shard_map.121
  79.5 0.0 all-to-all-done.3
  79.5 1.0 %shard_map.119 = (bf16[128,1152]{1,0:T(8,128)(2,1)}, bf16[128,1152]{1,0:T(8,128)(2,1)}, bf16[128,1152]{1,0:T(8,128)(2,1)}) custom-call(bf16[8,3,144,128]{3,2,1,0:T(8,128)(2,1)S(1)} %bitcast.19), custom_call_target="tpu_custom_call" | custom-call | bytes 1769472 | tf_op jit(solution)/shard_map/pallas_call | solution.py:34
  (4 shorter events, 0.0 us)
Async XLA Ops:
  2.9 17.9 %all-to-all-start = ((bf16[8,432,128]{2,1,0:T(8,128)(2,1)}), bf16[8,432,128]{2,1,0:T(8,128)(2,1)S(1)}, u32[]{:S(2)}, u32[]{:S(2)}) async-start(bf16[8,432,128]{2,1,0:T(8,128)(2,1)} %shard_map.110), calls=%async_computation | async-start | bytes 1769472 | tf_op jit(solution)/shard_map/all_to_all | solution.py:576
  20.8 3.2 %copy-start = (f32[3,3,1152]{2,1,0:T(4,128)S(1)}, f32[3,3,1152]{2,1,0:T(4,128)}, u32[]{:S(2)}) copy-start(f32[3,3,1152]{2,1,0:T(4,128)} %param.11) | copy-start | bytes 124420
  21.6 13.5 %collective-permute-start = (bf16[14,144,128]{2,1,0:T(8,128)(2,1)}, bf16[14,144,128]{2,1,0:T(8,128)(2,1)S(1)}, u32[]{:S(2)}, u32[]{:S(2)}) collective-permute-start(bf16[14,144,128]{2,1,0:T(8,128)(2,1)} %get-tuple-element.30), channel_id=1, source_target_pairs={{0,8},{8,0},{16,24},{24,16},{1,9},{9,1},{17,25},{25,17},{2,10},{10... | collective-permute-start | bytes 1548296 | tf_op jit(solution)/shard_map/ppermute | solution.py:611
  23.2 11.9 %collective-permute-start.1 = (bf16[14,144,128]{2,1,0:T(8,128)(2,1)S(1)}, bf16[14,144,128]{2,1,0:T(8,128)(2,1)S(1)}, u32[]{:S(2)}, u32[]{:S(2)}) collective-permute-start(bf16[14,144,128]{2,1,0:T(8,128)(2,1)S(1)} %get-tuple-element.31), channel_id=1, source_target_pairs={{8,16},{16,8},{9,17},{17,9},{10,18},{18,10},{11,19},{19,11},{12,20... | collective-permute-start | bytes 1548296 | tf_op jit(solution)/shard_map/ppermute | solution.py:611
  24.2 13.9 %all-to-all-start.1 = ((bf16[8,304,128]{2,1,0:T(8,128)(2,1)}), bf16[8,304,128]{2,1,0:T(8,128)(2,1)S(1)}, u32[]{:S(2)}, u32[]{:S(2)}) async-start(bf16[8,304,128]{2,1,0:T(8,128)(2,1)} %shard_map.111), calls=%async_computation.1 | async-start | bytes 1245184 | tf_op jit(solution)/shard_map/all_to_all | solution.py:576
  42.8 12.5 %collective-permute-start.2 = (bf16[10,144,128]{2,1,0:T(8,128)(2,1)S(1)}, bf16[10,144,128]{2,1,0:T(8,128)(2,1)}, u32[]{:S(2)}, u32[]{:S(2)}) collective-permute-start(bf16[10,144,128]{2,1,0:T(8,128)(2,1)S(1)} %get-tuple-element.39.refs_6_.refs_2_), channel_id=1, source_target_pairs={{0,8},{8,0},{16,24},{24,16},{1,9},{9,1},{17,25},{25,17},{2,10},{10... | collective-permute-start | bytes 1105928 | tf_op jit(solution)/shard_map/ppermute | solution.py:611
  47.3 8.1 %collective-permute-start.3 = (bf16[10,144,128]{2,1,0:T(8,128)(2,1)S(1)}, bf16[10,144,128]{2,1,0:T(8,128)(2,1)}, u32[]{:S(2)}, u32[]{:S(2)}) collective-permute-start(bf16[10,144,128]{2,1,0:T(8,128)(2,1)S(1)} %get-tuple-element.40.refs_7_.refs_3_), channel_id=1, source_target_pairs={{8,16},{16,8},{9,17},{17,9},{10,18},{18,10},{11,19},{19,11},{12,20... | collective-permute-start | bytes 1105928 | tf_op jit(solution)/shard_map/ppermute | solution.py:611
  51.9 10.5 %all-to-all-start.2 = ((bf16[8,176,128]{2,1,0:T(8,128)(2,1)}), bf16[8,176,128]{2,1,0:T(8,128)(2,1)S(1)}, u32[]{:S(2)}, u32[]{:S(2)}) async-start(bf16[8,176,128]{2,1,0:T(8,128)(2,1)} %get-tuple-element.41), calls=%async_computation.2 | async-start | bytes 720896 | tf_op jit(solution)/shard_map/all_to_all | solution.py:576
  62.4 17.1 %all-to-all-start.3 = ((bf16[8,432,128]{2,1,0:T(8,128)(2,1)}), bf16[8,432,128]{2,1,0:T(8,128)(2,1)S(1)}, u32[]{:S(2)}, u32[]{:S(2)}) async-start(bf16[8,432,128]{2,1,0:T(8,128)(2,1)} %bitcast.11), calls=%async_computation.3 | async-start | bytes 1769472 | tf_op jit(solution)/shard_map/all_to_all | solution.py:576
  67.0 5.1 %collective-permute-start.4 = (f32[16,1152]{1,0:T(8,128)S(1)}, f32[16,1152]{1,0:T(8,128)S(1)}, u32[]{:S(2)}, u32[]{:S(2)}) collective-permute-start(f32[16,1152]{1,0:T(8,128)S(1)} %get-tuple-element.48.x_ref), channel_id=1, source_target_pairs={{0,8},{8,0},{16,24},{24,16},{1,9},{9,1},{17,25},{25,17},{2,10},{10... | collective-permute-start | bytes 221192 | tf_op jit(solution)/shard_map/ppermute | solution.py:694
  72.1 6.8 %collective-permute-start.5 = (f32[16,1152]{1,0:T(8,128)S(1)}, f32[16,1152]{1,0:T(8,128)S(1)}, u32[]{:S(2)}, u32[]{:S(2)}) collective-permute-start(f32[16,1152]{1,0:T(8,128)S(1)} %shard_map.120.x_ref), channel_id=1, source_target_pairs={{0,16},{8,24},{16,0},{24,8},{1,17},{9,25},{17,1},{25,9},{2,18},{10... | collective-permute-start | bytes 221192 | tf_op jit(solution)/shard_map/ppermute | solution.py:697

commit v6 on v5

--- a/solution.py
+++ b/solution.py
@@ -130,8 +130,8 @@
     if ch % 16:
         pieces = [piece.astype(F32)[:ch] for piece in pieces]
     store_halves(out, jnp.concatenate(pieces, axis=0).T.astype(BF))
-    wide = gk_ref.shape[1]
-    total = [jnp.zeros((16, LANES), F32) for _ in range(wide // LANES + 2)]
+    count = out.shape[1] // LANES
+    total = [jnp.zeros((16, LANES), F32) for _ in range(count + 2)]
     lane = lax.broadcasted_iota(jnp.int32, (16, LANES), 1)
     for p in range(peers):
         table = x_ref[p, chp:].astype(F32)
@@ -146,17 +146,26 @@
             total[first + b] = total[first + b] + jnp.where(lane >= off, turned, 0.0)
             if off:
                 total[first + b + 1] = total[first + b + 1] + jnp.where(lane < off, turned, 0.0)
-    gk_ref[...] = jnp.concatenate(total[: wide // LANES], axis=1)
+    gk_ref[...] = jnp.zeros_like(gk_ref)
+    for n in range(count):
+        gk_ref[9 * n : 9 * n + 9] = total[n][:9]
 
 
 def taps_out_body(x_ref, y_ref, out):
     total = x_ref[...] + y_ref[...]
+    count = out.shape[2] // LANES
+    total = jnp.concatenate([total[9 * n : 9 * n + 9] for n in range(count)], axis=1)
     for a in range(3):
         out[a] = total[3 * a : 3 * a + 3]
 
 
 def add_body(x_ref, y_ref, out):
     out[...] = x_ref[...] + y_ref[...]
+
+
+def chunks(rows):
+    count = rows // 16
+    return pl.loop(0, count, unroll=1 if count % 3 else 3)
 
 
 def second_rows(rows):
@@ -261,7 +270,7 @@
 def own_values_body(a_ref, kc_ref, a_out, part_ref):
     cols = a_ref.shape[0] // ROWS
 
-    @pl.loop(0, a_ref.shape[2] // 16)
+    @chunks(a_ref.shape[2])
     def _(step):
         at = pl.ds(pl.multiple_of(step * 16, 16), 16)
         masks = lane_masks(16)
@@ -283,7 +292,7 @@
 def values_body(a_ref, u_ref, d_ref, part_ref, kc_ref, a_out, u_out, d_out):
     cols = a_ref.shape[0] // ROWS
 
-    @pl.loop(0, a_ref.shape[2] // 16)
+    @chunks(a_ref.shape[2])
     def _(step):
         at = pl.ds(pl.multiple_of(step * 16, 16), 16)
         masks = lane_masks(16)
@@ -428,7 +437,7 @@
     for copy in copies:
         copy.start()
 
-    @pl.loop(0, chp // 16)
+    @chunks(chp)
     def _(step):
         at = pl.ds(pl.multiple_of(step * 16, 16), 16)
         masks = lane_masks(16)
@@ -451,22 +460,23 @@
                     acc[3 + b] += here[j][b] * g
                     acc[6 + b] += jnp.where(second[j % 2], here[j][b], below[j][b]) * turned
             above, here = here, below
-        lane = lax.broadcasted_iota(jnp.int32, (16, LANES), 1)
-        out = jnp.zeros((16, LANES), F32)
-        for t in range(9):
-            out = jnp.where(lane == t, jnp.sum(acc[t], axis=1, keepdims=True), out)
-        sums[at, :] = out
-
+        for n in range(9):
+            sums[n, at, :] = acc[n]
+
+    lane = lax.broadcasted_iota(jnp.int32, (chp, LANES), 1)
+    whole = jnp.zeros((chp, LANES), F32)
+    for t in range(9):
+        whole = jnp.where(lane == t, jnp.sum(sums[t], axis=1, keepdims=True), whole)
     def split(x):
         high = x.astype(BF).astype(F32)
         return high, x - high
 
-    high, low = split(sums[: min(chp, LANES)])
+    high, low = split(whole[: min(chp, LANES)])
     table = high + pltpu.roll(low, 9, 1)
     if chp < LANES:
         table = jnp.concatenate([table, jnp.zeros((LANES - chp, LANES), F32)], axis=0)
     if chp > LANES:
-        more = jnp.concatenate(split(sums[LANES:]), axis=0)
+        more = jnp.concatenate(split(whole[LANES:]), axis=0)
         more = jnp.concatenate([more, jnp.zeros((LANES - more.shape[0], LANES), F32)], axis=0)
         table = table + pltpu.roll(more, 18, 1)
     table = table.T[:32].astype(BF)
@@ -479,7 +489,7 @@
 
 
 def finish_body(
-    dk_hbm, dv_hbm, up_ref, down_ref, u_ref, d_ref, kc_ref, out_ref, dk_ref, dv_ref, held, sems
+    dk_hbm, dv_hbm, up_ref, down_ref, u_hbm, d_hbm, kc_ref, out_ref, dk_ref, dv_ref, u_ref, d_ref, held, sems, ends
 ):
     cols = held.shape[0] // ROWS
     chp = held.shape[2]
@@ -487,26 +497,23 @@
     def chunk(step):
         return pl.ds(pl.multiple_of(step * 16, 16), 16)
 
-    def get(step):
-        at = chunk(step)
-        return [
-            pltpu.make_async_copy(dk_hbm.at[:, at], dk_ref.at[:, at], sems.at[0, step]),
-            pltpu.make_async_copy(dv_hbm.at[:, at], dv_ref.at[:, at], sems.at[1, step]),
-        ]
-
     def put(step):
         at = chunk(step)
-        return pltpu.make_async_copy(held.at[:, :, at], out_ref.at[:, :, at], sems.at[2, step])
+        return pltpu.make_async_copy(held.at[:, :, at], out_ref.at[:, :, at], ends.at[step])
+
+    gets = [
+        pltpu.make_async_copy(*pair, sems.at[n])
+        for n, pair in enumerate(
+            ((u_hbm, u_ref), (d_hbm, d_ref), (dk_hbm, dk_ref), (dv_hbm, dv_ref))
+        )
+    ]
+    for get in gets:
+        get.start()
+    for get in gets:
+        get.wait()
 
     @pl.loop(0, chp // 16)
     def _(step):
-        for copy in get(step):
-            copy.start()
-
-    @pl.loop(0, chp // 16)
-    def _(step):
-        for copy in get(step):
-            copy.wait()
         at = chunk(step)
         masks = lane_masks(16)
         coef = taps(kc_ref, at)[::-1]
@@ -659,7 +666,7 @@
         [((peers, chp + 32, LANES), BF), own, own],
         dq, mine, *sides, dk, dv, *terms,
         scratch=[
-            pltpu.VMEM((chp, LANES), F32),
+            pltpu.VMEM((9, chp, LANES), F32),
             pltpu.VMEM((peers, 32, LANES), BF),
             pltpu.SemaphoreType.DMA((4,)),
         ],
@@ -676,23 +683,27 @@
         scratch=[
             pltpu.VMEM((ROWS, chp, wide), F32),
             pltpu.VMEM((ROWS, chp, wide), F32),
+            pltpu.VMEM(side, BF),
+            pltpu.VMEM(side, BF),
             pltpu.VMEM((peers, 3, chp, LANES), BF),
-            pltpu.SemaphoreType.DMA((3, chp // 16)),
+            pltpu.SemaphoreType.DMA((4,)),
+            pltpu.SemaphoreType.DMA((chp // 16,)),
         ],
-        far_in=(0, 1),
+        far_in=(0, 1, 4, 5),
         far_out=(0,),
         flops=4 * 10**9,
     )
     back = swap(results).reshape(peers, 3, chp, LANES)
+    sums = (-(-9 * channels // (8 * LANES)) * 8, LANES)
     grad_query, taps_sum = call(
         functools.partial(unpack_query_body, ch, chp),
-        [((LANES, channels), BF), ((16, channels), F32)],
+        [((LANES, channels), BF), (sums, F32)],
         dq_back,
     )
     step = 1
     while 2 * step < planes:
         other = lax.ppermute(taps_sum, "z", [(i, i ^ step) for i in range(planes)])
-        (taps_sum,) = call(add_body, [((16, channels), F32)], taps_sum, other)
+        (taps_sum,) = call(add_body, [(sums, F32)], taps_sum, other)
         step *= 2
     other = lax.ppermute(taps_sum, "z", [(i, i ^ step) for i in range(planes)])
     (grad_kernel,) = call(taps_out_body, [((3, 3, channels), F32)], taps_sum, other)

time: 81.2 us -> 79.1 us (0.974)
  Pallas kernels: 26.7 us -> 24.8 us
    ppermute x2, waiting for transfers between devices: 8.03 us -> 5.95 us  [per_device(): other = lax.ppermute(taps_sum, 'z', [(i, i ^ step) for i in range(planes)])]
    pallas_call x12, Pallas kernels: 26.7 us -> 24.8 us  [call(): pl.pallas_call(body, out_shape=[(pltpu.HBM if n in hbm else jax.ShapeDtyp...]
    ppermute x4, waiting for transfers between devices: 4.96 us -> 6.22 us  [exchange(): return [lax.ppermute(x, 'z', pairs) for x, pairs in zip(messages, rounds)]]
  transfers between devices with their start and end apart: 10 -> 10, of which waited for: 5 -> 7; matrix products, arithmetic and copies ran while one was open for 2% -> 2% of each run, Pallas kernels for 22% -> 20%
where the time goes in v6:
time: 79.1 us; the launch traced here: 78.5 us
  starting transfers between devices  27.8 us (35%)
  Pallas kernels  24.8 us (31%)
  waiting for transfers between devices  23.5 us (30%)
  local copies, waits for them, and re-layouts  0.9 us (1%)
    pallas_call x12, Pallas kernels, call(): pl.pallas_call(body, out_shape=[(pltpu.HBM if n in hbm else jax.ShapeDtyp...  24.8 us
    all_to_all x4, starting transfers between devices, swap(): return lax.all_to_all(x.reshape(peers, -1, LANES), plane, 0, 0, tiled=True)  15.7 us
    all_to_all x4, waiting for transfers between devices, swap(): return lax.all_to_all(x.reshape(peers, -1, LANES), plane, 0, 0, tiled=True)  11.4 us
    ppermute x4, starting transfers between devices, exchange(): return [lax.ppermute(x, 'z', pairs) for x, pairs in zip(messages, rounds)]  8.14 us
    ppermute x4, waiting for transfers between devices, exchange(): return [lax.ppermute(x, 'z', pairs) for x, pairs in zip(messages, rounds)]  6.22 us
    ppermute x2, waiting for transfers between devices, per_device(): other = lax.ppermute(taps_sum, 'z', [(i, i ^ step) for i in range(planes)])  5.95 us
    ppermute x2, starting transfers between devices, per_device(): other = lax.ppermute(taps_sum, 'z', [(i, i ^ step) for i in range(planes)])  3.89 us
  transfers between devices with their start and end apart: 10, of which 7 were waited for; matrix products, arithmetic and copies ran while one was open for 2% of the time, Pallas kernels for 20%

profile of v6, /device:TPU:0, one launch (start us, length us, event | category | flops | bytes accessed | tf_op | source)
XLA Modules:
  0.0 78.5 jit_solution(17680256244994118231)
XLA Ops:
  0.6 2.2 %shard_map.110 = bf16[8,432,128]{2,1,0:T(8,128)(2,1)} custom-call(bf16[128,1152]{1,0:T(8,128)(2,1)} %bitcast.20, bf16[128,1152]{1,0:T(8,128)(2,1)} %bitcast.21, bf16[128,1152]{1,0:T(8,128)(2,1)} %bitcast.22), custom_call_target="tpu_custom_call" | custom-call | bytes 1769472 | tf_op jit(solution)/shard_map/pallas_call | solution.py:34
  2.9 5.2 %all-to-all-start = ((bf16[8,432,128]{2,1,0:T(8,128)(2,1)}), bf16[8,432,128]{2,1,0:T(8,128)(2,1)S(1)}, u32[]{:S(2)}, u32[]{:S(2)}) async-start(bf16[8,432,128]{2,1,0:T(8,128)(2,1)} %shard_map.110), calls=%async_computation | async-start | bytes 1769472 | tf_op jit(solution)/shard_map/all_to_all | solution.py:583
  8.1 0.7 bitcast_or_fusion
  8.7 0.1 pad_add_fusion
  8.8 0.7 broadcast_in_dim.16.refs_2_
  9.5 2.8 %shard_map.111 = bf16[8,304,128]{2,1,0:T(8,128)(2,1)} custom-call(bf16[128,1152]{1,0:T(8,128)(2,1)} %bitcast.24, bf16[128,1152]{1,0:T(8,128)(2,1)} %bitcast.25, f32[16,128]{1,0:T(8,128)} %broadcast_in_dim.16.refs_2_), custom_call_target="tpu_custom_call" | custom-call | bytes 1220608 | tf_op jit(solution)/shard_map/pallas_call | solution.py:34
  12.3 8.5 %all-to-all-done = bf16[8,432,128]{2,1,0:T(8,128)(2,1)S(1)} async-done(((bf16[8,432,128]{2,1,0:T(8,128)(2,1)}), bf16[8,432,128]{2,1,0:T(8,128)(2,1)S(1)}, u32[]{:S(2)}, u32[]{:S(2)}) %all-to-all-start) | async-done | bytes 884768 | tf_op jit(solution)/shard_map/all_to_all | solution.py:583
  20.8 0.0 copy-start
  20.8 0.9 %shard_map.113 = (bf16[14,144,128]{2,1,0:T(8,128)(2,1)}, bf16[14,144,128]{2,1,0:T(8,128)(2,1)S(1)}) custom-call(bf16[8,3,144,128]{3,2,1,0:T(8,128)(2,1)S(1)} %bitcast.17), custom_call_target="tpu_custom_call" | custom-call | bytes 1916928 | tf_op jit(solution)/shard_map/pallas_call | solution.py:34
  21.6 1.6 %collective-permute-start = (bf16[14,144,128]{2,1,0:T(8,128)(2,1)}, bf16[14,144,128]{2,1,0:T(8,128)(2,1)S(1)}, u32[]{:S(2)}, u32[]{:S(2)}) collective-permute-start(bf16[14,144,128]{2,1,0:T(8,128)(2,1)} %get-tuple-element.30), channel_id=1, source_target_pairs={{0,8},{8,0},{16,24},{24,16},{1,9},{9,1},{17,25},{25,17},{2,10},{10... | collective-permute-start | bytes 1548296 | tf_op jit(solution)/shard_map/ppermute | solution.py:618
  23.2 0.7 collective-permute-start.1
  23.9 0.0 copy-done
  24.0 0.1 constant_dynamic-slice_fusion
  24.0 0.1 copy.18
  24.2 3.6 %all-to-all-start.1 = ((bf16[8,304,128]{2,1,0:T(8,128)(2,1)}), bf16[8,304,128]{2,1,0:T(8,128)(2,1)S(1)}, u32[]{:S(2)}, u32[]{:S(2)}) async-start(bf16[8,304,128]{2,1,0:T(8,128)(2,1)} %shard_map.111), calls=%async_computation.1 | async-start | bytes 1245184 | tf_op jit(solution)/shard_map/all_to_all | solution.py:583
  27.7 2.4 %shard_map.112 = (bf16[8,3,144,128]{3,2,1,0:T(8,128)(2,1)S(1)}, f32[4,144,128]{2,1,0:T(8,128)S(1)}) custom-call(bf16[8,3,144,128]{3,2,1,0:T(8,128)(2,1)S(1)} %bitcast.18, f32[144,128]{1,0:T(8,128)S(1)} %pad.9.kc_ref.refs_4_.refs_6_), custom_call_target="tpu_custom_call", output_to_operand_aliasing={{0}: (0, {})} | custom-call | flops 3000000000 | bytes 2138112 | tf_op jit(solution)/shard_map/pallas_call | solution.py:34
  30.1 5.0 %collective-permute-done.refs_1_ = bf16[14,144,128]{2,1,0:T(8,128)(2,1)S(1)} collective-permute-done((bf16[14,144,128]{2,1,0:T(8,128)(2,1)}, bf16[14,144,128]{2,1,0:T(8,128)(2,1)S(1)}, u32[]{:S(2)}, u32[]{:S(2)}) %collective-permute-start) | collective-permute-done | bytes 516128 | tf_op jit(solution)/shard_map/ppermute | solution.py:618
  35.1 0.0 collective-permute-done.1.refs_2_
  35.1 2.5 %shard_map.114 = (bf16[8,3,144,128]{3,2,1,0:T(8,128)(2,1)S(1)}, bf16[14,144,128]{2,1,0:T(8,128)(2,1)S(1)}, bf16[14,144,128]{2,1,0:T(8,128)(2,1)S(1)}) custom-call(bf16[8,3,144,128]{3,2,1,0:T(8,128)(2,1)S(1)} %get-tuple-element.29.refs_0_, ...), custom_call_target="tpu_custom_call", output_to_operand_aliasing={{0}: (0, {}), {1}: (1, {}), {2}: (2, {})} | custom-call | flops 4000000000 | bytes 4202496 | tf_op jit(solution)/shard_map/pallas_call | solution.py:34
  37.6 0.0 all-to-all-done.1.refs_0_
  37.6 4.9 %shard_map.115 = (bf16[8,144,128]{2,1,0:T(8,128)(2,1)S(1)}, bf16[10,144,128]{2,1,0:T(8,128)(2,1)S(1)}, bf16[10,144,128]{2,1,0:T(8,128)(2,1)S(1)}, f32[2,144,512]{2,1,0:T(8,128)S(1)}, f32[2,144,512]{2,1,0:T(8,128)S(1)}) custom-call(bf16[8,304,128]{2,1,0:T(8,128)(2,1)S(1)} %all-to-all-done.1.refs_0_, bf16[8,3,144,128]{3,2,1,0:T(8,128)(2,1)S(1)} %get-tuple-element.33.refs_1_, ...), custom_call_target="tpu_custom_call" | custom-call | flops 4026531840 | bytes 4751360 | tf_op jit(solution)/shard_map/pallas_call | solution.py:34
  42.6 4.5 %collective-permute-start.2 = (bf16[10,144,128]{2,1,0:T(8,128)(2,1)S(1)}, bf16[10,144,128]{2,1,0:T(8,128)(2,1)}, u32[]{:S(2)}, u32[]{:S(2)}) collective-permute-start(bf16[10,144,128]{2,1,0:T(8,128)(2,1)S(1)} %get-tuple-element.39.refs_6_.refs_2_), channel_id=1, source_target_pairs={{0,8},{8,0},{16,24},{24,16},{1,9},{9,1},{17,25},{25,17},{2,10},{10... | collective-permute-start | bytes 1105928 | tf_op jit(solution)/shard_map/ppermute | solution.py:618
  47.0 1.4 %collective-permute-start.3 = (bf16[10,144,128]{2,1,0:T(8,128)(2,1)S(1)}, bf16[10,144,128]{2,1,0:T(8,128)(2,1)}, u32[]{:S(2)}, u32[]{:S(2)}) collective-permute-start(bf16[10,144,128]{2,1,0:T(8,128)(2,1)S(1)} %get-tuple-element.40.refs_7_.refs_3_), channel_id=1, source_target_pairs={{8,16},{16,8},{9,17},{17,9},{10,18},{18,10},{11,19},{19,11},{12,20... | collective-permute-start | bytes 1105928 | tf_op jit(solution)/shard_map/ppermute | solution.py:618
  48.4 2.3 %shard_map.116 = (bf16[8,176,128]{2,1,0:T(8,128)(2,1)}, f32[2,144,512]{2,1,0:T(8,128)}, f32[2,144,512]{2,1,0:T(8,128)}) custom-call(bf16[8,144,128]{2,1,0:T(8,128)(2,1)S(1)} %get-tuple-element.36.refs_0_, bf16[8,3,144,128]{3,2,1,0:T(8,128)(2,1)S(1)} %get-tuple-element.33.refs_1_, bf16[14,144,128]{2,1,0:T(8,128)(2,1)S(1)} %get-tuple-element.34.refs_2_, ...), custom_call_target="tpu_custom_call" | custom-call | flops 4000000000 | bytes 5668864 | tf_op jit(solution)/shard_map/pallas_call | solution.py:34
  50.8 3.5 %all-to-all-start.2 = ((bf16[8,176,128]{2,1,0:T(8,128)(2,1)}), bf16[8,176,128]{2,1,0:T(8,128)(2,1)S(1)}, u32[]{:S(2)}, u32[]{:S(2)}) async-start(bf16[8,176,128]{2,1,0:T(8,128)(2,1)} %get-tuple-element.41), calls=%async_computation.2 | async-start | bytes 720896 | tf_op jit(solution)/shard_map/all_to_all | solution.py:583
  54.2 1.2 %collective-permute-done.2.refs_4_ = bf16[10,144,128]{2,1,0:T(8,128)(2,1)} collective-permute-done((bf16[10,144,128]{2,1,0:T(8,128)(2,1)S(1)}, bf16[10,144,128]{2,1,0:T(8,128)(2,1)}, u32[]{:S(2)}, u32[]{:S(2)}) %collective-permute-start.2) | collective-permute-done | bytes 368672 | tf_op jit(solution)/shard_map/ppermute | solution.py:618
  55.4 0.0 collective-permute-done.3.refs_5_
  55.4 4.1 %shard_map.118 = bf16[8,3,144,128]{3,2,1,0:T(8,128)(2,1)} custom-call(f32[2,144,512]{2,1,0:T(8,128)} %get-tuple-element.43.refs_0_, f32[2,144,512]{2,1,0:T(8,128)} %get-tuple-element.44.refs_1_, bf16[10,144,128]{2,1,0:T(8,128)(2,1)S(1)} %get-tuple-element.39.refs_6_.refs_2_, bf16[10,144,128]{2,1,0:T(8,128)(2,1)S(1)} %get-tuple-element.40.refs_7_.refs_3_, ...), custom_call_target="tpu_custom_call" | custom-call | flops 4000000000 | bytes 3612672 | tf_op jit(solution)/shard_map/pallas_call | solution.py:34
  59.6 1.7 %all-to-all-done.2.x_ref = bf16[8,176,128]{2,1,0:T(8,128)(2,1)S(1)} async-done(((bf16[8,176,128]{2,1,0:T(8,128)(2,1)}), bf16[8,176,128]{2,1,0:T(8,128)(2,1)S(1)}, u32[]{:S(2)}, u32[]{:S(2)}) %all-to-all-start.2) | async-done | bytes 360480 | tf_op jit(solution)/shard_map/all_to_all | solution.py:583
  61.3 3.6 %all-to-all-start.3 = ((bf16[8,432,128]{2,1,0:T(8,128)(2,1)}), bf16[8,432,128]{2,1,0:T(8,128)(2,1)S(1)}, u32[]{:S(2)}, u32[]{:S(2)}) async-start(bf16[8,432,128]{2,1,0:T(8,128)(2,1)} %bitcast.11), calls=%async_computation.3 | async-start | bytes 1769472 | tf_op jit(solution)/shard_map/all_to_all | solution.py:583
  64.8 1.0 %shard_map.117 = (bf16[128,1152]{1,0:T(8,128)(2,1)}, f32[88,128]{1,0:T(8,128)S(1)}) custom-call(bf16[8,176,128]{2,1,0:T(8,128)(2,1)S(1)} %all-to-all-done.2.x_ref), custom_call_target="tpu_custom_call" | custom-call | bytes 700416 | tf_op jit(solution)/shard_map/pallas_call | solution.py:34
  65.8 2.3 %collective-permute-start.4 = (f32[88,128]{1,0:T(8,128)S(1)}, f32[88,128]{1,0:T(8,128)S(1)}, u32[]{:S(2)}, u32[]{:S(2)}) collective-permute-start(f32[88,128]{1,0:T(8,128)S(1)} %get-tuple-element.48.x_ref), channel_id=1, source_target_pairs={{0,8},{8,0},{16,24},{24,16},{1,9},{9,1},{17,25},{25,17},{2,10},{10... | collective-permute-start | bytes 135176 | tf_op jit(solution)/shard_map/ppermute | solution.py:705
  68.1 2.2 %collective-permute-done.4.y_ref = f32[88,128]{1,0:T(8,128)S(1)} collective-permute-done((f32[88,128]{1,0:T(8,128)S(1)}, f32[88,128]{1,0:T(8,128)S(1)}, u32[]{:S(2)}, u32[]{:S(2)}) %collective-permute-start.4) | collective-permute-done | bytes 45088 | tf_op jit(solution)/shard_map/ppermute | solution.py:705
  70.3 1.6 %collective-permute-start.5 = (f32[88,128]{1,0:T(8,128)S(1)}, f32[88,128]{1,0:T(8,128)S(1)}, u32[]{:S(2)}, u32[]{:S(2)}) collective-permute-start(f32[88,128]{1,0:T(8,128)S(1)} %shard_map.120.x_ref), channel_id=1, source_target_pairs={{0,16},{8,24},{16,0},{24,8},{1,17},{9,25},{17,1},{25,9},{2,18},{10... | collective-permute-start | bytes 135176 | tf_op jit(solution)/shard_map/ppermute | solution.py:708
  72.0 3.7 %collective-permute-done.5.y_ref = f32[88,128]{1,0:T(8,128)S(1)} collective-permute-done((f32[88,128]{1,0:T(8,128)S(1)}, f32[88,128]{1,0:T(8,128)S(1)}, u32[]{:S(2)}, u32[]{:S(2)}) %collective-permute-start.5) | collective-permute-done | bytes 45088 | tf_op jit(solution)/shard_map/ppermute | solution.py:708
  75.7 0.6 shard_map.121
  76.3 1.1 %all-to-all-done.3 = bf16[8,432,128]{2,1,0:T(8,128)(2,1)S(1)} async-done(((bf16[8,432,128]{2,1,0:T(8,128)(2,1)}), bf16[8,432,128]{2,1,0:T(8,128)(2,1)S(1)}, u32[]{:S(2)}, u32[]{:S(2)}) %all-to-all-start.3) | async-done | bytes 884768 | tf_op jit(solution)/shard_map/all_to_all | solution.py:583
  77.5 1.0 %shard_map.119 = (bf16[128,1152]{1,0:T(8,128)(2,1)}, bf16[128,1152]{1,0:T(8,128)(2,1)}, bf16[128,1152]{1,0:T(8,128)(2,1)}) custom-call(bf16[8,3,144,128]{3,2,1,0:T(8,128)(2,1)S(1)} %bitcast.19), custom_call_target="tpu_custom_call" | custom-call | bytes 1769472 | tf_op jit(solution)/shard_map/pallas_call | solution.py:34
  (4 shorter events, 0.0 us)
Async XLA Ops:
  2.9 17.9 %all-to-all-start = ((bf16[8,432,128]{2,1,0:T(8,128)(2,1)}), bf16[8,432,128]{2,1,0:T(8,128)(2,1)S(1)}, u32[]{:S(2)}, u32[]{:S(2)}) async-start(bf16[8,432,128]{2,1,0:T(8,128)(2,1)} %shard_map.110), calls=%async_computation | async-start | bytes 1769472 | tf_op jit(solution)/shard_map/all_to_all | solution.py:583
  20.8 3.2 %copy-start = (f32[3,3,1152]{2,1,0:T(4,128)S(1)}, f32[3,3,1152]{2,1,0:T(4,128)}, u32[]{:S(2)}) copy-start(f32[3,3,1152]{2,1,0:T(4,128)} %param.11) | copy-start | bytes 124420
  21.6 13.5 %collective-permute-start = (bf16[14,144,128]{2,1,0:T(8,128)(2,1)}, bf16[14,144,128]{2,1,0:T(8,128)(2,1)S(1)}, u32[]{:S(2)}, u32[]{:S(2)}) collective-permute-start(bf16[14,144,128]{2,1,0:T(8,128)(2,1)} %get-tuple-element.30), channel_id=1, source_target_pairs={{0,8},{8,0},{16,24},{24,16},{1,9},{9,1},{17,25},{25,17},{2,10},{10... | collective-permute-start | bytes 1548296 | tf_op jit(solution)/shard_map/ppermute | solution.py:618
  23.2 11.9 %collective-permute-start.1 = (bf16[14,144,128]{2,1,0:T(8,128)(2,1)S(1)}, bf16[14,144,128]{2,1,0:T(8,128)(2,1)S(1)}, u32[]{:S(2)}, u32[]{:S(2)}) collective-permute-start(bf16[14,144,128]{2,1,0:T(8,128)(2,1)S(1)} %get-tuple-element.31), channel_id=1, source_target_pairs={{8,16},{16,8},{9,17},{17,9},{10,18},{18,10},{11,19},{19,11},{12,20... | collective-permute-start | bytes 1548296 | tf_op jit(solution)/shard_map/ppermute | solution.py:618
  24.2 13.4 %all-to-all-start.1 = ((bf16[8,304,128]{2,1,0:T(8,128)(2,1)}), bf16[8,304,128]{2,1,0:T(8,128)(2,1)S(1)}, u32[]{:S(2)}, u32[]{:S(2)}) async-start(bf16[8,304,128]{2,1,0:T(8,128)(2,1)} %shard_map.111), calls=%async_computation.1 | async-start | bytes 1245184 | tf_op jit(solution)/shard_map/all_to_all | solution.py:583
  42.6 12.9 %collective-permute-start.2 = (bf16[10,144,128]{2,1,0:T(8,128)(2,1)S(1)}, bf16[10,144,128]{2,1,0:T(8,128)(2,1)}, u32[]{:S(2)}, u32[]{:S(2)}) collective-permute-start(bf16[10,144,128]{2,1,0:T(8,128)(2,1)S(1)} %get-tuple-element.39.refs_6_.refs_2_), channel_id=1, source_target_pairs={{0,8},{8,0},{16,24},{24,16},{1,9},{9,1},{17,25},{25,17},{2,10},{10... | collective-permute-start | bytes 1105928 | tf_op jit(solution)/shard_map/ppermute | solution.py:618
  47.0 8.4 %collective-permute-start.3 = (bf16[10,144,128]{2,1,0:T(8,128)(2,1)S(1)}, bf16[10,144,128]{2,1,0:T(8,128)(2,1)}, u32[]{:S(2)}, u32[]{:S(2)}) collective-permute-start(bf16[10,144,128]{2,1,0:T(8,128)(2,1)S(1)} %get-tuple-element.40.refs_7_.refs_3_), channel_id=1, source_target_pairs={{8,16},{16,8},{9,17},{17,9},{10,18},{18,10},{11,19},{19,11},{12,20... | collective-permute-start | bytes 1105928 | tf_op jit(solution)/shard_map/ppermute | solution.py:618
  50.8 10.5 %all-to-all-start.2 = ((bf16[8,176,128]{2,1,0:T(8,128)(2,1)}), bf16[8,176,128]{2,1,0:T(8,128)(2,1)S(1)}, u32[]{:S(2)}, u32[]{:S(2)}) async-start(bf16[8,176,128]{2,1,0:T(8,128)(2,1)} %get-tuple-element.41), calls=%async_computation.2 | async-start | bytes 720896 | tf_op jit(solution)/shard_map/all_to_all | solution.py:583
  61.3 16.2 %all-to-all-start.3 = ((bf16[8,432,128]{2,1,0:T(8,128)(2,1)}), bf16[8,432,128]{2,1,0:T(8,128)(2,1)S(1)}, u32[]{:S(2)}, u32[]{:S(2)}) async-start(bf16[8,432,128]{2,1,0:T(8,128)(2,1)} %bitcast.11), calls=%async_computation.3 | async-start | bytes 1769472 | tf_op jit(solution)/shard_map/all_to_all | solution.py:583
  65.8 4.5 %collective-permute-start.4 = (f32[88,128]{1,0:T(8,128)S(1)}, f32[88,128]{1,0:T(8,128)S(1)}, u32[]{:S(2)}, u32[]{:S(2)}) collective-permute-start(f32[88,128]{1,0:T(8,128)S(1)} %get-tuple-element.48.x_ref), channel_id=1, source_target_pairs={{0,8},{8,0},{16,24},{24,16},{1,9},{9,1},{17,25},{25,17},{2,10},{10... | collective-permute-start | bytes 135176 | tf_op jit(solution)/shard_map/ppermute | solution.py:705
  70.3 5.4 %collective-permute-start.5 = (f32[88,128]{1,0:T(8,128)S(1)}, f32[88,128]{1,0:T(8,128)S(1)}, u32[]{:S(2)}, u32[]{:S(2)}) collective-permute-start(f32[88,128]{1,0:T(8,128)S(1)} %shard_map.120.x_ref), channel_id=1, source_target_pairs={{0,16},{8,24},{16,0},{24,8},{1,17},{9,25},{17,1},{25,9},{2,18},{10... | collective-permute-start | bytes 135176 | tf_op jit(solution)/shard_map/ppermute | solution.py:708

commit v7 on v6

--- a/solution.py
+++ b/solution.py
@@ -501,19 +501,24 @@
         at = chunk(step)
         return pltpu.make_async_copy(held.at[:, :, at], out_ref.at[:, :, at], ends.at[step])
 
-    gets = [
-        pltpu.make_async_copy(*pair, sems.at[n])
-        for n, pair in enumerate(
-            ((u_hbm, u_ref), (d_hbm, d_ref), (dk_hbm, dk_ref), (dv_hbm, dv_ref))
-        )
-    ]
-    for get in gets:
-        get.start()
-    for get in gets:
-        get.wait()
+    def get(step):
+        at = chunk(step)
+        return [
+            pltpu.make_async_copy(far.at[:, at], near.at[:, at], sems.at[n, step])
+            for n, (far, near) in enumerate(
+                ((u_hbm, u_ref), (d_hbm, d_ref), (dv_hbm, dv_ref), (dk_hbm, dk_ref))
+            )
+        ]
 
     @pl.loop(0, chp // 16)
     def _(step):
+        for copy in get(step):
+            copy.start()
+
+    @pl.loop(0, chp // 16)
+    def _(step):
+        for copy in get(step):
+            copy.wait()
         at = chunk(step)
         masks = lane_masks(16)
         coef = taps(kc_ref, at)[::-1]
@@ -686,7 +691,7 @@
             pltpu.VMEM(side, BF),
             pltpu.VMEM(side, BF),
             pltpu.VMEM((peers, 3, chp, LANES), BF),
-            pltpu.SemaphoreType.DMA((4,)),
+            pltpu.SemaphoreType.DMA((4, chp // 16)),
             pltpu.SemaphoreType.DMA((chp // 16,)),
         ],
         far_in=(0, 1, 4, 5),

time: 79.1 us -> 79.1 us (level)
  no operation moved by 1% of the time
where the time goes in v7:
time: 79.1 us; the launch traced here: 78.5 us
  starting transfers between devices  27.8 us (35%)
  Pallas kernels  24.6 us (31%)
  waiting for transfers between devices  23.7 us (30%)
  local copies, waits for them, and re-layouts  0.9 us (1%)
    pallas_call x12, Pallas kernels, call(): pl.pallas_call(body, out_shape=[(pltpu.HBM if n in hbm else jax.ShapeDtyp...  24.6 us
    all_to_all x4, starting transfers between devices, swap(): return lax.all_to_all(x.reshape(peers, -1, LANES), plane, 0, 0, tiled=True)  15.7 us
    all_to_all x4, waiting for transfers between devices, swap(): return lax.all_to_all(x.reshape(peers, -1, LANES), plane, 0, 0, tiled=True)  11.6 us
    ppermute x4, starting transfers between devices, exchange(): return [lax.ppermute(x, 'z', pairs) for x, pairs in zip(messages, rounds)]  8.14 us
    ppermute x4, waiting for transfers between devices, exchange(): return [lax.ppermute(x, 'z', pairs) for x, pairs in zip(messages, rounds)]  6.22 us
    ppermute x2, waiting for transfers between devices, per_device(): other = lax.ppermute(taps_sum, 'z', [(i, i ^ step) for i in range(planes)])  5.95 us
    ppermute x2, starting transfers between devices, per_device(): other = lax.ppermute(taps_sum, 'z', [(i, i ^ step) for i in range(planes)])  3.89 us
  transfers between devices with their start and end apart: 10, of which 7 were waited for; matrix products, arithmetic and copies ran while one was open for 2% of the time, Pallas kernels for 20%

profile of v7, /device:TPU:0, one launch (start us, length us, event | category | flops | bytes accessed | tf_op | source)
XLA Modules:
  0.0 78.5 jit_solution(14324395313271947910)
XLA Ops:
  0.6 2.2 %shard_map.110 = bf16[8,432,128]{2,1,0:T(8,128)(2,1)} custom-call(bf16[128,1152]{1,0:T(8,128)(2,1)} %bitcast.20, bf16[128,1152]{1,0:T(8,128)(2,1)} %bitcast.21, bf16[128,1152]{1,0:T(8,128)(2,1)} %bitcast.22), custom_call_target="tpu_custom_call" | custom-call | bytes 1769472 | tf_op jit(solution)/shard_map/pallas_call | solution.py:34
  2.9 5.2 %all-to-all-start = ((bf16[8,432,128]{2,1,0:T(8,128)(2,1)}), bf16[8,432,128]{2,1,0:T(8,128)(2,1)S(1)}, u32[]{:S(2)}, u32[]{:S(2)}) async-start(bf16[8,432,128]{2,1,0:T(8,128)(2,1)} %shard_map.110), calls=%async_computation | async-start | bytes 1769472 | tf_op jit(solution)/shard_map/all_to_all | solution.py:588
  8.1 0.7 bitcast_or_fusion
  8.7 0.1 pad_add_fusion
  8.8 0.7 broadcast_in_dim.16.refs_2_
  9.5 2.8 %shard_map.111 = bf16[8,304,128]{2,1,0:T(8,128)(2,1)} custom-call(bf16[128,1152]{1,0:T(8,128)(2,1)} %bitcast.24, bf16[128,1152]{1,0:T(8,128)(2,1)} %bitcast.25, f32[16,128]{1,0:T(8,128)} %broadcast_in_dim.16.refs_2_), custom_call_target="tpu_custom_call" | custom-call | bytes 1220608 | tf_op jit(solution)/shard_map/pallas_call | solution.py:34
  12.3 8.5 %all-to-all-done = bf16[8,432,128]{2,1,0:T(8,128)(2,1)S(1)} async-done(((bf16[8,432,128]{2,1,0:T(8,128)(2,1)}), bf16[8,432,128]{2,1,0:T(8,128)(2,1)S(1)}, u32[]{:S(2)}, u32[]{:S(2)}) %all-to-all-start) | async-done | bytes 884768 | tf_op jit(solution)/shard_map/all_to_all | solution.py:588
  20.8 0.0 copy-start
  20.8 0.9 %shard_map.113 = (bf16[14,144,128]{2,1,0:T(8,128)(2,1)}, bf16[14,144,128]{2,1,0:T(8,128)(2,1)S(1)}) custom-call(bf16[8,3,144,128]{3,2,1,0:T(8,128)(2,1)S(1)} %bitcast.17), custom_call_target="tpu_custom_call" | custom-call | bytes 1916928 | tf_op jit(solution)/shard_map/pallas_call | solution.py:34
  21.6 1.6 %collective-permute-start = (bf16[14,144,128]{2,1,0:T(8,128)(2,1)}, bf16[14,144,128]{2,1,0:T(8,128)(2,1)S(1)}, u32[]{:S(2)}, u32[]{:S(2)}) collective-permute-start(bf16[14,144,128]{2,1,0:T(8,128)(2,1)} %get-tuple-element.30), channel_id=1, source_target_pairs={{0,8},{8,0},{16,24},{24,16},{1,9},{9,1},{17,25},{25,17},{2,10},{10... | collective-permute-start | bytes 1548296 | tf_op jit(solution)/shard_map/ppermute | solution.py:623
  23.2 0.7 collective-permute-start.1
  23.9 0.0 copy-done
  24.0 0.1 constant_dynamic-slice_fusion
  24.0 0.1 copy.18
  24.2 3.6 %all-to-all-start.1 = ((bf16[8,304,128]{2,1,0:T(8,128)(2,1)}), bf16[8,304,128]{2,1,0:T(8,128)(2,1)S(1)}, u32[]{:S(2)}, u32[]{:S(2)}) async-start(bf16[8,304,128]{2,1,0:T(8,128)(2,1)} %shard_map.111), calls=%async_computation.1 | async-start | bytes 1245184 | tf_op jit(solution)/shard_map/all_to_all | solution.py:588
  27.7 2.4 %shard_map.112 = (bf16[8,3,144,128]{3,2,1,0:T(8,128)(2,1)S(1)}, f32[4,144,128]{2,1,0:T(8,128)S(1)}) custom-call(bf16[8,3,144,128]{3,2,1,0:T(8,128)(2,1)S(1)} %bitcast.18, f32[144,128]{1,0:T(8,128)S(1)} %pad.9.kc_ref.refs_4_.refs_6_), custom_call_target="tpu_custom_call", output_to_operand_aliasing={{0}: (0, {})} | custom-call | flops 3000000000 | bytes 2138112 | tf_op jit(solution)/shard_map/pallas_call | solution.py:34
  30.1 5.0 %collective-permute-done.refs_1_ = bf16[14,144,128]{2,1,0:T(8,128)(2,1)S(1)} collective-permute-done((bf16[14,144,128]{2,1,0:T(8,128)(2,1)}, bf16[14,144,128]{2,1,0:T(8,128)(2,1)S(1)}, u32[]{:S(2)}, u32[]{:S(2)}) %collective-permute-start) | collective-permute-done | bytes 516128 | tf_op jit(solution)/shard_map/ppermute | solution.py:623
  35.1 0.0 collective-permute-done.1.refs_2_
  35.1 2.5 %shard_map.114 = (bf16[8,3,144,128]{3,2,1,0:T(8,128)(2,1)S(1)}, bf16[14,144,128]{2,1,0:T(8,128)(2,1)S(1)}, bf16[14,144,128]{2,1,0:T(8,128)(2,1)S(1)}) custom-call(bf16[8,3,144,128]{3,2,1,0:T(8,128)(2,1)S(1)} %get-tuple-element.29.refs_0_, ...), custom_call_target="tpu_custom_call", output_to_operand_aliasing={{0}: (0, {}), {1}: (1, {}), {2}: (2, {})} | custom-call | flops 4000000000 | bytes 4202496 | tf_op jit(solution)/shard_map/pallas_call | solution.py:34
  37.6 0.0 all-to-all-done.1.refs_0_
  37.6 4.9 %shard_map.115 = (bf16[8,144,128]{2,1,0:T(8,128)(2,1)S(1)}, bf16[10,144,128]{2,1,0:T(8,128)(2,1)S(1)}, bf16[10,144,128]{2,1,0:T(8,128)(2,1)S(1)}, f32[2,144,512]{2,1,0:T(8,128)S(1)}, f32[2,144,512]{2,1,0:T(8,128)S(1)}) custom-call(bf16[8,304,128]{2,1,0:T(8,128)(2,1)S(1)} %all-to-all-done.1.refs_0_, bf16[8,3,144,128]{3,2,1,0:T(8,128)(2,1)S(1)} %get-tuple-element.33.refs_1_, ...), custom_call_target="tpu_custom_call" | custom-call | flops 4026531840 | bytes 4751360 | tf_op jit(solution)/shard_map/pallas_call | solution.py:34
  42.6 4.5 %collective-permute-start.2 = (bf16[10,144,128]{2,1,0:T(8,128)(2,1)S(1)}, bf16[10,144,128]{2,1,0:T(8,128)(2,1)}, u32[]{:S(2)}, u32[]{:S(2)}) collective-permute-start(bf16[10,144,128]{2,1,0:T(8,128)(2,1)S(1)} %get-tuple-element.39.refs_6_.refs_2_), channel_id=1, source_target_pairs={{0,8},{8,0},{16,24},{24,16},{1,9},{9,1},{17,25},{25,17},{2,10},{10... | collective-permute-start | bytes 1105928 | tf_op jit(solution)/shard_map/ppermute | solution.py:623
  47.0 1.4 %collective-permute-start.3 = (bf16[10,144,128]{2,1,0:T(8,128)(2,1)S(1)}, bf16[10,144,128]{2,1,0:T(8,128)(2,1)}, u32[]{:S(2)}, u32[]{:S(2)}) collective-permute-start(bf16[10,144,128]{2,1,0:T(8,128)(2,1)S(1)} %get-tuple-element.40.refs_7_.refs_3_), channel_id=1, source_target_pairs={{8,16},{16,8},{9,17},{17,9},{10,18},{18,10},{11,19},{19,11},{12,20... | collective-permute-start | bytes 1105928 | tf_op jit(solution)/shard_map/ppermute | solution.py:623
  48.4 2.3 %shard_map.116 = (bf16[8,176,128]{2,1,0:T(8,128)(2,1)}, f32[2,144,512]{2,1,0:T(8,128)}, f32[2,144,512]{2,1,0:T(8,128)}) custom-call(bf16[8,144,128]{2,1,0:T(8,128)(2,1)S(1)} %get-tuple-element.36.refs_0_, bf16[8,3,144,128]{3,2,1,0:T(8,128)(2,1)S(1)} %get-tuple-element.33.refs_1_, bf16[14,144,128]{2,1,0:T(8,128)(2,1)S(1)} %get-tuple-element.34.refs_2_, ...), custom_call_target="tpu_custom_call" | custom-call | flops 4000000000 | bytes 5668864 | tf_op jit(solution)/shard_map/pallas_call | solution.py:34
  50.8 3.5 %all-to-all-start.2 = ((bf16[8,176,128]{2,1,0:T(8,128)(2,1)}), bf16[8,176,128]{2,1,0:T(8,128)(2,1)S(1)}, u32[]{:S(2)}, u32[]{:S(2)}) async-start(bf16[8,176,128]{2,1,0:T(8,128)(2,1)} %get-tuple-element.41), calls=%async_computation.2 | async-start | bytes 720896 | tf_op jit(solution)/shard_map/all_to_all | solution.py:588
  54.2 1.2 %collective-permute-done.2.refs_4_ = bf16[10,144,128]{2,1,0:T(8,128)(2,1)} collective-permute-done((bf16[10,144,128]{2,1,0:T(8,128)(2,1)S(1)}, bf16[10,144,128]{2,1,0:T(8,128)(2,1)}, u32[]{:S(2)}, u32[]{:S(2)}) %collective-permute-start.2) | collective-permute-done | bytes 368672 | tf_op jit(solution)/shard_map/ppermute | solution.py:623
  55.4 0.0 collective-permute-done.3.refs_5_
  55.4 3.9 %shard_map.118 = bf16[8,3,144,128]{3,2,1,0:T(8,128)(2,1)} custom-call(f32[2,144,512]{2,1,0:T(8,128)} %get-tuple-element.43.refs_0_, f32[2,144,512]{2,1,0:T(8,128)} %get-tuple-element.44.refs_1_, bf16[10,144,128]{2,1,0:T(8,128)(2,1)S(1)} %get-tuple-element.39.refs_6_.refs_2_, bf16[10,144,128]{2,1,0:T(8,128)(2,1)S(1)} %get-tuple-element.40.refs_7_.refs_3_, ...), custom_call_target="tpu_custom_call" | custom-call | flops 4000000000 | bytes 3612672 | tf_op jit(solution)/shard_map/pallas_call | solution.py:34
  59.4 1.9 %all-to-all-done.2.x_ref = bf16[8,176,128]{2,1,0:T(8,128)(2,1)S(1)} async-done(((bf16[8,176,128]{2,1,0:T(8,128)(2,1)}), bf16[8,176,128]{2,1,0:T(8,128)(2,1)S(1)}, u32[]{:S(2)}, u32[]{:S(2)}) %all-to-all-start.2) | async-done | bytes 360480 | tf_op jit(solution)/shard_map/all_to_all | solution.py:588
  61.3 3.6 %all-to-all-start.3 = ((bf16[8,432,128]{2,1,0:T(8,128)(2,1)}), bf16[8,432,128]{2,1,0:T(8,128)(2,1)S(1)}, u32[]{:S(2)}, u32[]{:S(2)}) async-start(bf16[8,432,128]{2,1,0:T(8,128)(2,1)} %bitcast.11), calls=%async_computation.3 | async-start | bytes 1769472 | tf_op jit(solution)/shard_map/all_to_all | solution.py:588
  64.8 1.0 %shard_map.117 = (bf16[128,1152]{1,0:T(8,128)(2,1)}, f32[88,128]{1,0:T(8,128)S(1)}) custom-call(bf16[8,176,128]{2,1,0:T(8,128)(2,1)S(1)} %all-to-all-done.2.x_ref), custom_call_target="tpu_custom_call" | custom-call | bytes 700416 | tf_op jit(solution)/shard_map/pallas_call | solution.py:34
  65.8 2.3 %collective-permute-start.4 = (f32[88,128]{1,0:T(8,128)S(1)}, f32[88,128]{1,0:T(8,128)S(1)}, u32[]{:S(2)}, u32[]{:S(2)}) collective-permute-start(f32[88,128]{1,0:T(8,128)S(1)} %get-tuple-element.48.x_ref), channel_id=1, source_target_pairs={{0,8},{8,0},{16,24},{24,16},{1,9},{9,1},{17,25},{25,17},{2,10},{10... | collective-permute-start | bytes 135176 | tf_op jit(solution)/shard_map/ppermute | solution.py:710
  68.1 2.2 %collective-permute-done.4.y_ref = f32[88,128]{1,0:T(8,128)S(1)} collective-permute-done((f32[88,128]{1,0:T(8,128)S(1)}, f32[88,128]{1,0:T(8,128)S(1)}, u32[]{:S(2)}, u32[]{:S(2)}) %collective-permute-start.4) | collective-permute-done | bytes 45088 | tf_op jit(solution)/shard_map/ppermute | solution.py:710
  70.3 1.6 %collective-permute-start.5 = (f32[88,128]{1,0:T(8,128)S(1)}, f32[88,128]{1,0:T(8,128)S(1)}, u32[]{:S(2)}, u32[]{:S(2)}) collective-permute-start(f32[88,128]{1,0:T(8,128)S(1)} %shard_map.120.x_ref), channel_id=1, source_target_pairs={{0,16},{8,24},{16,0},{24,8},{1,17},{9,25},{17,1},{25,9},{2,18},{10... | collective-permute-start | bytes 135176 | tf_op jit(solution)/shard_map/ppermute | solution.py:713
  72.0 3.7 %collective-permute-done.5.y_ref = f32[88,128]{1,0:T(8,128)S(1)} collective-permute-done((f32[88,128]{1,0:T(8,128)S(1)}, f32[88,128]{1,0:T(8,128)S(1)}, u32[]{:S(2)}, u32[]{:S(2)}) %collective-permute-start.5) | collective-permute-done | bytes 45088 | tf_op jit(solution)/shard_map/ppermute | solution.py:713
  75.7 0.6 shard_map.121
  76.3 1.1 %all-to-all-done.3 = bf16[8,432,128]{2,1,0:T(8,128)(2,1)S(1)} async-done(((bf16[8,432,128]{2,1,0:T(8,128)(2,1)}), bf16[8,432,128]{2,1,0:T(8,128)(2,1)S(1)}, u32[]{:S(2)}, u32[]{:S(2)}) %all-to-all-start.3) | async-done | bytes 884768 | tf_op jit(solution)/shard_map/all_to_all | solution.py:588
  77.5 1.0 %shard_map.119 = (bf16[128,1152]{1,0:T(8,128)(2,1)}, bf16[128,1152]{1,0:T(8,128)(2,1)}, bf16[128,1152]{1,0:T(8,128)(2,1)}) custom-call(bf16[8,3,144,128]{3,2,1,0:T(8,128)(2,1)S(1)} %bitcast.19), custom_call_target="tpu_custom_call" | custom-call | bytes 1769472 | tf_op jit(solution)/shard_map/pallas_call | solution.py:34
  (4 shorter events, 0.0 us)
Async XLA Ops:
  2.9 17.9 %all-to-all-start = ((bf16[8,432,128]{2,1,0:T(8,128)(2,1)}), bf16[8,432,128]{2,1,0:T(8,128)(2,1)S(1)}, u32[]{:S(2)}, u32[]{:S(2)}) async-start(bf16[8,432,128]{2,1,0:T(8,128)(2,1)} %shard_map.110), calls=%async_computation | async-start | bytes 1769472 | tf_op jit(solution)/shard_map/all_to_all | solution.py:588
  20.8 3.2 %copy-start = (f32[3,3,1152]{2,1,0:T(4,128)S(1)}, f32[3,3,1152]{2,1,0:T(4,128)}, u32[]{:S(2)}) copy-start(f32[3,3,1152]{2,1,0:T(4,128)} %param.11) | copy-start | bytes 124420
  21.6 13.5 %collective-permute-start = (bf16[14,144,128]{2,1,0:T(8,128)(2,1)}, bf16[14,144,128]{2,1,0:T(8,128)(2,1)S(1)}, u32[]{:S(2)}, u32[]{:S(2)}) collective-permute-start(bf16[14,144,128]{2,1,0:T(8,128)(2,1)} %get-tuple-element.30), channel_id=1, source_target_pairs={{0,8},{8,0},{16,24},{24,16},{1,9},{9,1},{17,25},{25,17},{2,10},{10... | collective-permute-start | bytes 1548296 | tf_op jit(solution)/shard_map/ppermute | solution.py:623
  23.2 11.9 %collective-permute-start.1 = (bf16[14,144,128]{2,1,0:T(8,128)(2,1)S(1)}, bf16[14,144,128]{2,1,0:T(8,128)(2,1)S(1)}, u32[]{:S(2)}, u32[]{:S(2)}) collective-permute-start(bf16[14,144,128]{2,1,0:T(8,128)(2,1)S(1)} %get-tuple-element.31), channel_id=1, source_target_pairs={{8,16},{16,8},{9,17},{17,9},{10,18},{18,10},{11,19},{19,11},{12,20... | collective-permute-start | bytes 1548296 | tf_op jit(solution)/shard_map/ppermute | solution.py:623
  24.2 13.4 %all-to-all-start.1 = ((bf16[8,304,128]{2,1,0:T(8,128)(2,1)}), bf16[8,304,128]{2,1,0:T(8,128)(2,1)S(1)}, u32[]{:S(2)}, u32[]{:S(2)}) async-start(bf16[8,304,128]{2,1,0:T(8,128)(2,1)} %shard_map.111), calls=%async_computation.1 | async-start | bytes 1245184 | tf_op jit(solution)/shard_map/all_to_all | solution.py:588
  42.6 12.9 %collective-permute-start.2 = (bf16[10,144,128]{2,1,0:T(8,128)(2,1)S(1)}, bf16[10,144,128]{2,1,0:T(8,128)(2,1)}, u32[]{:S(2)}, u32[]{:S(2)}) collective-permute-start(bf16[10,144,128]{2,1,0:T(8,128)(2,1)S(1)} %get-tuple-element.39.refs_6_.refs_2_), channel_id=1, source_target_pairs={{0,8},{8,0},{16,24},{24,16},{1,9},{9,1},{17,25},{25,17},{2,10},{10... | collective-permute-start | bytes 1105928 | tf_op jit(solution)/shard_map/ppermute | solution.py:623
  47.0 8.4 %collective-permute-start.3 = (bf16[10,144,128]{2,1,0:T(8,128)(2,1)S(1)}, bf16[10,144,128]{2,1,0:T(8,128)(2,1)}, u32[]{:S(2)}, u32[]{:S(2)}) collective-permute-start(bf16[10,144,128]{2,1,0:T(8,128)(2,1)S(1)} %get-tuple-element.40.refs_7_.refs_3_), channel_id=1, source_target_pairs={{8,16},{16,8},{9,17},{17,9},{10,18},{18,10},{11,19},{19,11},{12,20... | collective-permute-start | bytes 1105928 | tf_op jit(solution)/shard_map/ppermute | solution.py:623
  50.8 10.5 %all-to-all-start.2 = ((bf16[8,176,128]{2,1,0:T(8,128)(2,1)}), bf16[8,176,128]{2,1,0:T(8,128)(2,1)S(1)}, u32[]{:S(2)}, u32[]{:S(2)}) async-start(bf16[8,176,128]{2,1,0:T(8,128)(2,1)} %get-tuple-element.41), calls=%async_computation.2 | async-start | bytes 720896 | tf_op jit(solution)/shard_map/all_to_all | solution.py:588
  61.3 16.2 %all-to-all-start.3 = ((bf16[8,432,128]{2,1,0:T(8,128)(2,1)}), bf16[8,432,128]{2,1,0:T(8,128)(2,1)S(1)}, u32[]{:S(2)}, u32[]{:S(2)}) async-start(bf16[8,432,128]{2,1,0:T(8,128)(2,1)} %bitcast.11), calls=%async_computation.3 | async-start | bytes 1769472 | tf_op jit(solution)/shard_map/all_to_all | solution.py:588
  65.8 4.5 %collective-permute-start.4 = (f32[88,128]{1,0:T(8,128)S(1)}, f32[88,128]{1,0:T(8,128)S(1)}, u32[]{:S(2)}, u32[]{:S(2)}) collective-permute-start(f32[88,128]{1,0:T(8,128)S(1)} %get-tuple-element.48.x_ref), channel_id=1, source_target_pairs={{0,8},{8,0},{16,24},{24,16},{1,9},{9,1},{17,25},{25,17},{2,10},{10... | collective-permute-start | bytes 135176 | tf_op jit(solution)/shard_map/ppermute | solution.py:710
  70.3 5.4 %collective-permute-start.5 = (f32[88,128]{1,0:T(8,128)S(1)}, f32[88,128]{1,0:T(8,128)S(1)}, u32[]{:S(2)}, u32[]{:S(2)}) collective-permute-start(f32[88,128]{1,0:T(8,128)S(1)} %shard_map.120.x_ref), channel_id=1, source_target_pairs={{0,16},{8,24},{16,0},{24,8},{1,17},{9,25},{17,1},{25,9},{2,18},{10... | collective-permute-start | bytes 135176 | tf_op jit(solution)/shard_map/ppermute | solution.py:713
